TPU v7x, 128 devices: a whole 4x4x4 slice. The times are simulated.
128 devices in a mesh: comp: 32 (over y, z, core), grp: 4 (over x).
Axes of the slice: x: 4, y: 4, z: 4, core: 2. Of those that a mesh axis runs over, the one named last changes fastest.
Arguments:
- spectrum: float32 [32, 36, 4, 64, 512], P('comp', None, 'grp'), may hold values from 0.05 to 1
- courant: float32 [32], P('comp'), may hold values from 0.15 to 0.45
- sea_mask: int32 [4, 64, 512], P('grp'), may hold values 0 or 1
- wind_u: float32 [4, 64, 512], P('grp', 'comp'), may hold values from -4 to 4
- wind_v: float32 [4, 64, 512], P('grp', 'comp'), may hold values from -4 to 4
- boundary_cells: int32 [40, 128], replicated, may hold values from 0 to 131071, as said below
Outputs:
- updated: float32 [32, 36, 4, 64, 512], P(None, None, 'grp', 'comp')
- boundary: float32 [32, 36, 40, 128], P('comp', None, 'grp')
Inputs may be any that keep to these rules, and one draw needn't show every extreme that they name: `boundary_cells`: positions k * 32 to (k + 1) * 32 - 1 of every list name cells of row block k.
All inputs are finite; a program needn't handle non-finite values. No bound on the sum of `sea_mask` on one device may be relied on, other than what follows from the above.
Results may differ from a plain program's by a relative error of at most 0.000075.
Values sent between devices are 32-bit elements; how exact they have to be, the bound alone decides.
No kernel may reach another device: no remote copies, remote signals or barrier semaphores. Data moves between devices by JAX's collectives and lax.ppermute only.
A program may use at most 192 MiB of HBM per device.

v0:
```python
import jax
import jax.numpy as jnp
from jax import lax
from jax.sharding import PartitionSpec as P

NDIR = 36
NFREQ = 32
SUBSTEPS = 3


def extended_2(value, sides, width):
    for axis, dim in sides:
        size, length = (lax.axis_size(axis), value.shape[dim])
        up = [(i, (i + 1) % size) for i in range(size - 1)]
        down = [(j, i) for i, j in up]
        last = lax.slice_in_dim(value, length - width, length, axis=dim)
        leading = lax.slice_in_dim(value, 0, width, axis=dim)
        before = lax.ppermute(last, axis, up)
        after = lax.ppermute(leading, axis, down)
        value = jnp.concatenate([before, value, after], axis=dim)
    return value


def substep(extended, speed_east, speed_north, mask_float):
    energy = extended[:, 1:-1]
    south = extended[:, :-2]
    north = extended[:, 2:]
    west = jnp.roll(energy, 1, axis=2)
    east = jnp.roll(energy, -1, axis=2)
    flux = jnp.maximum(speed_east, 0.0) * (energy - west) + jnp.maximum(-speed_east, 0.0) * (
        energy - east
    )
    flux = (
        flux
        + jnp.maximum(speed_north, 0.0) * (energy - south)
        + jnp.maximum(-speed_north, 0.0) * (energy - north)
    )
    return mask_float * (energy - flux)


def sources(energy, wind_east, wind_north):
    extra = (1,) * (energy.ndim - 2)
    scale = 0.3 * 1.1 ** jnp.arange(NFREQ, dtype=jnp.float32)
    wavenum = scale * scale
    theta = 2.0 * jnp.pi * jnp.arange(NDIR, dtype=jnp.float32) / NDIR
    scale_b = scale.reshape((NFREQ, 1) + extra)
    wave_b = wavenum.reshape((NFREQ, 1) + extra)
    cos_b = jnp.cos(theta).reshape((1, NDIR) + extra)
    sin_b = jnp.sin(theta).reshape((1, NDIR) + extra)
    mean_energy = jnp.mean(energy, axis=(0, 1))
    mean_wave = jnp.mean(energy * wave_b, axis=(0, 1))
    ratio = jnp.maximum(mean_energy, 0.05) / jnp.maximum(mean_wave, 0.1)
    projected = wind_east * cos_b + wind_north * sin_b
    gain = 0.05 * scale_b * jnp.maximum(projected * scale_b - 1.0, 0.0)
    steep = mean_energy / 0.3
    loss = 0.1 * scale_b * wave_b * ratio * (steep * steep)
    return energy * jnp.exp(gain - loss)


def propagate(energy, speed_east, speed_north, mask_float):
    for turn_index in range(SUBSTEPS):
        extended = extended_2(energy, (("grp", 1),), 1)
        energy = substep(extended, speed_east, speed_north, mask_float)
    return energy


def per_device(spectrum, courant, sea_mask, wind_u, wind_v, boundary_cells):
    group_count = lax.axis_size("grp")
    group_index = lax.axis_index("grp")
    local_freq = spectrum.shape[0]
    row_count = spectrum.shape[3]
    col_count = spectrum.shape[4]
    theta = 2.0 * jnp.pi * jnp.arange(NDIR, dtype=jnp.float32) / NDIR
    speed_east = courant[:, None] * jnp.cos(theta)[None, :]
    speed_north = courant[:, None] * jnp.sin(theta)[None, :]
    mask_float = sea_mask.astype(jnp.float32)
    portions = 1
    dir_width = NDIR // portions
    energy = spectrum[:, 0:dir_width, 0].reshape(local_freq * dir_width, row_count, col_count)
    east_part = speed_east.reshape(local_freq * dir_width, 1, 1)
    north_part = speed_north.reshape(local_freq * dir_width, 1, 1)
    result = propagate(energy, east_part, north_part, mask_float)
    result = result.reshape(local_freq, dir_width, row_count, col_count)
    moved = lax.all_to_all(result, "comp", split_axis=2, concat_axis=0, tiled=True)
    flat_cells = result.reshape(local_freq, NDIR, row_count * col_count)
    nest_local = boundary_cells.shape[0] // group_count
    block_points = boundary_cells.shape[1] // group_count
    lists = boundary_cells.reshape(group_count, nest_local, group_count, block_points)
    mine = lax.dynamic_index_in_dim(lists, group_index, axis=2, keepdims=False)
    local_cells = mine - group_index * (row_count * col_count)
    picked = jnp.take(flat_cells, local_cells.reshape(-1), axis=2)
    picked = picked.reshape(local_freq, NDIR, group_count, nest_local, block_points)
    owners = lax.all_to_all(picked, "grp", split_axis=2, concat_axis=4, tiled=True)
    boundary = owners.reshape(local_freq, NDIR, nest_local, group_count * block_points)
    updated = sources(moved[:, :, None], wind_u, wind_v)
    return (updated, boundary)


def solution(mesh):
    placed = (
        P("comp", None, "grp", None, None),
        P("comp"),
        P("grp", None, None),
        P("grp", "comp", None),
        P("grp", "comp", None),
        P(),
    )
    return jax.shard_map(
        per_device,
        mesh=mesh,
        in_specs=placed,
        out_specs=(P(None, None, "grp", "comp", None), P("comp", None, "grp", None)),
        check_vma=False,
    )
```

profile of v0, /device:TPU:34, one launch (start us, length us, event | category | flops | bytes accessed | tf_op | source)
XLA Modules:
  0.0 202.1 jit_solution(15642794480732887241)
XLA Ops:
  0.6 1.4 fusion.48
  2.0 3.4 %collective-permute-start = (f32[36,1,512]{2,1,0:T(1,128)S(1)}, f32[36,1,512]{2,1,0:T(1,128)S(1)}, u32[]{:S(2)}, u32[]{:S(2)}) collective-permute-start(f32[36,1,512]{2,1,0:T(1,128)S(1)} %get-tuple-element.28), channel_id=1, source_target_pairs={{0,1},{1,2},{2,3},{4,5},{5,6},{6,7},{8,9},{9,10},{10,11},{12,13},{... | collective-permute-start | bytes 221192 | tf_op jit(solution)/shard_map/ppermute | solution.py:18
  5.4 2.7 %collective-permute-start.1 = (f32[36,1,512]{2,1,0:T(1,128)S(1)}, f32[36,1,512]{2,1,0:T(1,128)S(1)}, u32[]{:S(2)}, u32[]{:S(2)}) collective-permute-start(f32[36,1,512]{2,1,0:T(1,128)S(1)} %get-tuple-element.29), channel_id=1, source_target_pairs={{1,0},{2,1},{3,2},{5,4},{6,5},{7,6},{9,8},{10,9},{11,10},{13,12},{... | collective-permute-start | bytes 221192 | tf_op jit(solution)/shard_map/ppermute | solution.py:19
  8.2 8.9 %fusion.46 = (f32[36,64,511]{2,1,0:T(8,128)}, f32[36,64,511]{2,1,0:T(8,128)}) fusion(f32[36,64,512]{2,1,0:T(8,128)} %bitcast.43), kind=kLoop, calls=%fused_computation.80 | loop fusion | bytes 18837504 | tf_op jit(solution)/shard_map/jit(_roll_static)/slice | solution.py:29
  17.1 0.5 fusion.47
  18.9 11.1 %fusion.20 = f32[36,64,512]{2,1,0:T(8,128)S(1)} fusion(f32[36,64,512]{2,1,0:T(8,128)} %bitcast.44, f32[36,1,512]{2,1,0:T(1,128)S(1)} %collective-permute-done.1, f32[36,1,512]{2,1,0:T(1,128)S(1)} %collective-permute-done, f32[36,64,511]{2,1,0:T(8,128)} %get-tuple-element.25, f32[36,64,1]{2,1,0:T(8,128)S(1)} %get-tuple-element.27, ...), kind=kLoop, calls=%fused_computation.26 | loop fusion | flops 20054016 | bytes 19153472 | tf_op jit(solution)/shard_map/mul | solution.py:38
  30.0 1.9 fusion.43
  32.0 3.4 %collective-permute-start.2 = (f32[36,1,512]{2,1,0:T(1,128)S(1)}, f32[36,1,512]{2,1,0:T(1,128)S(1)}, u32[]{:S(2)}, u32[]{:S(2)}) collective-permute-start(f32[36,1,512]{2,1,0:T(1,128)S(1)} %get-tuple-element.22), channel_id=1, source_target_pairs={{0,1},{1,2},{2,3},{4,5},{5,6},{6,7},{8,9},{9,10},{10,11},{12,13},{... | collective-permute-start | bytes 221192 | tf_op jit(solution)/shard_map/ppermute | solution.py:18
  35.4 2.4 %collective-permute-start.3 = (f32[36,1,512]{2,1,0:T(1,128)S(1)}, f32[36,1,512]{2,1,0:T(1,128)S(1)}, u32[]{:S(2)}, u32[]{:S(2)}) collective-permute-start(f32[36,1,512]{2,1,0:T(1,128)S(1)} %get-tuple-element.23), channel_id=1, source_target_pairs={{1,0},{2,1},{3,2},{5,4},{6,5},{7,6},{9,8},{10,9},{11,10},{13,12},{... | collective-permute-start | bytes 221192 | tf_op jit(solution)/shard_map/ppermute | solution.py:19
  38.3 3.3 %collective-permute-done.3 = f32[36,1,512]{2,1,0:T(1,128)S(1)} collective-permute-done((f32[36,1,512]{2,1,0:T(1,128)S(1)}, f32[36,1,512]{2,1,0:T(1,128)S(1)}, u32[]{:S(2)}, u32[]{:S(2)}) %collective-permute-start.3) | collective-permute-done | bytes 73760 | tf_op jit(solution)/shard_map/ppermute | solution.py:19
  41.7 4.9 %fusion.12 = f32[36,64,512]{2,1,0:T(8,128)S(1)} fusion(f32[36,64,512]{2,1,0:T(8,128)S(1)} %fusion.20, f32[36,1,512]{2,1,0:T(1,128)S(1)} %collective-permute-done.3, f32[36,1,512]{2,1,0:T(1,128)S(1)} %collective-permute-done.2, f32[36,64,511]{2,1,0:T(8,128)S(1)} %get-tuple-element.19, f32[36,64,1]{2,1,0:T(8,128)S(1)} %get-tuple-element.21, ...), kind=kLoop, calls=%fused_computation.16 | loop fusion | flops 20054016 | bytes 19153472 | tf_op jit(solution)/shard_map/mul | solution.py:38
  46.6 1.9 fusion.40
  48.6 3.1 %collective-permute-start.4 = (f32[36,1,512]{2,1,0:T(1,128)S(1)}, f32[36,1,512]{2,1,0:T(1,128)S(1)}, u32[]{:S(2)}, u32[]{:S(2)}) collective-permute-start(f32[36,1,512]{2,1,0:T(1,128)S(1)} %get-tuple-element.16), channel_id=1, source_target_pairs={{0,1},{1,2},{2,3},{4,5},{5,6},{6,7},{8,9},{9,10},{10,11},{12,13},{... | collective-permute-start | bytes 221192 | tf_op jit(solution)/shard_map/ppermute | solution.py:18
  51.7 2.9 %collective-permute-start.5 = (f32[36,1,512]{2,1,0:T(1,128)S(1)}, f32[36,1,512]{2,1,0:T(1,128)S(1)}, u32[]{:S(2)}, u32[]{:S(2)}) collective-permute-start(f32[36,1,512]{2,1,0:T(1,128)S(1)} %get-tuple-element.17), channel_id=1, source_target_pairs={{1,0},{2,1},{3,2},{5,4},{6,5},{7,6},{9,8},{10,9},{11,10},{13,12},{... | collective-permute-start | bytes 221192 | tf_op jit(solution)/shard_map/ppermute | solution.py:19
  55.1 2.9 %collective-permute-done.5 = f32[36,1,512]{2,1,0:T(1,128)S(1)} collective-permute-done((f32[36,1,512]{2,1,0:T(1,128)S(1)}, f32[36,1,512]{2,1,0:T(1,128)S(1)}, u32[]{:S(2)}, u32[]{:S(2)}) %collective-permute-start.5) | collective-permute-done | bytes 73760 | tf_op jit(solution)/shard_map/ppermute | solution.py:19
  58.0 6.3 %fusion.4 = f32[36,64,512]{2,1,0:T(8,128)} fusion(f32[36,64,512]{2,1,0:T(8,128)S(1)} %fusion.12, f32[36,1,512]{2,1,0:T(1,128)S(1)} %collective-permute-done.5, f32[36,1,512]{2,1,0:T(1,128)S(1)} %collective-permute-done.4, f32[36,64,511]{2,1,0:T(8,128)S(1)} %get-tuple-element.13, f32[36,64,1]{2,1,0:T(8,128)S(1)} %get-tuple-element.15, ...), kind=kLoop, calls=%fused_computation.6 | loop fusion | flops 20054016 | bytes 19153472 | tf_op jit(solution)/shard_map/mul | solution.py:38
  64.3 10.8 %copy.42 = f32[36,64,512]{0,2,1:T(8,128)} copy(f32[36,64,512]{2,1,0:T(8,128)} %fusion.4) | data formatting | bytes 9437184 | tf_op jit(solution)/shard_map/mul | solution.py:38
  75.1 8.1 %gather_fusion = f32[1280,36]{1,0:T(8,128)S(1)} fusion(f32[36,32768]{0,1:T(8,128)} %bitcast.49, s32[2048]{0:T(1024)S(1)} %pad_clamp_fusion), kind=kCustom, calls=%fused_computation | custom fusion | bytes 373760 | tf_op jit(solution)/shard_map/jit(_take)/gather | solution.py:91
  83.5 1.4 reshape.267
  84.9 4.2 %all-to-all-start.1 = ((f32[4,1,11520]{2,1,0:T(1,128)}), f32[4,1,11520]{2,1,0:T(1,128)S(1)}, u32[]{:S(2)}, u32[]{:S(2)}) async-start(f32[4,1,11520]{2,1,0:T(1,128)} %reshape.267), calls=%async_computation.1 | async-start | bytes 368640 | tf_op jit(solution)/shard_map/all_to_all | solution.py:93
  89.0 9.4 %copy.37 = f32[1,36,64,512]{3,0,1,2:T(1,128)} copy(f32[1,36,64,512]{3,2,1,0:T(8,128)} %bitcast.48) | data formatting | bytes 9437184 | tf_op jit(solution)/shard_map/reshape | solution.py:83
  98.4 8.4 %all-to-all-start = ((f32[1,36,64,512]{3,0,1,2:T(1,128)}), f32[1,36,64,512]{3,0,1,2:T(1,128)}, u32[]{:S(2)}, u32[]{:S(2)}) async-start(f32[1,36,64,512]{3,0,1,2:T(1,128)} %copy.37), calls=%async_computation | async-start | bytes 9437184 | tf_op jit(solution)/shard_map/all_to_all | solution.py:84
  107.1 0.5 broadcast.338
  107.6 1.1 reduce.5
  108.8 0.8 reshape.268
  110.1 1.2 reshape.253
  111.2 58.2 %all-to-all-done = f32[1,36,64,512]{3,0,1,2:T(1,128)} async-done(((f32[1,36,64,512]{3,0,1,2:T(1,128)}), f32[1,36,64,512]{3,0,1,2:T(1,128)}, u32[]{:S(2)}, u32[]{:S(2)}) %all-to-all-start) | async-done | bytes 4718624 | tf_op jit(solution)/shard_map/all_to_all | solution.py:84
  169.4 9.8 %copy.38 = f32[1,36,64,512]{3,0,2,1:T(1,128)} copy(f32[1,36,64,512]{3,0,1,2:T(1,128)} %all-to-all-done) | data formatting | bytes 9437184 | tf_op jit(solution)/shard_map/all_to_all | solution.py:84
  179.3 4.9 %fusion.33 = f32[2,512]{1,0:T(2,128)S(1)} fusion(f32[32,1,36,2,512]{4,1,3,0,2:T(1,128)} %bitcast.39, f32[32]{0:T(128)S(1)} %fusion.39), kind=kLoop, calls=%fused_computation.48 | loop fusion | flops 2358272 | bytes 4722816 | tf_op jit(solution)/shard_map/reduce_sum | solution.py:51
  184.1 4.9 %reduce_sum.18 = f32[2,512]{1,0:T(2,128)S(1)} reduce(f32[32,1,36,2,512]{4,1,3,0,2:T(1,128)} %bitcast.40, f32[]{:T(128)} %constant.21.clone.1), dimensions={0,1,2}, to_apply=%region_0.1 | reduce | flops 1178624 | bytes 4722692 | tf_op jit(solution)/shard_map/reduce_sum | solution.py:50
  189.1 8.0 %bitcast_multiply_fusion = f32[32,36,1,2,512]{4,3,0,1,2:T(2,128)S(1)} fusion(f32[32,1,36,2,512]{4,1,3,0,2:T(1,128)} %bitcast.41, f32[32]{0:T(128)S(1)} %get-tuple-element.39, f32[32,2,512]{2,1,0:T(2,128)S(1)} %multiply_multiply_fusion, f32[36,2,512]{2,1,0:T(2,128)S(1)} %multiply_add_fusion, f32[32]{0:T(128)S(1)} %get-tuple-element.38), kind=kLoop, calls=%fused_computation.46 | loop fusion | flops 7077888 | bytes 9715968 | tf_op jit(solution)/shard_map/mul | solution.py:57
  197.1 5.0 %copy.45 = f32[32,36,1,2,512]{4,3,2,1,0:T(2,128)} copy(f32[32,36,1,2,512]{4,3,0,1,2:T(2,128)S(1)} %bitcast_multiply_fusion) | data formatting | bytes 9437184
  (43 shorter events, 2.8 us)
Async XLA Ops:
  2.0 16.9 %collective-permute-start = (f32[36,1,512]{2,1,0:T(1,128)S(1)}, f32[36,1,512]{2,1,0:T(1,128)S(1)}, u32[]{:S(2)}, u32[]{:S(2)}) collective-permute-start(f32[36,1,512]{2,1,0:T(1,128)S(1)} %get-tuple-element.28), channel_id=1, source_target_pairs={{0,1},{1,2},{2,3},{4,5},{5,6},{6,7},{8,9},{9,10},{10,11},{12,13},{... | collective-permute-start | bytes 221192 | tf_op jit(solution)/shard_map/ppermute | solution.py:18
  5.4 11.6 %slice-start = ((s8[4718592]{0:T(1024)(128)(4,1)}), s8[4194304]{0:T(1024)(128)(4,1)S(1)}, s32[]{:S(2)}) async-start(s8[4718592]{0:T(1024)(128)(4,1)} %bitcast.45), calls=%async_computation.2 | async-start | bytes 8388608
  5.4 11.6 %slice-start.1 = ((s8[4718592]{0:T(1024)(128)(4,1)}), s8[524288]{0:T(1024)(128)(4,1)S(1)}, s32[]{:S(2)}) async-start(s8[4718592]{0:T(1024)(128)(4,1)} %bitcast.45), calls=%async_computation.3 | async-start | bytes 1048576
  5.4 13.4 %collective-permute-start.1 = (f32[36,1,512]{2,1,0:T(1,128)S(1)}, f32[36,1,512]{2,1,0:T(1,128)S(1)}, u32[]{:S(2)}, u32[]{:S(2)}) collective-permute-start(f32[36,1,512]{2,1,0:T(1,128)S(1)} %get-tuple-element.29), channel_id=1, source_target_pairs={{1,0},{2,1},{3,2},{5,4},{6,5},{7,6},{9,8},{10,9},{11,10},{13,12},{... | collective-permute-start | bytes 221192 | tf_op jit(solution)/shard_map/ppermute | solution.py:19
  17.0 0.7 copy-start.1
  17.0 1.7 copy-start
  32.0 6.3 %collective-permute-start.2 = (f32[36,1,512]{2,1,0:T(1,128)S(1)}, f32[36,1,512]{2,1,0:T(1,128)S(1)}, u32[]{:S(2)}, u32[]{:S(2)}) collective-permute-start(f32[36,1,512]{2,1,0:T(1,128)S(1)} %get-tuple-element.22), channel_id=1, source_target_pairs={{0,1},{1,2},{2,3},{4,5},{5,6},{6,7},{8,9},{9,10},{10,11},{12,13},{... | collective-permute-start | bytes 221192 | tf_op jit(solution)/shard_map/ppermute | solution.py:18
  35.4 6.2 %collective-permute-start.3 = (f32[36,1,512]{2,1,0:T(1,128)S(1)}, f32[36,1,512]{2,1,0:T(1,128)S(1)}, u32[]{:S(2)}, u32[]{:S(2)}) collective-permute-start(f32[36,1,512]{2,1,0:T(1,128)S(1)} %get-tuple-element.23), channel_id=1, source_target_pairs={{1,0},{2,1},{3,2},{5,4},{6,5},{7,6},{9,8},{10,9},{11,10},{13,12},{... | collective-permute-start | bytes 221192 | tf_op jit(solution)/shard_map/ppermute | solution.py:19
  48.6 6.5 %collective-permute-start.4 = (f32[36,1,512]{2,1,0:T(1,128)S(1)}, f32[36,1,512]{2,1,0:T(1,128)S(1)}, u32[]{:S(2)}, u32[]{:S(2)}) collective-permute-start(f32[36,1,512]{2,1,0:T(1,128)S(1)} %get-tuple-element.16), channel_id=1, source_target_pairs={{0,1},{1,2},{2,3},{4,5},{5,6},{6,7},{8,9},{9,10},{10,11},{12,13},{... | collective-permute-start | bytes 221192 | tf_op jit(solution)/shard_map/ppermute | solution.py:18
  51.7 6.2 %collective-permute-start.5 = (f32[36,1,512]{2,1,0:T(1,128)S(1)}, f32[36,1,512]{2,1,0:T(1,128)S(1)}, u32[]{:S(2)}, u32[]{:S(2)}) collective-permute-start(f32[36,1,512]{2,1,0:T(1,128)S(1)} %get-tuple-element.17), channel_id=1, source_target_pairs={{1,0},{2,1},{3,2},{5,4},{6,5},{7,6},{9,8},{10,9},{11,10},{13,12},{... | collective-permute-start | bytes 221192 | tf_op jit(solution)/shard_map/ppermute | solution.py:19
  84.9 13.5 %all-to-all-start.1 = ((f32[4,1,11520]{2,1,0:T(1,128)}), f32[4,1,11520]{2,1,0:T(1,128)S(1)}, u32[]{:S(2)}, u32[]{:S(2)}) async-start(f32[4,1,11520]{2,1,0:T(1,128)} %reshape.267), calls=%async_computation.1 | async-start | bytes 368640 | tf_op jit(solution)/shard_map/all_to_all | solution.py:93
  98.4 8.5 %copy-start.2 = (f32[1,2,512]{2,1,0:T(2,128)S(1)}, f32[1,2,512]{2,1,0:T(2,128)}, u32[]{:S(2)}) copy-start(f32[1,2,512]{2,1,0:T(2,128)} %param.10) | copy-start | bytes 12292
  98.4 8.5 %copy-start.3 = (f32[1,2,512]{2,1,0:T(2,128)S(1)}, f32[1,2,512]{2,1,0:T(2,128)}, u32[]{:S(2)}) copy-start(f32[1,2,512]{2,1,0:T(2,128)} %param.9) | copy-start | bytes 12292
  98.4 71.0 %all-to-all-start = ((f32[1,36,64,512]{3,0,1,2:T(1,128)}), f32[1,36,64,512]{3,0,1,2:T(1,128)}, u32[]{:S(2)}, u32[]{:S(2)}) async-start(f32[1,36,64,512]{3,0,1,2:T(1,128)} %copy.37), calls=%async_computation | async-start | bytes 9437184 | tf_op jit(solution)/shard_map/all_to_all | solution.py:84
where the time goes:
time: 203 us; the launch traced here: 202 us
  waiting for transfers between devices  64.4 us (32%)
  local copies, waits for them, and re-layouts  63.7 us (31%)
  other arithmetic  41.8 us (21%)
  starting transfers between devices  30.5 us (15%)
    all_to_all x1, waiting for transfers between devices, per_device(): lax.all_to_all(result, 'comp', split_axis=2, concat_axis=0, tiled=True)  58.2 us
    mul x4, other arithmetic, substep(): return mask_float * (energy - flux)  22.2 us
    slice x6, local copies, waits for them, and re-layouts, substep(): east = jnp.roll(energy, -1, axis=2)  14.1 us
    mul x1, local copies, waits for them, and re-layouts, substep(): return mask_float * (energy - flux)  10.8 us
    ppermute x3, starting transfers between devices, extended_2(): before = lax.ppermute(last, axis, up)  9.9 us
    all_to_all x1, local copies, waits for them, and re-layouts, per_device(): lax.all_to_all(result, 'comp', split_axis=2, concat_axis=0, tiled=True)  9.84 us
    reshape x1, local copies, waits for them, and re-layouts, per_device(): result = result.reshape(local_freq, dir_width, row_count, col_count)  9.38 us
    all_to_all x1, starting transfers between devices, per_device(): lax.all_to_all(result, 'comp', split_axis=2, concat_axis=0, tiled=True)  8.41 us
  transfers between devices with their start and end apart: 8, of which 3 were waited for; matrix products, arithmetic and copies ran while one was open for 12% of the time, Pallas kernels for 0%

commit v1 on v0

v1 whole, which is shorter than its diff:
```python
import functools

import jax
import jax.numpy as jnp
import numpy as np
from jax import lax
from jax.experimental import pallas as pl
from jax.experimental.pallas import tpu as pltpu
from jax.sharding import PartitionSpec as P

NDIR = 36
NFREQ = 32
SUBSTEPS = 3
HALF = NDIR // 2
QUART = NDIR // 4
ROWS = 64
COLS = 512
LANES = 128
TILES = COLS // LANES
HALO = 3
SLOT = HALO * TILES
PACK = 240
MARGIN = 24
VMEM_LIMIT = 56 * 1024 * 1024

THETA = (2.0 * np.pi * np.arange(NDIR) / NDIR).astype(np.float32)
COS = np.cos(THETA).astype(np.float32)
SIN = np.sin(THETA).astype(np.float32)
SCALE = (0.3 * np.float32(1.1) ** np.arange(NFREQ, dtype=np.float32)).astype(np.float32)
LOG2E = 1.4426950408889634


def pack_kernel(last_ref, first_ref, mask_ref, up_ref, down_ref):
    for out, src, low, row in ((up_ref, last_ref, 5, 56), (down_ref, first_ref, 0, 0)):
        for d in range(HALF):
            for j in range(TILES):
                out[pl.ds(d * SLOT + j, HALO, stride=TILES), :] = src[
                    d, low : low + HALO, j * LANES : (j + 1) * LANES
                ]
        m = mask_ref[0, row : row + 8, :].astype(jnp.float32)
        for j in range(TILES):
            out[pl.ds(HALF * SLOT + j, HALO, stride=TILES), :] = m[
                low : low + HALO, j * LANES : (j + 1) * LANES
            ]
        out[(HALF + 1) * SLOT :, :] = jnp.zeros((PACK - (HALF + 1) * SLOT, LANES), jnp.float32)


def pack(spectrum, sea_mask):
    block = (HALF, 8, COLS)
    out = jax.ShapeDtypeStruct((PACK, LANES), jnp.float32)
    return pl.pallas_call(
        pack_kernel,
        grid=(1,),
        in_specs=[
            pl.BlockSpec(block, lambda i: (0, ROWS // 8 - 1, 0)),
            pl.BlockSpec(block, lambda i: (1, 0, 0)),
            pl.BlockSpec((1, ROWS, COLS), lambda i: (0, 0, 0)),
        ],
        out_specs=[pl.BlockSpec((PACK, LANES), lambda i: (0, 0))] * 2,
        out_shape=[out, out],
        compiler_params=pltpu.CompilerParams(vmem_limit_bytes=VMEM_LIMIT),
        name="pack",
    )(spectrum, spectrum, sea_mask)


def propagate_kernel(per, courant_ref, trig_ref, e_ref, mask_ref, south_ref, north_ref, out_ref, mask_s, mask_n, halo_s):
    step = pl.program_id(0)

    def halo_tile(slot, low):
        parts = [
            halo_s[pl.ds(MARGIN + slot * SLOT + j - low * TILES, 8, stride=TILES), :]
            for j in range(TILES)
        ]
        return jnp.concatenate(parts, axis=1)

    def load_halo(src):
        halo_s[0:MARGIN, :] = jnp.zeros((MARGIN, LANES), jnp.float32)
        halo_s[MARGIN : MARGIN + PACK, :] = src[...]

    @pl.when(step == 0)
    def _():
        load_halo(south_ref)
        m = mask_ref[0].astype(jnp.float32)
        mask_s[8:, :] = m
        mask_s[:8, :] = halo_tile(HALF, 5)
        mask_n[:ROWS, :] = m

    @pl.when(step == HALF // per)
    def _():
        load_halo(north_ref)
        mask_n[ROWS:, :] = halo_tile(HALF, 0)

    flat = out_ref.reshape(32 * per * 8, LANES)

    def advance(south, west):
        def body(k, carry):
            d = step * per + k
            slot = d if south else d - HALF
            a = courant_ref[0] * trig_ref[0, d]
            b = courant_ref[0] * trig_ref[1, d]
            c = 1.0 - a - b
            e = e_ref[k]
            if south:
                e = jnp.concatenate([halo_tile(slot, 5), e], axis=0)
                m = mask_s[...]
            else:
                e = jnp.concatenate([e, halo_tile(slot, 0)], axis=0)
                m = mask_n[...]
            for _ in range(SUBSTEPS):
                x = pltpu.roll(e, 1 if west else COLS - 1, 1)
                y = pltpu.roll(e, 1 if south else ROWS + 7, 0)
                e = m * (c * e + a * x + b * y)
            e = e[8:] if south else e[:ROWS]
            for j in range(TILES):
                flat[pl.ds(j, ROWS, stride=TILES), :] = e[:, j * LANES : (j + 1) * LANES]
            return carry

        lax.fori_loop(0, per, body, 0)

    quarter = step // (QUART // per)
    for q, (south, west) in enumerate(((True, True), (True, False), (False, False), (False, True))):
        pl.when(quarter == q)(functools.partial(advance, south, west))


def propagate(spectrum, courant, sea_mask, from_south, from_north):
    per = 1
    trig = jnp.asarray(np.stack([np.abs(COS), np.abs(SIN)]))
    whole = lambda *shape: pl.BlockSpec(shape, lambda i: (0,) * len(shape))
    return pl.pallas_call(
        functools.partial(propagate_kernel, per),
        grid=(NDIR // per,),
        in_specs=[
            pl.BlockSpec(memory_space=pltpu.SMEM),
            pl.BlockSpec(memory_space=pltpu.SMEM),
            pl.BlockSpec((per, ROWS, COLS), lambda i: (i, 0, 0)),
            whole(1, ROWS, COLS),
            whole(PACK, LANES),
            whole(PACK, LANES),
        ],
        out_specs=pl.BlockSpec((32, per, 8, LANES), lambda i: (0, i, 0, 0)),
        out_shape=jax.ShapeDtypeStruct((32, NDIR, 8, LANES), jnp.float32),
        scratch_shapes=[
            pltpu.VMEM((ROWS + 8, COLS), jnp.float32),
            pltpu.VMEM((ROWS + 8, COLS), jnp.float32),
            pltpu.VMEM((MARGIN + PACK + 16, LANES), jnp.float32),
        ],
        compiler_params=pltpu.CompilerParams(vmem_limit_bytes=VMEM_LIMIT),
        name="propagate",
    )(courant, trig, spectrum, sea_mask, from_south, from_north)


def pick_kernel(grp_ref, cells_ref, p_ref, *out_refs):
    group = grp_ref[0]
    count = len(out_refs)
    lane = lax.broadcasted_iota(jnp.int32, (NDIR, LANES), 1)
    points = LANES // count
    for k, out in enumerate(out_refs):
        owner = lax.rem(group + k, count)
        nests = out.shape[0]

        def nest_body(n, carry):
            def point_body(p, acc):
                for u in range(8):
                    col = group * points + p * 8 + u
                    cell = cells_ref[owner * nests + n, col] - group * (ROWS * COLS)
                    y = lax.shift_right_logical(cell, 9)
                    x = lax.bitwise_and(cell, COLS - 1)
                    row = lax.shift_right_logical(y, 1) * (NDIR * 8) + lax.bitwise_and(y, 1) * 4 + lax.shift_right_logical(x, 7)
                    got = p_ref[pl.ds(row, NDIR, stride=8), :]
                    turn = lax.bitwise_and(col - x, LANES - 1)
                    acc = jnp.where(lane == col, pltpu.roll(got, turn, 1), acc)
                return acc

            out[n] = lax.fori_loop(0, points // 8, point_body, jnp.zeros((NDIR, LANES), jnp.float32))
            return carry

        lax.fori_loop(0, nests, nest_body, 0)


def pick(group, cells, moved, count):
    nests = cells.shape[0] // count
    return pl.pallas_call(
        pick_kernel,
        in_specs=[
            pl.BlockSpec(memory_space=pltpu.SMEM),
            pl.BlockSpec(memory_space=pltpu.SMEM),
            pl.BlockSpec(memory_space=pltpu.VMEM),
        ],
        out_specs=[pl.BlockSpec(memory_space=pltpu.VMEM)] * count,
        out_shape=[jax.ShapeDtypeStruct((nests, NDIR, LANES), jnp.float32)] * count,
        compiler_params=pltpu.CompilerParams(vmem_limit_bytes=VMEM_LIMIT),
        cost_estimate=pl.CostEstimate(flops=10_000_000, bytes_accessed=6_000_000, transcendentals=0),
        name="pick",
    )(group, cells, moved.reshape(32 * NDIR * 8, LANES))


def merge_kernel(*refs):
    *ins, out = refs
    for n in range(ins[0].shape[0]):
        total = ins[0][n]
        for r in ins[1:]:
            total = total + r[n]
        out[:, n, :] = total


def merge(parts):
    nests = parts[0].shape[0]
    return pl.pallas_call(
        merge_kernel,
        out_shape=jax.ShapeDtypeStruct((NDIR, nests, LANES), jnp.float32),
        name="merge",
    )(*parts)


FCHUNK = 4
NCHUNK = NFREQ // FCHUNK


def source_kernel(recv_ref, u_ref, v_ref, out_ref, buf, outbuf, sem, osem):
    for c in range(NCHUNK):
        pltpu.make_async_copy(recv_ref.at[pl.ds(c * FCHUNK, FCHUNK)], buf.at[pl.ds(c * FCHUNK, FCHUNK)], sem.at[c]).start()
    total = jnp.zeros((8, LANES), jnp.float32)
    weighted = jnp.zeros((8, LANES), jnp.float32)
    for c in range(NCHUNK):
        pltpu.make_async_copy(recv_ref.at[pl.ds(c * FCHUNK, FCHUNK)], buf.at[pl.ds(c * FCHUNK, FCHUNK)], sem.at[c]).wait()
        for i in range(FCHUNK):
            f = c * FCHUNK + i
            s = jnp.sum(buf[f], axis=0)
            total = total + s
            weighted = weighted + s * float(SCALE[f] * SCALE[f])
    m0 = total * (1.0 / (NFREQ * NDIR))
    q = weighted * (1.0 / (NFREQ * NDIR))
    ratio = jnp.maximum(m0, 0.05) / jnp.maximum(q, 0.1)
    steep = m0 / 0.3
    base = ratio * (steep * steep)
    sub = lax.broadcasted_iota(jnp.int32, (8, LANES), 0)
    order = lax.rem(sub, 2) * 4 + lax.div(sub, 2)
    shuffle = lambda value: jnp.take_along_axis(value, order, axis=0)
    base = shuffle(base)
    u = u_ref[...]
    v = v_ref[...]

    for c in range(NCHUNK):
        fs = range(c * FCHUNK, (c + 1) * FCHUNK)
        loss = [base * float(0.1 * SCALE[f] ** 3 * LOG2E) for f in fs]
        for d in range(NDIR):
            proj = u * float(COS[d]) + v * float(SIN[d])
            for i, f in enumerate(fs):
                gain = jnp.maximum(proj * float(0.05 * SCALE[f] ** 2 * LOG2E) - float(0.05 * SCALE[f] * LOG2E), 0.0)
                outbuf[f, d] = shuffle(buf[f, d]) * jnp.exp2(gain - loss[i])
        pltpu.make_async_copy(outbuf.at[pl.ds(c * FCHUNK, FCHUNK)], out_ref.at[pl.ds(c * FCHUNK, FCHUNK)], osem.at[c]).start()
    for c in range(NCHUNK):
        pltpu.make_async_copy(outbuf.at[pl.ds(c * FCHUNK, FCHUNK)], out_ref.at[pl.ds(c * FCHUNK, FCHUNK)], osem.at[c]).wait()


def sources(recv, wind_u, wind_v):
    tile = lambda w: w.reshape(2, TILES, LANES).transpose(1, 0, 2).reshape(8, LANES)
    shape = (NFREQ, NDIR, 8, LANES)
    out = pl.pallas_call(
        source_kernel,
        in_specs=[
            pl.BlockSpec(memory_space=pl.ANY),
            pl.BlockSpec(memory_space=pltpu.VMEM),
            pl.BlockSpec(memory_space=pltpu.VMEM),
        ],
        out_specs=pl.BlockSpec(memory_space=pl.ANY),
        out_shape=jax.ShapeDtypeStruct(shape, jnp.float32),
        scratch_shapes=[
            pltpu.VMEM(shape, jnp.float32),
            pltpu.VMEM(shape, jnp.float32),
            pltpu.SemaphoreType.DMA((NCHUNK,)),
            pltpu.SemaphoreType.DMA((NCHUNK,)),
        ],
        compiler_params=pltpu.CompilerParams(vmem_limit_bytes=VMEM_LIMIT),
        name="sources",
    )(recv, tile(wind_u), tile(wind_v))
    out = out.reshape(NFREQ, NDIR, TILES, 2, LANES).transpose(0, 1, 3, 2, 4)
    return out.reshape(NFREQ, NDIR, 1, 2, COLS)


def per_device(spectrum, courant, sea_mask, wind_u, wind_v, boundary_cells):
    size = lax.axis_size("grp")
    group = lax.axis_index("grp").astype(jnp.int32).reshape(1)
    block = spectrum.reshape(NDIR, ROWS, COLS)
    up, down = pack(block, sea_mask)
    from_south = lax.ppermute(up, "grp", [(i, i + 1) for i in range(size - 1)])
    from_north = lax.ppermute(down, "grp", [(i + 1, i) for i in range(size - 1)])
    result = propagate(block, courant, sea_mask, from_south, from_north)
    moved = lax.all_to_all(result, "comp", split_axis=0, concat_axis=0, tiled=True)
    picked = pick(group, boundary_cells, result, size)
    parts = [picked[0]]
    for k in range(1, size):
        parts.append(lax.ppermute(picked[k], "grp", [(i, (i + k) % size) for i in range(size)]))
    boundary = merge(parts)[None]
    updated = sources(moved, wind_u.reshape(2, COLS), wind_v.reshape(2, COLS))
    return updated, boundary


def solution(mesh):
    placed = (
        P("comp", None, "grp", None, None),
        P("comp"),
        P("grp", None, None),
        P("grp", "comp", None),
        P("grp", "comp", None),
        P(),
    )
    return jax.shard_map(
        per_device,
        mesh=mesh,
        in_specs=placed,
        out_specs=(P(None, None, "grp", "comp", None), P("comp", None, "grp", None)),
        check_vma=False,
    )
```

time: 203 us -> 116 us (0.57)
  local copies, waits for them, and re-layouts: 63.7 us -> 3.16 us
  Pallas kernels: 0 us -> 58.5 us
  other arithmetic: 41.8 us -> 0 us
  waiting for transfers between devices: 64.4 us -> 34.8 us
  starting transfers between devices: 30.5 us -> 17.4 us
    pallas_call x0 -> x5, Pallas kernels: none -> 58.5 us  [the longest x1 25.1 us: propagate(): pl.pallas_call(functools.partial(propagate_kernel, per), grid=(NDIR // pe...]
    all_to_all x2 -> x1, waiting for transfers between devices: 58.2 us -> 20.4 us  [per_device(): lax.all_to_all(result, 'comp', split_axis=0, concat_axis=0, tiled=True)]
    mul x9 -> x0, other arithmetic: 30.4 us -> none  [the longest x4 22.2 us: substep(): return mask_float * (energy - flux)]
    slice x9 -> x0, local copies, waits for them, and re-layouts: 15.7 us -> none  [the longest x6 14.1 us: substep(): east = jnp.roll(energy, -1, axis=2)]
    mul x1 -> x0, local copies, waits for them, and re-layouts: 10.8 us -> none  [substep(): return mask_float * (energy - flux)]
    all_to_all x4 -> x0, local copies, waits for them, and re-layouts: 10.8 us -> none  [the longest x1 9.84 us: per_device(): lax.all_to_all(result, 'comp', split_axis=2, concat_axis=0, tiled=True)]
    reshape x3 -> x0, local copies, waits for them, and re-layouts: 10.6 us -> none  [the longest x1 9.38 us: per_device(): result = result.reshape(local_freq, dir_width, row_count, col_count)]
    reduce_sum x2 -> x0, other arithmetic: 9.72 us -> none  [the longest x1 4.87 us: sources(): mean_energy = jnp.mean(energy, axis=(0, 1))]
  transfers between devices with their start and end apart: 8 -> 6, of which waited for: 3 -> 6; matrix products, arithmetic and copies ran while one was open for 12% -> 2% of each run, Pallas kernels for 0% -> 23%
where the time goes in v1:
time: 116 us; the launch traced here: 115 us
  Pallas kernels  58.5 us (50%)
  waiting for transfers between devices  34.8 us (30%)
  starting transfers between devices  17.4 us (15%)
  local copies, waits for them, and re-layouts  3.16 us (3%)
  between operations  1.32 us (1%)
    pallas_call x1, Pallas kernels, propagate(): pl.pallas_call(functools.partial(propagate_kernel, per), grid=(NDIR // pe...  25.1 us
    pallas_call x1, Pallas kernels, pick(): pl.pallas_call(pick_kernel, in_specs=[pl.BlockSpec(memory_space=pltpu.SME...  23.9 us
    all_to_all x1, waiting for transfers between devices, per_device(): lax.all_to_all(result, 'comp', split_axis=0, concat_axis=0, tiled=True)  20.4 us
    ppermute x3, waiting for transfers between devices, per_device(): lax.ppermute(picked[k], 'grp', [(i, (i + k) % size) for i in range(size)])  10.5 us
    all_to_all x1, starting transfers between devices, per_device(): lax.all_to_all(result, 'comp', split_axis=0, concat_axis=0, tiled=True)  8.26 us
    pallas_call x1, Pallas kernels, sources(): pl.pallas_call(source_kernel, in_specs=[pl.BlockSpec(memory_space=pl.ANY)...  5.54 us
    ppermute x1, starting transfers between devices, per_device(): from_south = lax.ppermute(up, 'grp', [(i, i + 1) for i in range(size - 1)])  3.39 us
    ppermute x3, starting transfers between devices, per_device(): lax.ppermute(picked[k], 'grp', [(i, (i + k) % size) for i in range(size)])  3.27 us
  transfers between devices with their start and end apart: 6, of which 6 were waited for; matrix products, arithmetic and copies ran while one was open for 2% of the time, Pallas kernels for 23%

profile of v1, /device:TPU:34, one launch (start us, length us, event | category | flops | bytes accessed | tf_op | source)
XLA Modules:
  0.0 115.1 jit_solution(17699755092684940245)
XLA Ops:
  0.6 1.9 %pack.1 = (f32[240,128]{1,0:T(8,128)}, f32[240,128]{1,0:T(8,128)}) custom-call(f32[36,64,512]{2,1,0:T(8,128)} %bitcast.19, f32[36,64,512]{2,1,0:T(8,128)} %bitcast.20, s32[1,64,512]{2,1,0:T(8,128)} %mask_ref.3), custom_call_target="tpu_custom_call" | custom-call | tf_op jit(solution)/shard_map/pack/pallas_call | solution.py:51
  2.5 3.4 %collective-permute-start = (f32[240,128]{1,0:T(8,128)}, f32[240,128]{1,0:T(8,128)S(1)}, u32[]{:S(2)}, u32[]{:S(2)}) collective-permute-start(f32[240,128]{1,0:T(8,128)} %get-tuple-element.8), channel_id=1, source_target_pairs={{0,1},{1,2},{2,3},{4,5},{5,6},{6,7},{8,9},{9,10},{10,11},{12,13},{... | collective-permute-start | bytes 368648 | tf_op jit(solution)/shard_map/ppermute | solution.py:286
  5.9 2.4 %collective-permute-start.1 = (f32[240,128]{1,0:T(8,128)}, f32[240,128]{1,0:T(8,128)S(1)}, u32[]{:S(2)}, u32[]{:S(2)}) collective-permute-start(f32[240,128]{1,0:T(8,128)} %get-tuple-element.9), channel_id=1, source_target_pairs={{1,0},{2,1},{3,2},{5,4},{6,5},{7,6},{9,8},{10,9},{11,10},{13,12},{... | collective-permute-start | bytes 368648 | tf_op jit(solution)/shard_map/ppermute | solution.py:287
  9.0 0.7 collective-permute-done.south_ref
  9.6 0.0 copy-start.3
  9.6 3.2 %collective-permute-done.1.north_ref = f32[240,128]{1,0:T(8,128)S(1)} collective-permute-done((f32[240,128]{1,0:T(8,128)}, f32[240,128]{1,0:T(8,128)S(1)}, u32[]{:S(2)}, u32[]{:S(2)}) %collective-permute-start.1) | collective-permute-done | bytes 122912 | tf_op jit(solution)/shard_map/ppermute | solution.py:287
  12.9 0.0 copy-done.3
  12.9 0.0 copy-start.4
  12.9 0.6 copy-done.4
  13.5 25.1 %propagate.1 = f32[32,36,8,128]{3,2,1,0:T(8,128)} custom-call(f32[1]{0:T(128)S(6)} %copy.13.courant_ref, f32[2,36]{1,0:T(2,128)} %constant.6.clone.trig_ref, f32[36,64,512]{2,1,0:T(8,128)} %bitcast.21, s32[1,64,512]{2,1,0:T(8,128)} %mask_ref.3, f32[240,128]{1,0:T(8,128)} %copy-done.3, f32[240,128]{1,0:T(8,128)} %copy-done.4), custom_call_target="tpu_custom_call" | custom-call | tf_op jit(solution)/shard_map/propagate/pallas_call | solution.py:129
  38.6 8.3 %all-to-all-start = ((f32[32,36,8,128]{3,2,1,0:T(8,128)}), f32[32,36,8,128]{3,2,1,0:T(8,128)}, u32[]{:S(2)}, u32[]{:S(2)}) async-start(f32[32,36,8,128]{3,2,1,0:T(8,128)} %propagate.1), calls=%async_computation | async-start | bytes 9437184 | tf_op jit(solution)/shard_map/all_to_all | solution.py:289
  46.9 23.9 %pick.1 = (f32[10,36,128]{2,1,0:T(8,128)}, f32[10,36,128]{2,1,0:T(8,128)}, f32[10,36,128]{2,1,0:T(8,128)}, f32[10,36,128]{2,1,0:T(8,128)}) custom-call(s32[1]{0:T(128)} %bitcast.10.grp_ref, s32[40,128]{1,0:T(8,128)} %cells_ref.1, f32[9216,128]{1,0:T(8,128)} %bitcast.22), custom_call_target="tpu_custom_call" | custom-call | flops 10000000 | bytes 6000000 | tf_op jit(solution)/shard_map/pick/pallas_call | solution.py:182
  70.8 1.2 %collective-permute-start.2 = (f32[10,36,128]{2,1,0:T(8,128)}, f32[10,36,128]{2,1,0:T(8,128)S(1)}, u32[]{:S(2)}, u32[]{:S(2)}) collective-permute-start(f32[10,36,128]{2,1,0:T(8,128)} %get-tuple-element.11), channel_id=1, source_target_pairs={{0,1},{1,2},{2,3},{3,0},{4,5},{5,6},{6,7},{7,4},{8,9},{9,10},{10,1... | collective-permute-start | bytes 552968 | tf_op jit(solution)/shard_map/ppermute | solution.py:293
  72.0 1.4 %collective-permute-start.3 = (f32[10,36,128]{2,1,0:T(8,128)}, f32[10,36,128]{2,1,0:T(8,128)S(1)}, u32[]{:S(2)}, u32[]{:S(2)}) collective-permute-start(f32[10,36,128]{2,1,0:T(8,128)} %get-tuple-element.12), channel_id=1, source_target_pairs={{0,2},{1,3},{2,0},{3,1},{4,6},{5,7},{6,4},{7,5},{8,10},{9,11},{10,... | collective-permute-start | bytes 552968 | tf_op jit(solution)/shard_map/ppermute | solution.py:293
  73.4 0.7 collective-permute-start.4
  74.0 4.9 %collective-permute-done.2.refs_1_ = f32[10,36,128]{2,1,0:T(8,128)S(1)} collective-permute-done((f32[10,36,128]{2,1,0:T(8,128)}, f32[10,36,128]{2,1,0:T(8,128)S(1)}, u32[]{:S(2)}, u32[]{:S(2)}) %collective-permute-start.2) | collective-permute-done | bytes 184352 | tf_op jit(solution)/shard_map/ppermute | solution.py:293
  78.9 0.0 copy-start
  78.9 2.7 %collective-permute-done.3.refs_2_ = f32[10,36,128]{2,1,0:T(8,128)S(1)} collective-permute-done((f32[10,36,128]{2,1,0:T(8,128)}, f32[10,36,128]{2,1,0:T(8,128)S(1)}, u32[]{:S(2)}, u32[]{:S(2)}) %collective-permute-start.3) | collective-permute-done | bytes 184352 | tf_op jit(solution)/shard_map/ppermute | solution.py:293
  81.7 0.0 copy-start.1
  81.7 2.9 %collective-permute-done.4.refs_3_ = f32[10,36,128]{2,1,0:T(8,128)S(1)} collective-permute-done((f32[10,36,128]{2,1,0:T(8,128)}, f32[10,36,128]{2,1,0:T(8,128)S(1)}, u32[]{:S(2)}, u32[]{:S(2)}) %collective-permute-start.4) | collective-permute-done | bytes 184352 | tf_op jit(solution)/shard_map/ppermute | solution.py:293
  84.6 0.0 copy-start.2
  84.6 0.0 copy-done
  84.6 0.0 copy-done.1
  84.6 0.7 copy-done.2
  85.2 2.1 %merge.1 = f32[36,10,128]{2,1,0:T(8,128)} custom-call(f32[10,36,128]{2,1,0:T(8,128)} %get-tuple-element.10.refs_0_, f32[10,36,128]{2,1,0:T(8,128)} %copy-done, f32[10,36,128]{2,1,0:T(8,128)} %copy-done.1, f32[10,36,128]{2,1,0:T(8,128)} %copy-done.2), custom_call_target="tpu_custom_call" | custom-call | tf_op jit(solution)/shard_map/merge/pallas_call | solution.py:208
  87.3 1.8 %copy.12 = f32[1,36,10,128]{3,0,2,1:T(1,128)} copy(f32[1,36,10,128]{3,2,1,0:T(8,128)} %bitcast.24) | data formatting | bytes 368640
  89.2 20.4 %all-to-all-done.recv_ref = f32[32,36,8,128]{3,2,1,0:T(8,128)} async-done(((f32[32,36,8,128]{3,2,1,0:T(8,128)}), f32[32,36,8,128]{3,2,1,0:T(8,128)}, u32[]{:S(2)}, u32[]{:S(2)}) %all-to-all-start) | async-done | bytes 4718624 | tf_op jit(solution)/shard_map/all_to_all | solution.py:289
  109.6 5.5 %sources.1 = f32[32,36,8,128]{3,2,1,0:T(8,128)} custom-call(f32[32,36,8,128]{3,2,1,0:T(8,128)} %all-to-all-done.recv_ref, f32[8,128]{1,0:T(8,128)} %bitcast.25, f32[8,128]{1,0:T(8,128)} %bitcast.26), custom_call_target="tpu_custom_call" | custom-call | tf_op jit(solution)/shard_map/sources/pallas_call | solution.py:259
Async XLA Ops:
  2.5 7.2 %collective-permute-start = (f32[240,128]{1,0:T(8,128)}, f32[240,128]{1,0:T(8,128)S(1)}, u32[]{:S(2)}, u32[]{:S(2)}) collective-permute-start(f32[240,128]{1,0:T(8,128)} %get-tuple-element.8), channel_id=1, source_target_pairs={{0,1},{1,2},{2,3},{4,5},{5,6},{6,7},{8,9},{9,10},{10,11},{12,13},{... | collective-permute-start | bytes 368648 | tf_op jit(solution)/shard_map/ppermute | solution.py:286
  5.9 7.0 %collective-permute-start.1 = (f32[240,128]{1,0:T(8,128)}, f32[240,128]{1,0:T(8,128)S(1)}, u32[]{:S(2)}, u32[]{:S(2)}) collective-permute-start(f32[240,128]{1,0:T(8,128)} %get-tuple-element.9), channel_id=1, source_target_pairs={{1,0},{2,1},{3,2},{5,4},{6,5},{7,6},{9,8},{10,9},{11,10},{13,12},{... | collective-permute-start | bytes 368648 | tf_op jit(solution)/shard_map/ppermute | solution.py:287
  9.6 3.2 %copy-start.3 = (f32[240,128]{1,0:T(8,128)}, f32[240,128]{1,0:T(8,128)S(1)}, u32[]{:S(2)}) copy-start(f32[240,128]{1,0:T(8,128)S(1)} %collective-permute-done.south_ref) | copy-start | bytes 368644
  12.9 0.7 copy-start.4
  38.6 71.0 %all-to-all-start = ((f32[32,36,8,128]{3,2,1,0:T(8,128)}), f32[32,36,8,128]{3,2,1,0:T(8,128)}, u32[]{:S(2)}, u32[]{:S(2)}) async-start(f32[32,36,8,128]{3,2,1,0:T(8,128)} %propagate.1), calls=%async_computation | async-start | bytes 9437184 | tf_op jit(solution)/shard_map/all_to_all | solution.py:289
  70.8 8.1 %collective-permute-start.2 = (f32[10,36,128]{2,1,0:T(8,128)}, f32[10,36,128]{2,1,0:T(8,128)S(1)}, u32[]{:S(2)}, u32[]{:S(2)}) collective-permute-start(f32[10,36,128]{2,1,0:T(8,128)} %get-tuple-element.11), channel_id=1, source_target_pairs={{0,1},{1,2},{2,3},{3,0},{4,5},{5,6},{6,7},{7,4},{8,9},{9,10},{10,1... | collective-permute-start | bytes 552968 | tf_op jit(solution)/shard_map/ppermute | solution.py:293
  72.0 9.7 %collective-permute-start.3 = (f32[10,36,128]{2,1,0:T(8,128)}, f32[10,36,128]{2,1,0:T(8,128)S(1)}, u32[]{:S(2)}, u32[]{:S(2)}) collective-permute-start(f32[10,36,128]{2,1,0:T(8,128)} %get-tuple-element.12), channel_id=1, source_target_pairs={{0,2},{1,3},{2,0},{3,1},{4,6},{5,7},{6,4},{7,5},{8,10},{9,11},{10,... | collective-permute-start | bytes 552968 | tf_op jit(solution)/shard_map/ppermute | solution.py:293
  73.4 11.2 %collective-permute-start.4 = (f32[10,36,128]{2,1,0:T(8,128)}, f32[10,36,128]{2,1,0:T(8,128)S(1)}, u32[]{:S(2)}, u32[]{:S(2)}) collective-permute-start(f32[10,36,128]{2,1,0:T(8,128)} %get-tuple-element.13), channel_id=1, source_target_pairs={{0,3},{1,0},{2,1},{3,2},{4,7},{5,4},{6,5},{7,6},{8,11},{9,8},{10,9... | collective-permute-start | bytes 552968 | tf_op jit(solution)/shard_map/ppermute | solution.py:293
  78.9 5.6 %copy-start = (f32[10,36,128]{2,1,0:T(8,128)}, f32[10,36,128]{2,1,0:T(8,128)S(1)}, u32[]{:S(2)}) copy-start(f32[10,36,128]{2,1,0:T(8,128)S(1)} %collective-permute-done.2.refs_1_) | copy-start | bytes 552964
  81.7 2.9 %copy-start.1 = (f32[10,36,128]{2,1,0:T(8,128)}, f32[10,36,128]{2,1,0:T(8,128)S(1)}, u32[]{:S(2)}) copy-start(f32[10,36,128]{2,1,0:T(8,128)S(1)} %collective-permute-done.3.refs_2_) | copy-start | bytes 552964
  84.6 0.7 copy-start.2

commit v2 on v1

--- a/solution.py
+++ b/solution.py
@@ -18,9 +18,10 @@
 LANES = 128
 TILES = COLS // LANES
 HALO = 3
-SLOT = HALO * TILES
-PACK = 240
-MARGIN = 24
+EDGE = 4
+SLOT = HALO * HALF + 2
+PACK = TILES * SLOT
+ROWBLOCK = TILES * 8
 VMEM_LIMIT = 56 * 1024 * 1024
 
 THETA = (2.0 * np.pi * np.arange(NDIR) / NDIR).astype(np.float32)
@@ -30,89 +31,103 @@
 LOG2E = 1.4426950408889634
 
 
-def pack_kernel(last_ref, first_ref, mask_ref, up_ref, down_ref):
-    for out, src, low, row in ((up_ref, last_ref, 5, 56), (down_ref, first_ref, 0, 0)):
-        for d in range(HALF):
-            for j in range(TILES):
-                out[pl.ds(d * SLOT + j, HALO, stride=TILES), :] = src[
-                    d, low : low + HALO, j * LANES : (j + 1) * LANES
-                ]
-        m = mask_ref[0, row : row + 8, :].astype(jnp.float32)
+def tiled(value):
+    lead = value.shape[:-2]
+    n = len(lead)
+    value = value.reshape(*lead, ROWS // 8, 8, TILES, LANES)
+    return value.transpose(*range(n), n, n + 2, n + 1, n + 3)
+
+
+def groups():
+    return ((0, 8), (8, 8), (16, 2))
+
+
+def pack_kernel(spectrum_ref, mask_ref, up_ref, down_ref, last, first, sem):
+    copies = [
+        pltpu.make_async_copy(spectrum_ref.at[pl.ds(0, HALF), ROWS // 8 - 1], last, sem.at[0]),
+        pltpu.make_async_copy(spectrum_ref.at[pl.ds(HALF, HALF), 0], first, sem.at[1]),
+    ]
+    for c in copies:
+        c.start()
+    flat_mask = mask_ref.reshape(ROWS * TILES, LANES)
+    for c, out, src, low, mrow in (
+        (copies[0], up_ref, last, 5, (ROWS // 8 - 1) * ROWBLOCK + 6),
+        (copies[1], down_ref, first, 0, 0),
+    ):
         for j in range(TILES):
-            out[pl.ds(HALF * SLOT + j, HALO, stride=TILES), :] = m[
-                low : low + HALO, j * LANES : (j + 1) * LANES
-            ]
-        out[(HALF + 1) * SLOT :, :] = jnp.zeros((PACK - (HALF + 1) * SLOT, LANES), jnp.float32)
-
-
-def pack(spectrum, sea_mask):
-    block = (HALF, 8, COLS)
+            m = flat_mask[mrow + j * 8 : mrow + j * 8 + 2, :]
+            out[j * SLOT + HALO * HALF : (j + 1) * SLOT, :] = m.astype(jnp.float32)
+        c.wait()
+        flat = src.reshape(HALF * ROWBLOCK, LANES)
+        for j in range(TILES):
+            for h in range(HALO):
+                for g, n in groups():
+                    row = j * SLOT + h * HALF + g
+                    out[row : row + n, :] = flat[pl.ds(g * ROWBLOCK + j * 8 + low + h, n, stride=ROWBLOCK), :]
+
+
+def pack(spectrum, mask):
     out = jax.ShapeDtypeStruct((PACK, LANES), jnp.float32)
+    edge = pltpu.VMEM((HALF, TILES, 8, LANES), jnp.float32)
     return pl.pallas_call(
         pack_kernel,
-        grid=(1,),
-        in_specs=[
-            pl.BlockSpec(block, lambda i: (0, ROWS // 8 - 1, 0)),
-            pl.BlockSpec(block, lambda i: (1, 0, 0)),
-            pl.BlockSpec((1, ROWS, COLS), lambda i: (0, 0, 0)),
-        ],
-        out_specs=[pl.BlockSpec((PACK, LANES), lambda i: (0, 0))] * 2,
+        in_specs=[pl.BlockSpec(memory_space=pl.ANY), pl.BlockSpec(memory_space=pltpu.VMEM)],
+        out_specs=[pl.BlockSpec(memory_space=pltpu.VMEM)] * 2,
         out_shape=[out, out],
+        scratch_shapes=[edge, edge, pltpu.SemaphoreType.DMA((2,))],
         compiler_params=pltpu.CompilerParams(vmem_limit_bytes=VMEM_LIMIT),
         name="pack",
-    )(spectrum, spectrum, sea_mask)
-
-
-def propagate_kernel(per, courant_ref, trig_ref, e_ref, mask_ref, south_ref, north_ref, out_ref, mask_s, mask_n, halo_s):
+    )(spectrum, mask)
+
+
+def interior_kernel(per, courant_ref, trig_ref, e_ref, mask_ref, out_ref, mask_s):
     step = pl.program_id(0)
-
-    def halo_tile(slot, low):
-        parts = [
-            halo_s[pl.ds(MARGIN + slot * SLOT + j - low * TILES, 8, stride=TILES), :]
-            for j in range(TILES)
-        ]
-        return jnp.concatenate(parts, axis=1)
-
-    def load_halo(src):
-        halo_s[0:MARGIN, :] = jnp.zeros((MARGIN, LANES), jnp.float32)
-        halo_s[MARGIN : MARGIN + PACK, :] = src[...]
+    lane = lax.broadcasted_iota(jnp.int32, (8, LANES), 1)
+    flat = out_ref.reshape(32 * per * 8, LANES)
+    src = e_ref.reshape(per * ROWS * TILES, LANES)
 
     @pl.when(step == 0)
     def _():
-        load_halo(south_ref)
-        m = mask_ref[0].astype(jnp.float32)
-        mask_s[8:, :] = m
-        mask_s[:8, :] = halo_tile(HALF, 5)
-        mask_n[:ROWS, :] = m
-
-    @pl.when(step == HALF // per)
-    def _():
-        load_halo(north_ref)
-        mask_n[ROWS:, :] = halo_tile(HALF, 0)
-
-    flat = out_ref.reshape(32 * per * 8, LANES)
+        flat_mask = mask_ref.reshape(ROWS * TILES, LANES)
+        for t in range(8):
+            for j in range(TILES):
+                mask_s[t, j] = flat_mask[pl.ds(j * 8 + t, 8, stride=ROWBLOCK), :].astype(jnp.float32)
 
     def advance(south, west):
         def body(k, carry):
             d = step * per + k
-            slot = d if south else d - HALF
             a = courant_ref[0] * trig_ref[0, d]
             b = courant_ref[0] * trig_ref[1, d]
             c = 1.0 - a - b
-            e = e_ref[k]
-            if south:
-                e = jnp.concatenate([halo_tile(slot, 5), e], axis=0)
-                m = mask_s[...]
-            else:
-                e = jnp.concatenate([e, halo_tile(slot, 0)], axis=0)
-                m = mask_n[...]
+            e = [
+                [src[pl.ds(k * ROWS * TILES + j * 8 + t, 8, stride=ROWBLOCK), :] for j in range(TILES)]
+                for t in range(8)
+            ]
             for _ in range(SUBSTEPS):
-                x = pltpu.roll(e, 1 if west else COLS - 1, 1)
-                y = pltpu.roll(e, 1 if south else ROWS + 7, 0)
-                e = m * (c * e + a * x + b * y)
-            e = e[8:] if south else e[:ROWS]
-            for j in range(TILES):
-                flat[pl.ds(j, ROWS, stride=TILES), :] = e[:, j * LANES : (j + 1) * LANES]
+                if south:
+                    wrap = [pltpu.roll(e[7][j], 1, 0) for j in range(TILES)]
+                else:
+                    wrap = [pltpu.roll(e[0][j], 7, 0) for j in range(TILES)]
+                new = [None] * 8
+                for t in range(8):
+                    if south:
+                        y = e[t - 1] if t > 0 else wrap
+                    else:
+                        y = e[t + 1] if t < 7 else wrap
+                    r = [pltpu.roll(e[t][j], 1 if west else LANES - 1, 1) for j in range(TILES)]
+                    row = []
+                    for j in range(TILES):
+                        if west:
+                            x = jnp.where(lane == 0, r[j - 1], r[j])
+                        else:
+                            x = jnp.where(lane == LANES - 1, r[(j + 1) % TILES], r[j])
+                        row.append(mask_s[t, j] * (c * e[t][j] + a * x + b * y[j]))
+                    new[t] = row
+                e = new
+            for t in range(8):
+                for j in range(TILES):
+                    row = (t // 2) * per * 8 + k * 8 + 2 * j + t % 2
+                    flat[pl.ds(row, 8, stride=ROWBLOCK * per), :] = e[t][j]
             return carry
 
         lax.fori_loop(0, per, body, 0)
@@ -122,31 +137,134 @@
         pl.when(quarter == q)(functools.partial(advance, south, west))
 
 
-def propagate(spectrum, courant, sea_mask, from_south, from_north):
-    per = 1
+def interior(spectrum, courant, mask):
+    per = PER
     trig = jnp.asarray(np.stack([np.abs(COS), np.abs(SIN)]))
-    whole = lambda *shape: pl.BlockSpec(shape, lambda i: (0,) * len(shape))
     return pl.pallas_call(
-        functools.partial(propagate_kernel, per),
+        functools.partial(interior_kernel, per),
         grid=(NDIR // per,),
         in_specs=[
             pl.BlockSpec(memory_space=pltpu.SMEM),
             pl.BlockSpec(memory_space=pltpu.SMEM),
-            pl.BlockSpec((per, ROWS, COLS), lambda i: (i, 0, 0)),
-            whole(1, ROWS, COLS),
-            whole(PACK, LANES),
-            whole(PACK, LANES),
+            pl.BlockSpec((per, ROWS // 8, TILES, 8, LANES), lambda i: (i, 0, 0, 0, 0)),
+            pl.BlockSpec(memory_space=pltpu.VMEM),
         ],
         out_specs=pl.BlockSpec((32, per, 8, LANES), lambda i: (0, i, 0, 0)),
         out_shape=jax.ShapeDtypeStruct((32, NDIR, 8, LANES), jnp.float32),
+        scratch_shapes=[pltpu.VMEM((8, TILES, 8, LANES), jnp.float32)],
+        compiler_params=pltpu.CompilerParams(vmem_limit_bytes=VMEM_LIMIT),
+        cost_estimate=pl.CostEstimate(flops=40_000_000, bytes_accessed=9_500_000, transcendentals=0),
+        name="interior",
+    )(courant, trig, spectrum, mask)
+
+
+PER = 3
+
+
+def edges_kernel(courant_ref, trig_ref, spectrum_ref, mask_ref, south_ref, north_ref, p_in, p_ref, first, last, out, sem):
+    del p_in
+    loads = [
+        pltpu.make_async_copy(spectrum_ref.at[pl.ds(0, HALF), 0], first, sem.at[0]),
+        pltpu.make_async_copy(spectrum_ref.at[pl.ds(HALF, HALF), ROWS // 8 - 1], last, sem.at[1]),
+    ]
+    for c in loads:
+        c.start()
+    lane = lax.broadcasted_iota(jnp.int32, (8, LANES), 1)
+    sub = lax.broadcasted_iota(jnp.int32, (8, LANES), 0)
+    flat_mask = mask_ref.reshape(ROWS * TILES, LANES)
+    total = HALO + EDGE
+    stores = []
+
+    def eight(ref, start, n, stride):
+        value = ref[pl.ds(start, n, stride=stride), :]
+        if n < 8:
+            value = jnp.concatenate([value, jnp.zeros((8 - n, LANES), jnp.float32)], axis=0)
+        return value
+
+    for side, (edge, halo) in enumerate(((first, south_ref), (last, north_ref))):
+        south = side == 0
+        loads[side].wait()
+        flat = edge.reshape(HALF * ROWBLOCK, LANES)
+        flat_out = out.at[side].reshape(2 * HALF * 8, LANES)
+        own = lambda p: (p - HALO) if south else (7 - (p - HALO))
+        base = 0 if south else (ROWS // 8 - 1) * ROWBLOCK
+        m = []
+        for p in range(total):
+            row = []
+            for j in range(TILES):
+                if p < HALO:
+                    at = j * SLOT + HALO * HALF + (p - 1 if south else HALO - 1 - p)
+                    value = halo[at : at + 1, :] if p > 0 else None
+                else:
+                    at = base + j * 8 + own(p)
+                    value = flat_mask[at : at + 1, :].astype(jnp.float32)
+                row.append(value)
+            m.append(row)
+        for g, n in groups():
+            a = courant_ref[0] * trig_ref[2 * side, g : g + 8, :]
+            b = courant_ref[0] * trig_ref[2 * side + 1, g : g + 8, :]
+            c = 1.0 - a - b
+            turned = sub + g >= QUART
+            e = []
+            for p in range(total):
+                row = []
+                for j in range(TILES):
+                    if p < HALO:
+                        h = p if south else HALO - 1 - p
+                        row.append(eight(halo, j * SLOT + h * HALF + g, n, 1))
+                    else:
+                        row.append(eight(flat, g * ROWBLOCK + j * 8 + own(p), n, ROWBLOCK))
+                e.append(row)
+            for k in range(SUBSTEPS):
+                new = [None] * total
+                for p in range(k + 1, total):
+                    rw = [pltpu.roll(e[p][j], 1, 1) for j in range(TILES)]
+                    re = [pltpu.roll(e[p][j], LANES - 1, 1) for j in range(TILES)]
+                    row = []
+                    for j in range(TILES):
+                        xw = jnp.where(lane == 0, rw[j - 1], rw[j])
+                        xe = jnp.where(lane == LANES - 1, re[(j + 1) % TILES], re[j])
+                        x = jnp.where(turned, xe, xw) if south else jnp.where(turned, xw, xe)
+                        row.append(m[p][j] * (c * e[p][j] + a * x + b * e[p - 1][j]))
+                    new[p] = row
+                e = new
+            for p in range(HALO, total):
+                y = p - HALO if south else EDGE - 1 - (p - HALO)
+                for j in range(TILES):
+                    at = ((y // 2) * HALF + g) * 8 + 2 * j + y % 2
+                    flat_out[pl.ds(at, n, stride=8), :] = e[p][j][:n]
+        target = p_ref.at[pl.ds(0 if south else 30, 2), pl.ds(0 if south else HALF, HALF)]
+        copy = pltpu.make_async_copy(out.at[side], target, sem.at[2 + side])
+        copy.start()
+        stores.append(copy)
+    for copy in stores:
+        copy.wait()
+
+
+def edges(spectrum, courant, mask, from_south, from_north, inner):
+    table = np.zeros((4, 24, LANES), np.float32)
+    for side in range(2):
+        ds = slice(side * HALF, (side + 1) * HALF)
+        table[2 * side, :HALF] = np.abs(COS[ds])[:, None]
+        table[2 * side + 1, :HALF] = np.abs(SIN[ds])[:, None]
+    edge = pltpu.VMEM((HALF, TILES, 8, LANES), jnp.float32)
+    vmem = pl.BlockSpec(memory_space=pltpu.VMEM)
+    hbm = pl.BlockSpec(memory_space=pl.ANY)
+    return pl.pallas_call(
+        edges_kernel,
+        in_specs=[pl.BlockSpec(memory_space=pltpu.SMEM), vmem, hbm, vmem, vmem, vmem, hbm],
+        out_specs=hbm,
+        out_shape=jax.ShapeDtypeStruct(inner.shape, inner.dtype),
         scratch_shapes=[
-            pltpu.VMEM((ROWS + 8, COLS), jnp.float32),
-            pltpu.VMEM((ROWS + 8, COLS), jnp.float32),
-            pltpu.VMEM((MARGIN + PACK + 16, LANES), jnp.float32),
+            edge,
+            edge,
+            pltpu.VMEM((2, 2, HALF, 8, LANES), jnp.float32),
+            pltpu.SemaphoreType.DMA((4,)),
         ],
+        input_output_aliases={6: 0},
         compiler_params=pltpu.CompilerParams(vmem_limit_bytes=VMEM_LIMIT),
-        name="propagate",
-    )(courant, trig, spectrum, sea_mask, from_south, from_north)
+        name="edges",
+    )(courant, jnp.asarray(table), spectrum, mask, from_south, from_north, inner)
 
 
 def pick_kernel(grp_ref, cells_ref, p_ref, *out_refs):
@@ -165,7 +283,7 @@
                     cell = cells_ref[owner * nests + n, col] - group * (ROWS * COLS)
                     y = lax.shift_right_logical(cell, 9)
                     x = lax.bitwise_and(cell, COLS - 1)
-                    row = lax.shift_right_logical(y, 1) * (NDIR * 8) + lax.bitwise_and(y, 1) * 4 + lax.shift_right_logical(x, 7)
+                    row = lax.shift_right_logical(y, 1) * (NDIR * 8) + lax.shift_right_logical(x, 7) * 2 + lax.bitwise_and(y, 1)
                     got = p_ref[pl.ds(row, NDIR, stride=8), :]
                     turn = lax.bitwise_and(col - x, LANES - 1)
                     acc = jnp.where(lane == col, pltpu.roll(got, turn, 1), acc)
@@ -233,10 +351,6 @@
     ratio = jnp.maximum(m0, 0.05) / jnp.maximum(q, 0.1)
     steep = m0 / 0.3
     base = ratio * (steep * steep)
-    sub = lax.broadcasted_iota(jnp.int32, (8, LANES), 0)
-    order = lax.rem(sub, 2) * 4 + lax.div(sub, 2)
-    shuffle = lambda value: jnp.take_along_axis(value, order, axis=0)
-    base = shuffle(base)
     u = u_ref[...]
     v = v_ref[...]
 
@@ -247,7 +361,7 @@
             proj = u * float(COS[d]) + v * float(SIN[d])
             for i, f in enumerate(fs):
                 gain = jnp.maximum(proj * float(0.05 * SCALE[f] ** 2 * LOG2E) - float(0.05 * SCALE[f] * LOG2E), 0.0)
-                outbuf[f, d] = shuffle(buf[f, d]) * jnp.exp2(gain - loss[i])
+                outbuf[f, d] = buf[f, d] * jnp.exp2(gain - loss[i])
         pltpu.make_async_copy(outbuf.at[pl.ds(c * FCHUNK, FCHUNK)], out_ref.at[pl.ds(c * FCHUNK, FCHUNK)], osem.at[c]).start()
     for c in range(NCHUNK):
         pltpu.make_async_copy(outbuf.at[pl.ds(c * FCHUNK, FCHUNK)], out_ref.at[pl.ds(c * FCHUNK, FCHUNK)], osem.at[c]).wait()
@@ -281,11 +395,13 @@
 def per_device(spectrum, courant, sea_mask, wind_u, wind_v, boundary_cells):
     size = lax.axis_size("grp")
     group = lax.axis_index("grp").astype(jnp.int32).reshape(1)
-    block = spectrum.reshape(NDIR, ROWS, COLS)
-    up, down = pack(block, sea_mask)
+    block = tiled(spectrum.reshape(NDIR, ROWS, COLS))
+    mask = tiled(sea_mask.reshape(ROWS, COLS))
+    up, down = pack(block, mask)
     from_south = lax.ppermute(up, "grp", [(i, i + 1) for i in range(size - 1)])
     from_north = lax.ppermute(down, "grp", [(i + 1, i) for i in range(size - 1)])
-    result = propagate(block, courant, sea_mask, from_south, from_north)
+    inner = interior(block, courant, mask)
+    result = edges(block, courant, mask, from_south, from_north, inner)
     moved = lax.all_to_all(result, "comp", split_axis=0, concat_axis=0, tiled=True)
     picked = pick(group, boundary_cells, result, size)
     parts = [picked[0]]

time: 116 us -> 106 us (0.914)
  Pallas kernels: 58.5 us -> 52.2 us
  waiting for transfers between devices: 34.8 us -> 29.4 us
  starting transfers between devices: 17.4 us -> 18.9 us
    pallas_call x2 -> x3, Pallas kernels: 27 us -> 20.7 us  [the longest x1 14.5 us: interior(): pl.pallas_call(functools.partial(interior_kernel, per), grid=(NDIR // per...]
    ppermute x1, waiting for transfers between devices: 3.22 us -> 0.01 us  [per_device(): lax.ppermute(down, 'grp', [(i + 1, i) for i in range(size - 1)])]
    ppermute x3, waiting for transfers between devices: 10.5 us -> 8.82 us  [per_device(): lax.ppermute(picked[k], 'grp', [(i, (i + k) % size) for i in range(size)])]
    ppermute x3, starting transfers between devices: 3.27 us -> 4.76 us  [per_device(): lax.ppermute(picked[k], 'grp', [(i, (i + k) % size) for i in range(size)])]
  transfers between devices with their start and end apart: 6 -> 6, of which waited for: 6 -> 4; matrix products, arithmetic and copies ran while one was open for 2% -> 2% of each run, Pallas kernels for 23% -> 38%
where the time goes in v2:
time: 106 us
  Pallas kernels  52.2 us (49%)
  waiting for transfers between devices  29.4 us (28%)
  starting transfers between devices  18.9 us (18%)
  local copies, waits for them, and re-layouts  3.79 us (4%)
  between operations  1.33 us (1%)
    pallas_call x1, Pallas kernels, pick(): pl.pallas_call(pick_kernel, in_specs=[pl.BlockSpec(memory_space=pltpu.SME...  23.9 us
    all_to_all x1, waiting for transfers between devices, per_device(): lax.all_to_all(result, 'comp', split_axis=0, concat_axis=0, tiled=True)  20.6 us
    pallas_call x1, Pallas kernels, interior(): pl.pallas_call(functools.partial(interior_kernel, per), grid=(NDIR // per...  14.5 us
    ppermute x3, waiting for transfers between devices, per_device(): lax.ppermute(picked[k], 'grp', [(i, (i + k) % size) for i in range(size)])  8.82 us
    all_to_all x1, starting transfers between devices, per_device(): lax.all_to_all(result, 'comp', split_axis=0, concat_axis=0, tiled=True)  8.27 us
    pallas_call x1, Pallas kernels, sources(): pl.pallas_call(source_kernel, in_specs=[pl.BlockSpec(memory_space=pl.ANY)...  5.51 us
    ppermute x3, starting transfers between devices, per_device(): lax.ppermute(picked[k], 'grp', [(i, (i + k) % size) for i in range(size)])  4.76 us
    unnamed x11, local copies, waits for them, and re-layouts  3.79 us
  transfers between devices with their start and end apart: 6, of which 4 were waited for; matrix products, arithmetic and copies ran while one was open for 2% of the time, Pallas kernels for 38%

profile of v2, /device:TPU:34, one launch (start us, length us, event | category | flops | bytes accessed | tf_op | source)
XLA Modules:
  0.0 105.7 jit_solution(16189226123808622521)
XLA Ops:
  0.6 2.7 %pack.1 = (f32[224,128]{1,0:T(8,128)}, f32[224,128]{1,0:T(8,128)}) custom-call(f32[36,8,4,8,128]{4,3,2,1,0:T(8,128)} %bitcast.25, s32[8,4,8,128]{3,2,1,0:T(8,128)} %bitcast.29), custom_call_target="tpu_custom_call" | custom-call | tf_op jit(solution)/shard_map/pack/pallas_call | solution.py:72
  3.3 3.4 %collective-permute-start = (f32[224,128]{1,0:T(8,128)}, f32[224,128]{1,0:T(8,128)S(1)}, u32[]{:S(2)}, u32[]{:S(2)}) collective-permute-start(f32[224,128]{1,0:T(8,128)} %get-tuple-element.8), channel_id=1, source_target_pairs={{0,1},{1,2},{2,3},{4,5},{5,6},{6,7},{8,9},{9,10},{10,11},{12,13},{... | collective-permute-start | bytes 344072 | tf_op jit(solution)/shard_map/ppermute | solution.py:401
  6.7 2.4 %collective-permute-start.1 = (f32[224,128]{1,0:T(8,128)}, f32[224,128]{1,0:T(8,128)S(1)}, u32[]{:S(2)}, u32[]{:S(2)}) collective-permute-start(f32[224,128]{1,0:T(8,128)} %get-tuple-element.9), channel_id=1, source_target_pairs={{1,0},{2,1},{3,2},{5,4},{6,5},{7,6},{9,8},{10,9},{11,10},{13,12},{... | collective-permute-start | bytes 344072 | tf_op jit(solution)/shard_map/ppermute | solution.py:402
  9.8 14.5 %interior.1.p_in = f32[32,36,8,128]{3,2,1,0:T(8,128)} custom-call(f32[1]{0:T(128)S(6)} %copy.16.courant_ref, f32[2,36]{1,0:T(2,128)} %constant.8.clone.trig_ref, f32[36,8,4,8,128]{4,3,2,1,0:T(8,128)} %bitcast.26, s32[8,4,8,128]{3,2,1,0:T(8,128)} %bitcast.30), custom_call_target="tpu_custom_call" | custom-call | flops 40000000 | bytes 9500000 | tf_op jit(solution)/shard_map/interior/pallas_call | solution.py:143
  24.4 0.0 collective-permute-done.south_ref
  24.4 0.0 copy-start.3
  24.4 0.0 collective-permute-done.1.north_ref
  24.4 0.6 copy-done.3
  25.0 0.0 copy-start.4
  25.0 0.6 copy-done.4
  25.7 3.5 %edges.1 = f32[32,36,8,128]{3,2,1,0:T(8,128)} custom-call(f32[1]{0:T(128)S(6)} %copy.16.courant_ref, f32[4,24,128]{2,1,0:T(8,128)} %constant.9.clone.trig_ref, f32[36,8,4,8,128]{4,3,2,1,0:T(8,128)} %bitcast.27, s32[8,4,8,128]{3,2,1,0:T(8,128)} %bitcast.31, f32[224,128]{1,0:T(8,128)} %copy-done.3, ...), custom_call_target="tpu_custom_call", output_to_operand_aliasing={{}: (6, {})} | custom-call | tf_op jit(solution)/shard_map/edges/pallas_call | solution.py:253
  29.2 8.3 %all-to-all-start = ((f32[32,36,8,128]{3,2,1,0:T(8,128)}), f32[32,36,8,128]{3,2,1,0:T(8,128)}, u32[]{:S(2)}, u32[]{:S(2)}) async-start(f32[32,36,8,128]{3,2,1,0:T(8,128)} %edges.1), calls=%async_computation | async-start | bytes 9437184 | tf_op jit(solution)/shard_map/all_to_all | solution.py:405
  37.5 23.9 %pick.1 = (f32[10,36,128]{2,1,0:T(8,128)}, f32[10,36,128]{2,1,0:T(8,128)}, f32[10,36,128]{2,1,0:T(8,128)}, f32[10,36,128]{2,1,0:T(8,128)}) custom-call(s32[1]{0:T(128)} %bitcast.15.grp_ref, s32[40,128]{1,0:T(8,128)} %cells_ref.1, f32[9216,128]{1,0:T(8,128)} %bitcast.24), custom_call_target="tpu_custom_call" | custom-call | flops 10000000 | bytes 6000000 | tf_op jit(solution)/shard_map/pick/pallas_call | solution.py:300
  61.4 1.5 %collective-permute-start.2 = (f32[10,36,128]{2,1,0:T(8,128)}, f32[10,36,128]{2,1,0:T(8,128)S(1)}, u32[]{:S(2)}, u32[]{:S(2)}) collective-permute-start(f32[10,36,128]{2,1,0:T(8,128)} %get-tuple-element.11), channel_id=1, source_target_pairs={{0,1},{1,2},{2,3},{3,0},{4,5},{5,6},{6,7},{7,4},{8,9},{9,10},{10,1... | collective-permute-start | bytes 552968 | tf_op jit(solution)/shard_map/ppermute | solution.py:409
  62.8 0.6 collective-permute-start.3
  63.5 2.6 %collective-permute-start.4 = (f32[10,36,128]{2,1,0:T(8,128)}, f32[10,36,128]{2,1,0:T(8,128)S(1)}, u32[]{:S(2)}, u32[]{:S(2)}) collective-permute-start(f32[10,36,128]{2,1,0:T(8,128)} %get-tuple-element.13), channel_id=1, source_target_pairs={{0,3},{1,0},{2,1},{3,2},{4,7},{5,4},{6,5},{7,6},{8,11},{9,8},{10,9... | collective-permute-start | bytes 552968 | tf_op jit(solution)/shard_map/ppermute | solution.py:409
  66.1 3.4 %collective-permute-done.2.refs_1_ = f32[10,36,128]{2,1,0:T(8,128)S(1)} collective-permute-done((f32[10,36,128]{2,1,0:T(8,128)}, f32[10,36,128]{2,1,0:T(8,128)S(1)}, u32[]{:S(2)}, u32[]{:S(2)}) %collective-permute-start.2) | collective-permute-done | bytes 184352 | tf_op jit(solution)/shard_map/ppermute | solution.py:409
  69.5 0.0 copy-start
  69.5 3.0 %collective-permute-done.3.refs_2_ = f32[10,36,128]{2,1,0:T(8,128)S(1)} collective-permute-done((f32[10,36,128]{2,1,0:T(8,128)}, f32[10,36,128]{2,1,0:T(8,128)S(1)}, u32[]{:S(2)}, u32[]{:S(2)}) %collective-permute-start.3) | collective-permute-done | bytes 184352 | tf_op jit(solution)/shard_map/ppermute | solution.py:409
  72.5 0.0 copy-start.1
  72.5 2.4 %collective-permute-done.4.refs_3_ = f32[10,36,128]{2,1,0:T(8,128)S(1)} collective-permute-done((f32[10,36,128]{2,1,0:T(8,128)}, f32[10,36,128]{2,1,0:T(8,128)S(1)}, u32[]{:S(2)}, u32[]{:S(2)}) %collective-permute-start.4) | collective-permute-done | bytes 184352 | tf_op jit(solution)/shard_map/ppermute | solution.py:409
  74.9 0.0 copy-start.2
  74.9 0.0 copy-done
  74.9 0.0 copy-done.1
  74.9 0.7 copy-done.2
  75.6 2.1 %merge.1 = f32[36,10,128]{2,1,0:T(8,128)} custom-call(f32[10,36,128]{2,1,0:T(8,128)} %get-tuple-element.10.refs_0_, f32[10,36,128]{2,1,0:T(8,128)} %copy-done, f32[10,36,128]{2,1,0:T(8,128)} %copy-done.1, f32[10,36,128]{2,1,0:T(8,128)} %copy-done.2), custom_call_target="tpu_custom_call" | custom-call | tf_op jit(solution)/shard_map/merge/pallas_call | solution.py:326
  77.7 1.8 %copy.14 = f32[1,36,10,128]{3,0,2,1:T(1,128)} copy(f32[1,36,10,128]{3,2,1,0:T(8,128)} %bitcast.32) | data formatting | bytes 368640
  79.5 20.6 %all-to-all-done.recv_ref = f32[32,36,8,128]{3,2,1,0:T(8,128)} async-done(((f32[32,36,8,128]{3,2,1,0:T(8,128)}), f32[32,36,8,128]{3,2,1,0:T(8,128)}, u32[]{:S(2)}, u32[]{:S(2)}) %all-to-all-start) | async-done | bytes 4718624 | tf_op jit(solution)/shard_map/all_to_all | solution.py:405
  100.1 5.5 %sources.1 = f32[32,36,8,128]{3,2,1,0:T(8,128)} custom-call(f32[32,36,8,128]{3,2,1,0:T(8,128)} %all-to-all-done.recv_ref, f32[8,128]{1,0:T(8,128)} %bitcast.33, f32[8,128]{1,0:T(8,128)} %bitcast.34), custom_call_target="tpu_custom_call" | custom-call | tf_op jit(solution)/shard_map/sources/pallas_call | solution.py:373
Async XLA Ops:
  3.3 21.0 %collective-permute-start = (f32[224,128]{1,0:T(8,128)}, f32[224,128]{1,0:T(8,128)S(1)}, u32[]{:S(2)}, u32[]{:S(2)}) collective-permute-start(f32[224,128]{1,0:T(8,128)} %get-tuple-element.8), channel_id=1, source_target_pairs={{0,1},{1,2},{2,3},{4,5},{5,6},{6,7},{8,9},{9,10},{10,11},{12,13},{... | collective-permute-start | bytes 344072 | tf_op jit(solution)/shard_map/ppermute | solution.py:401
  6.7 17.6 %collective-permute-start.1 = (f32[224,128]{1,0:T(8,128)}, f32[224,128]{1,0:T(8,128)S(1)}, u32[]{:S(2)}, u32[]{:S(2)}) collective-permute-start(f32[224,128]{1,0:T(8,128)} %get-tuple-element.9), channel_id=1, source_target_pairs={{1,0},{2,1},{3,2},{5,4},{6,5},{7,6},{9,8},{10,9},{11,10},{13,12},{... | collective-permute-start | bytes 344072 | tf_op jit(solution)/shard_map/ppermute | solution.py:402
  24.4 0.6 copy-start.3
  25.0 0.6 copy-start.4
  29.2 71.0 %all-to-all-start = ((f32[32,36,8,128]{3,2,1,0:T(8,128)}), f32[32,36,8,128]{3,2,1,0:T(8,128)}, u32[]{:S(2)}, u32[]{:S(2)}) async-start(f32[32,36,8,128]{3,2,1,0:T(8,128)} %edges.1), calls=%async_computation | async-start | bytes 9437184 | tf_op jit(solution)/shard_map/all_to_all | solution.py:405
  61.4 8.1 %collective-permute-start.2 = (f32[10,36,128]{2,1,0:T(8,128)}, f32[10,36,128]{2,1,0:T(8,128)S(1)}, u32[]{:S(2)}, u32[]{:S(2)}) collective-permute-start(f32[10,36,128]{2,1,0:T(8,128)} %get-tuple-element.11), channel_id=1, source_target_pairs={{0,1},{1,2},{2,3},{3,0},{4,5},{5,6},{6,7},{7,4},{8,9},{9,10},{10,1... | collective-permute-start | bytes 552968 | tf_op jit(solution)/shard_map/ppermute | solution.py:409
  62.8 9.7 %collective-permute-start.3 = (f32[10,36,128]{2,1,0:T(8,128)}, f32[10,36,128]{2,1,0:T(8,128)S(1)}, u32[]{:S(2)}, u32[]{:S(2)}) collective-permute-start(f32[10,36,128]{2,1,0:T(8,128)} %get-tuple-element.12), channel_id=1, source_target_pairs={{0,2},{1,3},{2,0},{3,1},{4,6},{5,7},{6,4},{7,5},{8,10},{9,11},{10,... | collective-permute-start | bytes 552968 | tf_op jit(solution)/shard_map/ppermute | solution.py:409
  63.5 11.5 %collective-permute-start.4 = (f32[10,36,128]{2,1,0:T(8,128)}, f32[10,36,128]{2,1,0:T(8,128)S(1)}, u32[]{:S(2)}, u32[]{:S(2)}) collective-permute-start(f32[10,36,128]{2,1,0:T(8,128)} %get-tuple-element.13), channel_id=1, source_target_pairs={{0,3},{1,0},{2,1},{3,2},{4,7},{5,4},{6,5},{7,6},{8,11},{9,8},{10,9... | collective-permute-start | bytes 552968 | tf_op jit(solution)/shard_map/ppermute | solution.py:409
  69.5 5.5 %copy-start = (f32[10,36,128]{2,1,0:T(8,128)}, f32[10,36,128]{2,1,0:T(8,128)S(1)}, u32[]{:S(2)}) copy-start(f32[10,36,128]{2,1,0:T(8,128)S(1)} %collective-permute-done.2.refs_1_) | copy-start | bytes 552964
  72.5 2.4 %copy-start.1 = (f32[10,36,128]{2,1,0:T(8,128)}, f32[10,36,128]{2,1,0:T(8,128)S(1)}, u32[]{:S(2)}) copy-start(f32[10,36,128]{2,1,0:T(8,128)S(1)} %collective-permute-done.3.refs_2_) | copy-start | bytes 552964
  74.9 0.7 copy-start.2

commit v3 on v1

v3 whole, which is shorter than its diff:
```python
import functools

import jax
import jax.numpy as jnp
import numpy as np
from jax import lax
from jax.experimental import pallas as pl
from jax.experimental.pallas import tpu as pltpu
from jax.sharding import PartitionSpec as P

NDIR = 36
NFREQ = 32
SUBSTEPS = 3
HALF = NDIR // 2
QUART = NDIR // 4
ROWS = 64
COLS = 512
LANES = 128
TILES = COLS // LANES
HALO = 3
SLOTS = HALF + 2
SLOT = TILES * HALO
ROWBLOCK = TILES * 8
MIB = 1024 * 1024

THETA = (2.0 * np.pi * np.arange(NDIR) / NDIR).astype(np.float32)
COS = np.cos(THETA).astype(np.float32)
SIN = np.sin(THETA).astype(np.float32)
SCALE = (0.3 * np.float32(1.1) ** np.arange(NFREQ, dtype=np.float32)).astype(np.float32)
LOG2E = 1.4426950408889634


def tiled(value):
    lead = value.shape[:-2]
    n = len(lead)
    value = value.reshape(*lead, ROWS // 8, 8, TILES, LANES)
    return value.transpose(*range(n), n, n + 2, n + 1, n + 3)


def in_hbm(value):
    return pltpu.with_memory_space_constraint(value, pltpu.HBM)


def pack_kernel(spectrum_ref, mask_ref, up_ref, down_ref, mask_s, sem):
    sides = ((up_ref, 0, ROWS // 8 - 1, 8 - HALO), (down_ref, HALF, 0, 0))
    copies = []
    for side, (out, d, tile, low) in enumerate(sides):
        for k, (src, dst) in enumerate((
            (spectrum_ref.at[pl.ds(d, HALF), tile, :, pl.ds(low, HALO)], out.at[pl.ds(0, HALF)]),
            (mask_ref.at[tile, :, pl.ds(low, HALO)], mask_s.at[side]),
        )):
            copies.append(pltpu.make_async_copy(src, dst, sem.at[2 * side + k]))
    for c in copies:
        c.start()
    for side in range(2):
        copies[2 * side + 1].wait()
        sides[side][0][HALF] = mask_s[side].astype(jnp.float32)
    for side in range(2):
        copies[2 * side].wait()


def pack(spectrum, mask):
    out = jax.ShapeDtypeStruct((SLOTS, TILES, HALO, 1, LANES), jnp.float32)
    up, down = pl.pallas_call(
        pack_kernel,
        in_specs=[pl.BlockSpec(memory_space=pl.ANY)] * 2,
        out_specs=[pl.BlockSpec(memory_space=pltpu.VMEM)] * 2,
        out_shape=[out, out],
        scratch_shapes=[pltpu.VMEM((2, TILES, HALO, 1, LANES), jnp.int32), pltpu.SemaphoreType.DMA((4,))],
        compiler_params=pltpu.CompilerParams(vmem_limit_bytes=2 * MIB),
        name="pack",
    )(in_hbm(spectrum[..., None, :]), in_hbm(mask[..., None, :]))
    return up.reshape(SLOTS * SLOT, LANES), down.reshape(SLOTS * SLOT, LANES)


FETCH = 3
INTER = FETCH


def propagate_kernel(
    courant_ref, trig_ref, table_ref, e_ref, mask_ref, south_ref, north_ref, out_ref, e_buf, out_buf, mask_s, edge_s, sem, out_sem
):
    fetch = lambda c: pltpu.make_async_copy(e_ref.at[pl.ds(c * FETCH, FETCH)], e_buf.at[pl.ds(c * FETCH, FETCH)], sem.at[c])
    put = lambda c: pltpu.make_async_copy(out_buf.at[:, pl.ds(c * FETCH, FETCH)], out_ref.at[:, pl.ds(c * FETCH, FETCH)], out_sem.at[c])
    for c in range(NDIR // FETCH):
        fetch(c).start()
    lane = lax.broadcasted_iota(jnp.int32, (8, LANES), 1)
    sub = lax.broadcasted_iota(jnp.int32, (8, LANES), 0)

    def shifted(row, west):
        r = [pltpu.roll(v, 1 if west else LANES - 1, 1) for v in row]
        if west:
            return [jnp.where(lane == 0, r[j - 1], r[j]) for j in range(TILES)]
        return [jnp.where(lane == LANES - 1, r[(j + 1) % TILES], r[j]) for j in range(TILES)]

    mask_s[...] = mask_ref[...].astype(jnp.float32)

    for side, halo in enumerate((south_ref, north_ref)):
        south = side == 0
        near = lambda p: HALO - 1 - p if south else p
        m = [[halo[HALF * SLOT + j * HALO + near(p) : HALF * SLOT + j * HALO + near(p) + 1, :] for j in range(TILES)] for p in range(2)]
        for g, n in ((0, 8), (8, 8), (16, 2)):
            a = courant_ref[0] * table_ref[2 * side, g : g + 8, :]
            b = courant_ref[0] * table_ref[2 * side + 1, g : g + 8, :]
            c = 1.0 - a - b
            turned = sub + g >= QUART
            rows = []
            for p in range(HALO):
                row = []
                for j in range(TILES):
                    v = halo[pl.ds(g * SLOT + j * HALO + near(p), n, stride=SLOT), :]
                    row.append(v if n == 8 else jnp.concatenate([v, jnp.zeros((8 - n, LANES), jnp.float32)], axis=0))
                rows.append(row)
            for k in range(HALO):
                for j in range(TILES):
                    edge_s[side, k, j, g : g + 8, :] = rows[0][j]
                new = []
                for p in range(len(rows) - 1):
                    w, e = shifted(rows[p], True), shifted(rows[p], False)
                    x = [jnp.where(turned, e[j], w[j]) if south else jnp.where(turned, w[j], e[j]) for j in range(TILES)]
                    new.append([m[p][j] * (c * rows[p][j] + a * x[j] + b * rows[p + 1][j]) for j in range(TILES)])
                rows = new

    def advance(south, west, first, i, carry):
        ds = [first + i * INTER + u for u in range(INTER)]
        many = range(INTER)
        side = 0 if south else 1
        at, turn = (0, 1) if south else (7, 7)
        fetch(first // FETCH + i).wait()
        a = [courant_ref[0] * trig_ref[0, d] for d in ds]
        b = [courant_ref[0] * trig_ref[1, d] for d in ds]
        c = [1.0 - x - y for x, y in zip(a, b)]
        e = [[[e_buf[d, t, j] for j in range(TILES)] for t in range(8)] for d in ds]
        for stage in range(SUBSTEPS):
            new = [[None] * 8 for _ in many]
            moved = [[[pltpu.roll(v, turn, 0) for v in row] for row in e[u]] for u in many]
            for t in range(8):
                for u in many:
                    if t == at:
                        beyond = [edge_s[side, stage, j, pl.ds(ds[u] - side * HALF, 1), :] for j in range(TILES)]
                    else:
                        beyond = moved[u][t - 1 if south else t + 1]
                    x = shifted(e[u][t], west)
                    y = [jnp.where(sub == at, beyond[j], moved[u][t][j]) for j in range(TILES)]
                    new[u][t] = [mask_s[t, j] * (c[u] * e[u][t][j] + a[u] * x[j] + b[u] * y[j]) for j in range(TILES)]
            e = new
        odd, high = sub & 2 != 0, sub >= 4
        for u in many:
            for t in range(8):
                v = e[u][t]
                w = [
                    jnp.where(odd, pltpu.roll(v[1], 2, 0), v[0]),
                    jnp.where(odd, v[1], pltpu.roll(v[0], 6, 0)),
                    jnp.where(odd, pltpu.roll(v[3], 2, 0), v[2]),
                    jnp.where(odd, v[3], pltpu.roll(v[2], 6, 0)),
                ]
                out_buf[4 * t, ds[u]] = jnp.where(high, pltpu.roll(w[2], 4, 0), w[0])
                out_buf[4 * t + 1, ds[u]] = jnp.where(high, pltpu.roll(w[3], 4, 0), w[1])
                out_buf[4 * t + 2, ds[u]] = jnp.where(high, w[2], pltpu.roll(w[0], 4, 0))
                out_buf[4 * t + 3, ds[u]] = jnp.where(high, w[3], pltpu.roll(w[1], 4, 0))
        put(first // FETCH + i).start()
        return carry

    for q, (south, west) in enumerate(((True, True), (True, False), (False, False), (False, True))):
        lax.fori_loop(0, QUART // INTER, functools.partial(advance, south, west, q * QUART), 0)
    for c in range(NDIR // FETCH):
        put(c).wait()


def propagate(spectrum, courant, mask, from_south, from_north):
    trig = np.stack([np.abs(COS), np.abs(SIN)])
    table = np.zeros((4, 24, LANES), np.float32)
    for side in range(2):
        ds = slice(side * HALF, (side + 1) * HALF)
        table[2 * side, :HALF] = np.abs(COS[ds])[:, None]
        table[2 * side + 1, :HALF] = np.abs(SIN[ds])[:, None]
    smem = pl.BlockSpec(memory_space=pltpu.SMEM)
    vmem = pl.BlockSpec(memory_space=pltpu.VMEM)
    return pl.pallas_call(
        propagate_kernel,
        in_specs=[smem, smem, vmem, pl.BlockSpec(memory_space=pl.ANY), vmem, vmem, vmem],
        out_specs=pl.BlockSpec(memory_space=pl.ANY),
        out_shape=pltpu.HBM((32, NDIR, 8, LANES), jnp.float32),
        scratch_shapes=[
            pltpu.VMEM((NDIR, ROWS // 8, TILES, 8, LANES), jnp.float32),
            pltpu.VMEM((32, NDIR, 8, LANES), jnp.float32),
            pltpu.VMEM((8, TILES, 8, LANES), jnp.float32),
            pltpu.VMEM((2, HALO, TILES, 24, LANES), jnp.float32),
            pltpu.SemaphoreType.DMA((NDIR // FETCH,)),
            pltpu.SemaphoreType.DMA((NDIR // FETCH,)),
        ],
        compiler_params=pltpu.CompilerParams(vmem_limit_bytes=13 * MIB),
        cost_estimate=pl.CostEstimate(flops=40_000_000, bytes_accessed=9_500_000, transcendentals=0),
        name="propagate",
    )(courant, jnp.asarray(trig), jnp.asarray(table), in_hbm(spectrum), mask, from_south, from_north)


def pick_kernel(grp_ref, cells_ref, p_ref, *out_refs):
    group = grp_ref[0]
    count = len(out_refs)
    lane = lax.broadcasted_iota(jnp.int32, (NDIR, LANES), 1)
    points = LANES // count
    for k, out in enumerate(out_refs):
        owner = lax.rem(group + k, count)
        nests = out.shape[0]

        def nest_body(n, carry):
            def point_body(p, acc):
                for u in range(8):
                    col = group * points + p * 8 + u
                    cell = lax.bitwise_and(cells_ref[owner * nests + n, col], ROWS * COLS - 1)
                    y = lax.shift_right_logical(cell, 9)
                    x = lax.bitwise_and(cell, COLS - 1)
                    row = lax.shift_right_logical(y, 1) * (NDIR * 8) + lax.shift_right_logical(x, 7) * 2 + lax.bitwise_and(y, 1)
                    got = p_ref[pl.ds(row, NDIR, stride=8), :]
                    turn = lax.bitwise_and(col - x, LANES - 1)
                    acc = jnp.where(lane == col, pltpu.roll(got, turn, 1), acc)
                return acc

            out[n] = lax.fori_loop(0, points // 8, point_body, jnp.zeros((NDIR, LANES), jnp.float32))
            return carry

        lax.fori_loop(0, nests, nest_body, 0)


def pick(group, cells, moved, count):
    nests = cells.shape[0] // count
    return pl.pallas_call(
        pick_kernel,
        in_specs=[
            pl.BlockSpec(memory_space=pltpu.SMEM),
            pl.BlockSpec(memory_space=pltpu.SMEM),
            pl.BlockSpec(memory_space=pltpu.VMEM),
        ],
        out_specs=[pl.BlockSpec(memory_space=pltpu.VMEM)] * count,
        out_shape=[jax.ShapeDtypeStruct((nests, NDIR, LANES), jnp.float32)] * count,
        compiler_params=pltpu.CompilerParams(vmem_limit_bytes=8 * MIB),
        cost_estimate=pl.CostEstimate(flops=10_000_000, bytes_accessed=6_000_000, transcendentals=0),
        name="pick",
    )(group, cells, moved.reshape(32 * NDIR * 8, LANES))


def merge_kernel(*refs):
    *ins, out = refs
    for n in range(ins[0].shape[0]):
        total = ins[0][n]
        for r in ins[1:]:
            total = total + r[n]
        out[:, n, :] = total


def merge(parts):
    nests = parts[0].shape[0]
    return pl.pallas_call(
        merge_kernel,
        out_shape=jax.ShapeDtypeStruct((NDIR, nests, LANES), jnp.float32),
        compiler_params=pltpu.CompilerParams(vmem_limit_bytes=4 * MIB),
        name="merge",
    )(*parts)


FCHUNK = 4
NCHUNK = NFREQ // FCHUNK


def source_kernel(recv_ref, u_ref, v_ref, out_ref, buf, outbuf, sem, osem):
    put = lambda c: pltpu.make_async_copy(
        outbuf.at[pl.ds(c * FCHUNK, FCHUNK)], out_ref.at[pl.ds(c * FCHUNK, FCHUNK)], osem.at[c]
    )
    fetch = lambda c: pltpu.make_async_copy(recv_ref.at[pl.ds(c * FCHUNK, FCHUNK)], buf.at[pl.ds(c * FCHUNK, FCHUNK)], sem.at[c])
    for c in range(NCHUNK):
        fetch(c).start()
    total = jnp.zeros((8, LANES), jnp.float32)
    weighted = jnp.zeros((8, LANES), jnp.float32)
    for f in range(NFREQ):
        if f % FCHUNK == 0:
            fetch(f // FCHUNK).wait()
        s = jnp.sum(buf[f], axis=0)
        total = total + s
        weighted = weighted + s * float(SCALE[f] * SCALE[f])
    m0 = total * (1.0 / (NFREQ * NDIR))
    q = weighted * (1.0 / (NFREQ * NDIR))
    ratio = jnp.maximum(m0, 0.05) / jnp.maximum(q, 0.1)
    steep = m0 / 0.3
    base = ratio * (steep * steep)
    u = u_ref[...]
    v = v_ref[...]

    for c in range(NCHUNK):
        fs = range(c * FCHUNK, (c + 1) * FCHUNK)
        loss = [base * float(0.1 * SCALE[f] ** 3 * LOG2E) for f in fs]
        for d in range(NDIR):
            proj = u * float(COS[d]) + v * float(SIN[d])
            for i, f in enumerate(fs):
                gain = jnp.maximum(proj * float(0.05 * SCALE[f] ** 2 * LOG2E) - float(0.05 * SCALE[f] * LOG2E), 0.0)
                outbuf[f, d] = buf[f, d] * jnp.exp2(gain - loss[i])
        put(c).start()
    for c in range(NCHUNK):
        put(c).wait()


def sources(recv, wind_u, wind_v):
    tile = lambda w: w.reshape(2, TILES, LANES).transpose(1, 0, 2).reshape(8, LANES)
    shape = (NFREQ, NDIR, 8, LANES)
    out = pl.pallas_call(
        source_kernel,
        in_specs=[pl.BlockSpec(memory_space=pl.ANY)] + [pl.BlockSpec(memory_space=pltpu.VMEM)] * 2,
        out_specs=pl.BlockSpec(memory_space=pltpu.HBM),
        out_shape=jax.ShapeDtypeStruct(shape, jnp.float32),
        scratch_shapes=[
            pltpu.VMEM(shape, jnp.float32),
            pltpu.VMEM(shape, jnp.float32),
            pltpu.SemaphoreType.DMA((NCHUNK,)),
            pltpu.SemaphoreType.DMA((NCHUNK,)),
        ],
        compiler_params=pltpu.CompilerParams(vmem_limit_bytes=12 * MIB),
        name="sources",
    )(in_hbm(recv), tile(wind_u), tile(wind_v))
    out = out.reshape(NFREQ, NDIR, TILES, 2, LANES).transpose(0, 1, 3, 2, 4)
    return out.reshape(NFREQ, NDIR, 1, 2, COLS)


def per_device(spectrum, courant, sea_mask, wind_u, wind_v, boundary_cells):
    size = lax.axis_size("grp")
    group = lax.axis_index("grp").astype(jnp.int32).reshape(1)
    block = tiled(spectrum.reshape(NDIR, ROWS, COLS))
    mask = tiled(sea_mask.reshape(ROWS, COLS))
    up, down = pack(block, mask)
    from_south = lax.ppermute(up, "grp", [(i, i + 1) for i in range(size - 1)])
    from_north = lax.ppermute(down, "grp", [(i + 1, i) for i in range(size - 1)])
    result = propagate(block, courant, mask, from_south, from_north)
    moved = lax.all_to_all(result, "comp", split_axis=0, concat_axis=0, tiled=True)
    picked = pick(group, boundary_cells, result, size)
    parts = [picked[0]]
    for k in range(1, size):
        parts.append(lax.ppermute(picked[k], "grp", [(i, (i + k) % size) for i in range(size)]))
    boundary = merge(parts)[None]
    updated = sources(moved, wind_u.reshape(2, COLS), wind_v.reshape(2, COLS))
    return updated, boundary


def solution(mesh):
    placed = (
        P("comp", None, "grp", None, None),
        P("comp"),
        P("grp", None, None),
        P("grp", "comp", None),
        P("grp", "comp", None),
        P(),
    )
    return jax.shard_map(
        per_device,
        mesh=mesh,
        in_specs=placed,
        out_specs=(P(None, None, "grp", "comp", None), P("comp", None, "grp", None)),
        check_vma=False,
    )
```

time: 116 us -> 96.3 us (0.83)
  Pallas kernels: 58.5 us -> 35.4 us
  waiting for transfers between devices: 34.8 us -> 38.4 us
    pallas_call x2, Pallas kernels: 27 us -> 9.37 us  [the longest x1 8.31 us: propagate(): pl.pallas_call(propagate_kernel, in_specs=[smem, smem, vmem, pl.BlockSpec...]
    all_to_all x1, waiting for transfers between devices: 20.4 us -> 24.5 us  [per_device(): lax.all_to_all(result, 'comp', split_axis=0, concat_axis=0, tiled=True)]
    pallas_call x1, Pallas kernels: 23.9 us -> 21.1 us  [pick(): pl.pallas_call(pick_kernel, in_specs=[pl.BlockSpec(memory_space=pltpu.SME...]
    pallas_call x1, Pallas kernels: 2.09 us -> 0.13 us  [merge(): pl.pallas_call(merge_kernel, out_shape=jax.ShapeDtypeStruct((NDIR, nests,...]
    unnamed x11 -> x15, local copies, waits for them, and re-layouts: 3.16 us -> 3.26 us
  transfers between devices with their start and end apart: 6 -> 6, of which waited for: 6 -> 6; matrix products, arithmetic and copies ran while one was open for 2% -> 1% of each run, Pallas kernels for 23% -> 22%
where the time goes in v3:
time: 96.3 us; the launch traced here: 96 us
  waiting for transfers between devices  38.4 us (40%)
  Pallas kernels  35.4 us (37%)
  starting transfers between devices  17.5 us (18%)
  local copies, waits for them, and re-layouts  3.26 us (3%)
  between operations  1.41 us (1%)
    all_to_all x1, waiting for transfers between devices, per_device(): lax.all_to_all(result, 'comp', split_axis=0, concat_axis=0, tiled=True)  24.5 us
    pallas_call x1, Pallas kernels, pick(): pl.pallas_call(pick_kernel, in_specs=[pl.BlockSpec(memory_space=pltpu.SME...  21.1 us
    ppermute x3, waiting for transfers between devices, per_device(): lax.ppermute(picked[k], 'grp', [(i, (i + k) % size) for i in range(size)])  10.2 us
    pallas_call x1, Pallas kernels, propagate(): pl.pallas_call(propagate_kernel, in_specs=[smem, smem, vmem, pl.BlockSpec...  8.31 us
    all_to_all x1, starting transfers between devices, per_device(): lax.all_to_all(result, 'comp', split_axis=0, concat_axis=0, tiled=True)  8.27 us
    pallas_call x1, Pallas kernels, sources(): pl.pallas_call(source_kernel, in_specs=[pl.BlockSpec(memory_space=pl.ANY)...  4.81 us
    ppermute x3, starting transfers between devices, per_device(): lax.ppermute(picked[k], 'grp', [(i, (i + k) % size) for i in range(size)])  3.43 us
    ppermute x1, starting transfers between devices, per_device(): from_south = lax.ppermute(up, 'grp', [(i, i + 1) for i in range(size - 1)])  3.4 us
  transfers between devices with their start and end apart: 6, of which 6 were waited for; matrix products, arithmetic and copies ran while one was open for 1% of the time, Pallas kernels for 22%

profile of v3, /device:TPU:34, one launch (start us, length us, event | category | flops | bytes accessed | tf_op | source)
XLA Modules:
  0.0 96.0 jit_solution(12625146895798267588)
XLA Ops:
  0.6 0.0 copy-start.6
  0.6 0.0 copy-start.2
  0.7 0.0 copy-start.1
  0.7 1.1 %pack.1 = (f32[20,4,3,1,128]{4,3,2,1,0:T(1,128)S(1)}, f32[20,4,3,1,128]{4,3,2,1,0:T(1,128)S(1)}) custom-call(f32[36,8,4,8,1,128]{5,4,3,2,1,0:T(1,128)} %bitcast.42, s32[8,4,8,1,128]{4,3,2,1,0:T(1,128)} %bitcast.36), custom_call_target="tpu_custom_call" | custom-call | tf_op jit(solution)/shard_map/pack/pallas_call | solution.py:64
  1.7 3.4 %collective-permute-start = (f32[240,128]{1,0:T(8,128)S(1)}, f32[240,128]{1,0:T(8,128)S(1)}, u32[]{:S(2)}, u32[]{:S(2)}) collective-permute-start(f32[240,128]{1,0:T(8,128)S(1)} %bitcast.41), channel_id=1, source_target_pairs={{0,1},{1,2},{2,3},{4,5},{5,6},{6,7},{8,9},{9,10},{10,11},{12,13},{... | collective-permute-start | bytes 368648 | tf_op jit(solution)/shard_map/ppermute | solution.py:329
  5.1 2.4 %collective-permute-start.1 = (f32[240,128]{1,0:T(8,128)S(1)}, f32[240,128]{1,0:T(8,128)S(1)}, u32[]{:S(2)}, u32[]{:S(2)}) collective-permute-start(f32[240,128]{1,0:T(8,128)S(1)} %bitcast.40), channel_id=1, source_target_pairs={{1,0},{2,1},{3,2},{5,4},{6,5},{7,6},{9,8},{10,9},{11,10},{13,12},{... | collective-permute-start | bytes 368648 | tf_op jit(solution)/shard_map/ppermute | solution.py:330
  8.2 0.4 collective-permute-done.south_ref
  8.7 3.2 %collective-permute-done.1.north_ref = f32[240,128]{1,0:T(8,128)S(1)} collective-permute-done((f32[240,128]{1,0:T(8,128)S(1)}, f32[240,128]{1,0:T(8,128)S(1)}, u32[]{:S(2)}, u32[]{:S(2)}) %collective-permute-start.1) | collective-permute-done | bytes 122912 | tf_op jit(solution)/shard_map/ppermute | solution.py:330
  11.9 0.0 copy-done.6
  11.9 0.0 copy-done.2
  11.9 0.0 copy-done.1
  11.9 8.3 %propagate.1 = f32[32,36,8,128]{3,2,1,0:T(8,128)} custom-call(f32[1]{0:T(128)S(6)} %copy.16.courant_ref, f32[2,36]{1,0:T(2,128)S(1)} %copy-done.6, f32[4,24,128]{2,1,0:T(8,128)S(1)} %copy-done.2, f32[36,8,4,8,128]{4,3,2,1,0:T(8,128)} %bitcast.43, s32[8,4,8,128]{3,2,1,0:T(8,128)S(1)} %bitcast.37, f32[240,128]{1,0:T(8,128)S(1)} %collective-permute-done.south_ref, ...), custom_call_target="tpu_custom_call" | custom-call | flops 40000000 | bytes 9500000 | tf_op jit(solution)/shard_map/propagate/pallas_call | solution.py:179
  20.2 0.0 copy-start.3
  20.3 8.3 %all-to-all-start = ((f32[32,36,8,128]{3,2,1,0:T(8,128)}), f32[32,36,8,128]{3,2,1,0:T(8,128)}, u32[]{:S(2)}, u32[]{:S(2)}) async-start(f32[32,36,8,128]{3,2,1,0:T(8,128)} %propagate.1), calls=%async_computation | async-start | bytes 9437184 | tf_op jit(solution)/shard_map/all_to_all | solution.py:332
  28.5 0.0 copy-start.4
  28.5 0.0 copy-start.5
  28.6 0.0 copy-done.3
  28.6 0.0 copy-start
  28.6 2.4 %copy-done = f32[32,36,8,128]{3,2,1,0:T(8,128)S(1)} copy-done((f32[32,36,8,128]{3,2,1,0:T(8,128)S(1)}, f32[32,36,8,128]{3,2,1,0:T(8,128)}, u32[]{:S(2)}) %copy-start) | copy-done | bytes 4718616
  30.9 21.1 %pick.1 = (f32[10,36,128]{2,1,0:T(8,128)S(1)}, f32[10,36,128]{2,1,0:T(8,128)S(1)}, f32[10,36,128]{2,1,0:T(8,128)S(1)}, f32[10,36,128]{2,1,0:T(8,128)S(1)}) custom-call(s32[1]{0:T(128)} %bitcast.21.grp_ref, s32[40,128]{1,0:T(8,128)S(1)} %copy-done.3, f32[9216,128]{1,0:T(8,128)S(1)} %bitcast.34), custom_call_target="tpu_custom_call" | custom-call | flops 10000000 | bytes 6000000 | tf_op jit(solution)/shard_map/pick/pallas_call | solution.py:228
  52.1 1.3 %collective-permute-start.2 = (f32[10,36,128]{2,1,0:T(8,128)S(1)}, f32[10,36,128]{2,1,0:T(8,128)S(1)}, u32[]{:S(2)}, u32[]{:S(2)}) collective-permute-start(f32[10,36,128]{2,1,0:T(8,128)S(1)} %get-tuple-element.11), channel_id=1, source_target_pairs={{0,1},{1,2},{2,3},{3,0},{4,5},{5,6},{6,7},{7,4},{8,9},{9,10},{10,1... | collective-permute-start | bytes 552968 | tf_op jit(solution)/shard_map/ppermute | solution.py:336
  53.3 1.4 %collective-permute-start.3 = (f32[10,36,128]{2,1,0:T(8,128)S(1)}, f32[10,36,128]{2,1,0:T(8,128)S(1)}, u32[]{:S(2)}, u32[]{:S(2)}) collective-permute-start(f32[10,36,128]{2,1,0:T(8,128)S(1)} %get-tuple-element.12), channel_id=1, source_target_pairs={{0,2},{1,3},{2,0},{3,1},{4,6},{5,7},{6,4},{7,5},{8,10},{9,11},{10,... | collective-permute-start | bytes 552968 | tf_op jit(solution)/shard_map/ppermute | solution.py:336
  54.7 0.8 collective-permute-start.4
  55.5 4.6 %collective-permute-done.2.refs_1_ = f32[10,36,128]{2,1,0:T(8,128)S(1)} collective-permute-done((f32[10,36,128]{2,1,0:T(8,128)S(1)}, f32[10,36,128]{2,1,0:T(8,128)S(1)}, u32[]{:S(2)}, u32[]{:S(2)}) %collective-permute-start.2) | collective-permute-done | bytes 184352 | tf_op jit(solution)/shard_map/ppermute | solution.py:336
  60.1 2.7 %collective-permute-done.3.refs_2_ = f32[10,36,128]{2,1,0:T(8,128)S(1)} collective-permute-done((f32[10,36,128]{2,1,0:T(8,128)S(1)}, f32[10,36,128]{2,1,0:T(8,128)S(1)}, u32[]{:S(2)}, u32[]{:S(2)}) %collective-permute-start.3) | collective-permute-done | bytes 184352 | tf_op jit(solution)/shard_map/ppermute | solution.py:336
  62.8 2.9 %collective-permute-done.4.refs_3_ = f32[10,36,128]{2,1,0:T(8,128)S(1)} collective-permute-done((f32[10,36,128]{2,1,0:T(8,128)S(1)}, f32[10,36,128]{2,1,0:T(8,128)S(1)}, u32[]{:S(2)}, u32[]{:S(2)}) %collective-permute-start.4) | collective-permute-done | bytes 184352 | tf_op jit(solution)/shard_map/ppermute | solution.py:336
  65.7 0.1 merge.1
  65.8 0.9 copy.15
  66.7 24.5 %all-to-all-done.recv_ref = f32[32,36,8,128]{3,2,1,0:T(8,128)} async-done(((f32[32,36,8,128]{3,2,1,0:T(8,128)}), f32[32,36,8,128]{3,2,1,0:T(8,128)}, u32[]{:S(2)}, u32[]{:S(2)}) %all-to-all-start) | async-done | bytes 4718624 | tf_op jit(solution)/shard_map/all_to_all | solution.py:332
  91.2 0.0 copy-done.4
  91.2 0.0 copy-done.5
  91.2 4.8 %sources.1 = f32[32,36,8,128]{3,2,1,0:T(8,128)} custom-call(f32[32,36,8,128]{3,2,1,0:T(8,128)} %all-to-all-done.recv_ref, f32[8,128]{1,0:T(8,128)S(1)} %bitcast.38, f32[8,128]{1,0:T(8,128)S(1)} %bitcast.39), custom_call_target="tpu_custom_call" | custom-call | tf_op jit(solution)/shard_map/sources/pallas_call | solution.py:305
Async XLA Ops:
  0.6 11.3 %copy-start.6 = (f32[2,36]{1,0:T(2,128)S(1)}, f32[2,36]{1,0:T(2,128)}, u32[]{:S(2)}) copy-start(f32[2,36]{1,0:T(2,128)} %constant.8.clone.trig_ref) | copy-start | bytes 868
  0.6 11.3 %copy-start.2 = (f32[4,24,128]{2,1,0:T(8,128)S(1)}, f32[4,24,128]{2,1,0:T(8,128)}, u32[]{:S(2)}) copy-start(f32[4,24,128]{2,1,0:T(8,128)} %constant.9.clone.table_ref) | copy-start | bytes 147460
  0.7 11.3 %copy-start.1 = (s32[1,64,512]{2,1,0:T(8,128)S(1)}, s32[1,64,512]{2,1,0:T(8,128)}, u32[]{:S(2)}) copy-start(s32[1,64,512]{2,1,0:T(8,128)} %param.10) | copy-start | bytes 393220
  1.7 7.0 %collective-permute-start = (f32[240,128]{1,0:T(8,128)S(1)}, f32[240,128]{1,0:T(8,128)S(1)}, u32[]{:S(2)}, u32[]{:S(2)}) collective-permute-start(f32[240,128]{1,0:T(8,128)S(1)} %bitcast.41), channel_id=1, source_target_pairs={{0,1},{1,2},{2,3},{4,5},{5,6},{6,7},{8,9},{9,10},{10,11},{12,13},{... | collective-permute-start | bytes 368648 | tf_op jit(solution)/shard_map/ppermute | solution.py:329
  5.1 6.8 %collective-permute-start.1 = (f32[240,128]{1,0:T(8,128)S(1)}, f32[240,128]{1,0:T(8,128)S(1)}, u32[]{:S(2)}, u32[]{:S(2)}) collective-permute-start(f32[240,128]{1,0:T(8,128)S(1)} %bitcast.40), channel_id=1, source_target_pairs={{1,0},{2,1},{3,2},{5,4},{6,5},{7,6},{9,8},{10,9},{11,10},{13,12},{... | collective-permute-start | bytes 368648 | tf_op jit(solution)/shard_map/ppermute | solution.py:330
  20.2 8.3 %copy-start.3 = (s32[40,128]{1,0:T(8,128)S(1)}, s32[40,128]{1,0:T(8,128)}, u32[]{:S(2)}) copy-start(s32[40,128]{1,0:T(8,128)} %cells_ref.1) | copy-start | bytes 61444
  20.3 71.0 %all-to-all-start = ((f32[32,36,8,128]{3,2,1,0:T(8,128)}), f32[32,36,8,128]{3,2,1,0:T(8,128)}, u32[]{:S(2)}, u32[]{:S(2)}) async-start(f32[32,36,8,128]{3,2,1,0:T(8,128)} %propagate.1), calls=%async_computation | async-start | bytes 9437184 | tf_op jit(solution)/shard_map/all_to_all | solution.py:332
  28.5 62.7 %copy-start.4 = (f32[1,2,512]{2,1,0:T(2,128)S(1)}, f32[1,2,512]{2,1,0:T(2,128)}, u32[]{:S(2)}) copy-start(f32[1,2,512]{2,1,0:T(2,128)} %param.11) | copy-start | bytes 12292
  28.5 62.7 %copy-start.5 = (f32[1,2,512]{2,1,0:T(2,128)S(1)}, f32[1,2,512]{2,1,0:T(2,128)}, u32[]{:S(2)}) copy-start(f32[1,2,512]{2,1,0:T(2,128)} %param.12) | copy-start | bytes 12292
  28.6 2.4 %copy-start = (f32[32,36,8,128]{3,2,1,0:T(8,128)S(1)}, f32[32,36,8,128]{3,2,1,0:T(8,128)}, u32[]{:S(2)}) copy-start(f32[32,36,8,128]{3,2,1,0:T(8,128)} %propagate.1) | copy-start | bytes 14155780
  52.1 8.0 %collective-permute-start.2 = (f32[10,36,128]{2,1,0:T(8,128)S(1)}, f32[10,36,128]{2,1,0:T(8,128)S(1)}, u32[]{:S(2)}, u32[]{:S(2)}) collective-permute-start(f32[10,36,128]{2,1,0:T(8,128)S(1)} %get-tuple-element.11), channel_id=1, source_target_pairs={{0,1},{1,2},{2,3},{3,0},{4,5},{5,6},{6,7},{7,4},{8,9},{9,10},{10,1... | collective-permute-start | bytes 552968 | tf_op jit(solution)/shard_map/ppermute | solution.py:336
  53.3 9.5 %collective-permute-start.3 = (f32[10,36,128]{2,1,0:T(8,128)S(1)}, f32[10,36,128]{2,1,0:T(8,128)S(1)}, u32[]{:S(2)}, u32[]{:S(2)}) collective-permute-start(f32[10,36,128]{2,1,0:T(8,128)S(1)} %get-tuple-element.12), channel_id=1, source_target_pairs={{0,2},{1,3},{2,0},{3,1},{4,6},{5,7},{6,4},{7,5},{8,10},{9,11},{10,... | collective-permute-start | bytes 552968 | tf_op jit(solution)/shard_map/ppermute | solution.py:336
  54.7 11.0 %collective-permute-start.4 = (f32[10,36,128]{2,1,0:T(8,128)S(1)}, f32[10,36,128]{2,1,0:T(8,128)S(1)}, u32[]{:S(2)}, u32[]{:S(2)}) collective-permute-start(f32[10,36,128]{2,1,0:T(8,128)S(1)} %get-tuple-element.13), channel_id=1, source_target_pairs={{0,3},{1,0},{2,1},{3,2},{4,7},{5,4},{6,5},{7,6},{8,11},{9,8},{10,9... | collective-permute-start | bytes 552968 | tf_op jit(solution)/shard_map/ppermute | solution.py:336

commit v4 on v3

--- a/solution.py
+++ b/solution.py
@@ -28,6 +28,9 @@
 SIN = np.sin(THETA).astype(np.float32)
 SCALE = (0.3 * np.float32(1.1) ** np.arange(NFREQ, dtype=np.float32)).astype(np.float32)
 LOG2E = 1.4426950408889634
+
+ORDER = (15, 27, 28, 26, 22, 18, 24, 3, 9, 25, 6, 13, 7, 31, 20, 12, 1, 17, 23, 2, 30, 14, 16, 10, 0, 21, 5, 4, 8, 11, 19, 29)
+PLACE = tuple(int(p) for p in np.argsort(ORDER))
 
 
 def tiled(value):
@@ -74,74 +77,47 @@
 
 
 FETCH = 3
-INTER = FETCH
-
-
-def propagate_kernel(
-    courant_ref, trig_ref, table_ref, e_ref, mask_ref, south_ref, north_ref, out_ref, e_buf, out_buf, mask_s, edge_s, sem, out_sem
-):
+CHUNKS = NDIR // FETCH
+
+
+def shifted(row, west):
+    lane = lax.broadcasted_iota(jnp.int32, (8, LANES), 1)
+    r = [pltpu.roll(v, 1 if west else LANES - 1, 1) for v in row]
+    if west:
+        return [jnp.where(lane == 0, r[j - 1], r[j]) for j in range(TILES)]
+    return [jnp.where(lane == LANES - 1, r[(j + 1) % TILES], r[j]) for j in range(TILES)]
+
+
+def interior_kernel(courant_ref, trig_ref, e_ref, mask_ref, out_ref, tile_ref, e_buf, out_buf, mask_s, sem, out_sem):
     fetch = lambda c: pltpu.make_async_copy(e_ref.at[pl.ds(c * FETCH, FETCH)], e_buf.at[pl.ds(c * FETCH, FETCH)], sem.at[c])
     put = lambda c: pltpu.make_async_copy(out_buf.at[:, pl.ds(c * FETCH, FETCH)], out_ref.at[:, pl.ds(c * FETCH, FETCH)], out_sem.at[c])
-    for c in range(NDIR // FETCH):
+    for c in range(CHUNKS):
         fetch(c).start()
-    lane = lax.broadcasted_iota(jnp.int32, (8, LANES), 1)
     sub = lax.broadcasted_iota(jnp.int32, (8, LANES), 0)
-
-    def shifted(row, west):
-        r = [pltpu.roll(v, 1 if west else LANES - 1, 1) for v in row]
-        if west:
-            return [jnp.where(lane == 0, r[j - 1], r[j]) for j in range(TILES)]
-        return [jnp.where(lane == LANES - 1, r[(j + 1) % TILES], r[j]) for j in range(TILES)]
-
     mask_s[...] = mask_ref[...].astype(jnp.float32)
 
-    for side, halo in enumerate((south_ref, north_ref)):
-        south = side == 0
-        near = lambda p: HALO - 1 - p if south else p
-        m = [[halo[HALF * SLOT + j * HALO + near(p) : HALF * SLOT + j * HALO + near(p) + 1, :] for j in range(TILES)] for p in range(2)]
-        for g, n in ((0, 8), (8, 8), (16, 2)):
-            a = courant_ref[0] * table_ref[2 * side, g : g + 8, :]
-            b = courant_ref[0] * table_ref[2 * side + 1, g : g + 8, :]
-            c = 1.0 - a - b
-            turned = sub + g >= QUART
-            rows = []
-            for p in range(HALO):
-                row = []
-                for j in range(TILES):
-                    v = halo[pl.ds(g * SLOT + j * HALO + near(p), n, stride=SLOT), :]
-                    row.append(v if n == 8 else jnp.concatenate([v, jnp.zeros((8 - n, LANES), jnp.float32)], axis=0))
-                rows.append(row)
-            for k in range(HALO):
-                for j in range(TILES):
-                    edge_s[side, k, j, g : g + 8, :] = rows[0][j]
-                new = []
-                for p in range(len(rows) - 1):
-                    w, e = shifted(rows[p], True), shifted(rows[p], False)
-                    x = [jnp.where(turned, e[j], w[j]) if south else jnp.where(turned, w[j], e[j]) for j in range(TILES)]
-                    new.append([m[p][j] * (c * rows[p][j] + a * x[j] + b * rows[p + 1][j]) for j in range(TILES)])
-                rows = new
-
     def advance(south, west, first, i, carry):
-        ds = [first + i * INTER + u for u in range(INTER)]
-        many = range(INTER)
-        side = 0 if south else 1
+        ds = [first + i * FETCH + u for u in range(FETCH)]
+        many = range(FETCH)
         at, turn = (0, 1) if south else (7, 7)
         fetch(first // FETCH + i).wait()
         a = [courant_ref[0] * trig_ref[0, d] for d in ds]
         b = [courant_ref[0] * trig_ref[1, d] for d in ds]
         c = [1.0 - x - y for x, y in zip(a, b)]
         e = [[[e_buf[d, t, j] for j in range(TILES)] for t in range(8)] for d in ds]
+        for u in many:
+            for j in range(TILES):
+                tile_ref[0 if south else 1, ds[u] - (0 if south else HALF), j] = e[u][at][j]
         for stage in range(SUBSTEPS):
             new = [[None] * 8 for _ in many]
             moved = [[[pltpu.roll(v, turn, 0) for v in row] for row in e[u]] for u in many]
             for t in range(8):
                 for u in many:
-                    if t == at:
-                        beyond = [edge_s[side, stage, j, pl.ds(ds[u] - side * HALF, 1), :] for j in range(TILES)]
-                    else:
+                    x = shifted(e[u][t], west)
+                    y = moved[u][t]
+                    if t != at:
                         beyond = moved[u][t - 1 if south else t + 1]
-                    x = shifted(e[u][t], west)
-                    y = [jnp.where(sub == at, beyond[j], moved[u][t][j]) for j in range(TILES)]
+                        y = [jnp.where(sub == at, beyond[j], y[j]) for j in range(TILES)]
                     new[u][t] = [mask_s[t, j] * (c[u] * e[u][t][j] + a[u] * x[j] + b[u] * y[j]) for j in range(TILES)]
             e = new
         odd, high = sub & 2 != 0, sub >= 4
@@ -154,48 +130,136 @@
                     jnp.where(odd, pltpu.roll(v[3], 2, 0), v[2]),
                     jnp.where(odd, v[3], pltpu.roll(v[2], 6, 0)),
                 ]
-                out_buf[4 * t, ds[u]] = jnp.where(high, pltpu.roll(w[2], 4, 0), w[0])
-                out_buf[4 * t + 1, ds[u]] = jnp.where(high, pltpu.roll(w[3], 4, 0), w[1])
-                out_buf[4 * t + 2, ds[u]] = jnp.where(high, w[2], pltpu.roll(w[0], 4, 0))
-                out_buf[4 * t + 3, ds[u]] = jnp.where(high, w[3], pltpu.roll(w[1], 4, 0))
+                out_buf[PLACE[4 * t], ds[u]] = jnp.where(high, pltpu.roll(w[2], 4, 0), w[0])
+                out_buf[PLACE[4 * t + 1], ds[u]] = jnp.where(high, pltpu.roll(w[3], 4, 0), w[1])
+                out_buf[PLACE[4 * t + 2], ds[u]] = jnp.where(high, w[2], pltpu.roll(w[0], 4, 0))
+                out_buf[PLACE[4 * t + 3], ds[u]] = jnp.where(high, w[3], pltpu.roll(w[1], 4, 0))
         put(first // FETCH + i).start()
         return carry
 
     for q, (south, west) in enumerate(((True, True), (True, False), (False, False), (False, True))):
-        lax.fori_loop(0, QUART // INTER, functools.partial(advance, south, west, q * QUART), 0)
-    for c in range(NDIR // FETCH):
+        lax.fori_loop(0, QUART // FETCH, functools.partial(advance, south, west, q * QUART), 0)
+    for c in range(CHUNKS):
         put(c).wait()
 
 
-def propagate(spectrum, courant, mask, from_south, from_north):
+def interior(spectrum, courant, mask):
     trig = np.stack([np.abs(COS), np.abs(SIN)])
+    smem = pl.BlockSpec(memory_space=pltpu.SMEM)
+    vmem = pl.BlockSpec(memory_space=pltpu.VMEM)
+    hbm = pl.BlockSpec(memory_space=pl.ANY)
+    return pl.pallas_call(
+        interior_kernel,
+        in_specs=[smem, smem, hbm, vmem],
+        out_specs=[hbm, vmem],
+        out_shape=[
+            pltpu.HBM((32, NDIR, 8, LANES), jnp.float32),
+            jax.ShapeDtypeStruct((2, HALF, TILES, 8, LANES), jnp.float32),
+        ],
+        scratch_shapes=[
+            pltpu.VMEM((NDIR, ROWS // 8, TILES, 8, LANES), jnp.float32),
+            pltpu.VMEM((32, NDIR, 8, LANES), jnp.float32),
+            pltpu.VMEM((8, TILES, 8, LANES), jnp.float32),
+            pltpu.SemaphoreType.DMA((CHUNKS,)),
+            pltpu.SemaphoreType.DMA((CHUNKS,)),
+        ],
+        compiler_params=pltpu.CompilerParams(vmem_limit_bytes=12 * MIB),
+        cost_estimate=pl.CostEstimate(flops=40_000_000, bytes_accessed=9_500_000, transcendentals=0),
+        name="interior",
+    )(courant, jnp.asarray(trig), in_hbm(spectrum), mask)
+
+
+EDGE = 4
+
+
+def edges_kernel(courant_ref, table_ref, tile_ref, mask_ref, south_ref, north_ref, p_in, p_ref, fixed, sem):
+    del p_in
+    sub = lax.broadcasted_iota(jnp.int32, (8, LANES), 0)
+    flat_mask = mask_ref.reshape(ROWS * TILES, LANES)
+    total = HALO + EDGE
+    puts = []
+
+    def eight(ref, start, n, stride):
+        v = ref[pl.ds(start, n, stride=stride), :]
+        return v if n == 8 else jnp.concatenate([v, jnp.zeros((8 - n, LANES), jnp.float32)], axis=0)
+
+    for side, halo in enumerate((south_ref, north_ref)):
+        south = side == 0
+        tiles = tile_ref.at[side].reshape(HALF * ROWBLOCK, LANES)
+        rows_out = fixed.at[side].reshape(2 * HALF * 8, LANES)
+        own = lambda p: p - HALO if south else 7 - (p - HALO)
+        sent = lambda p: p if south else HALO - 1 - p
+        base = 0 if south else (ROWS // 8 - 1) * ROWBLOCK
+        m = [None]
+        for p in range(1, total):
+            row = []
+            for j in range(TILES):
+                if p < HALO:
+                    at = HALF * SLOT + j * HALO + sent(p)
+                    row.append(halo[at : at + 1, :])
+                else:
+                    at = base + j * 8 + own(p)
+                    row.append(flat_mask[at : at + 1, :].astype(jnp.float32))
+            m.append(row)
+        for g, n in ((0, 8), (8, 8), (16, 2)):
+            a = courant_ref[0] * table_ref[2 * side, g : g + 8, :]
+            b = courant_ref[0] * table_ref[2 * side + 1, g : g + 8, :]
+            c = 1.0 - a - b
+            e = []
+            for p in range(total):
+                if p < HALO:
+                    e.append([eight(halo, g * SLOT + j * HALO + sent(p), n, SLOT) for j in range(TILES)])
+                else:
+                    e.append([eight(tiles, g * ROWBLOCK + j * 8 + own(p), n, ROWBLOCK) for j in range(TILES)])
+            for k in range(SUBSTEPS):
+                new = [None] * total
+                for p in range(k + 1, total):
+                    first = shifted(e[p], south) if g < 16 else None
+                    second = shifted(e[p], not south) if g > 0 else None
+                    if g == 0:
+                        x = first
+                    elif g == 16:
+                        x = second
+                    else:
+                        x = [jnp.where(sub == 0, f, s) for f, s in zip(first, second)]
+                    new[p] = [m[p][j] * (c * e[p][j] + a * x[j] + b * e[p - 1][j]) for j in range(TILES)]
+                e = new
+            for p in range(HALO, total):
+                y = p - HALO if south else EDGE - 1 - (p - HALO)
+                for j in range(TILES):
+                    rows_out[pl.ds(((y // 2) * HALF + g) * 8 + 2 * j + y % 2, n, stride=8), :] = e[p][j][:n]
+        for i in range(2):
+            place = PLACE[i if south else 30 + i]
+            put = pltpu.make_async_copy(
+                fixed.at[side, i], p_ref.at[place, pl.ds(side * HALF, HALF)], sem.at[2 * side + i]
+            )
+            put.start()
+            puts.append(put)
+    for put in puts:
+        put.wait()
+
+
+def edges(tiles, courant, mask, from_south, from_north, inner):
     table = np.zeros((4, 24, LANES), np.float32)
     for side in range(2):
         ds = slice(side * HALF, (side + 1) * HALF)
         table[2 * side, :HALF] = np.abs(COS[ds])[:, None]
         table[2 * side + 1, :HALF] = np.abs(SIN[ds])[:, None]
-    smem = pl.BlockSpec(memory_space=pltpu.SMEM)
     vmem = pl.BlockSpec(memory_space=pltpu.VMEM)
+    hbm = pl.BlockSpec(memory_space=pl.ANY)
     return pl.pallas_call(
-        propagate_kernel,
-        in_specs=[smem, smem, vmem, pl.BlockSpec(memory_space=pl.ANY), vmem, vmem, vmem],
-        out_specs=pl.BlockSpec(memory_space=pl.ANY),
-        out_shape=pltpu.HBM((32, NDIR, 8, LANES), jnp.float32),
-        scratch_shapes=[
-            pltpu.VMEM((NDIR, ROWS // 8, TILES, 8, LANES), jnp.float32),
-            pltpu.VMEM((32, NDIR, 8, LANES), jnp.float32),
-            pltpu.VMEM((8, TILES, 8, LANES), jnp.float32),
-            pltpu.VMEM((2, HALO, TILES, 24, LANES), jnp.float32),
-            pltpu.SemaphoreType.DMA((NDIR // FETCH,)),
-            pltpu.SemaphoreType.DMA((NDIR // FETCH,)),
-        ],
-        compiler_params=pltpu.CompilerParams(vmem_limit_bytes=13 * MIB),
-        cost_estimate=pl.CostEstimate(flops=40_000_000, bytes_accessed=9_500_000, transcendentals=0),
-        name="propagate",
-    )(courant, jnp.asarray(trig), jnp.asarray(table), in_hbm(spectrum), mask, from_south, from_north)
-
-
-def pick_kernel(grp_ref, cells_ref, p_ref, *out_refs):
+        edges_kernel,
+        in_specs=[pl.BlockSpec(memory_space=pltpu.SMEM), vmem, vmem, vmem, vmem, vmem, hbm],
+        out_specs=hbm,
+        out_shape=pltpu.HBM(inner.shape, inner.dtype),
+        scratch_shapes=[pltpu.VMEM((2, 2, HALF, 8, LANES), jnp.float32), pltpu.SemaphoreType.DMA((4,))],
+        input_output_aliases={6: 0},
+        compiler_params=pltpu.CompilerParams(vmem_limit_bytes=4 * MIB),
+        name="edges",
+    )(courant, jnp.asarray(table), tiles, mask, from_south, from_north, in_hbm(inner))
+
+
+def pick_kernel(grp_ref, cells_ref, place_ref, p_ref, *out_refs):
     group = grp_ref[0]
     count = len(out_refs)
     lane = lax.broadcasted_iota(jnp.int32, (NDIR, LANES), 1)
@@ -211,7 +275,7 @@
                     cell = lax.bitwise_and(cells_ref[owner * nests + n, col], ROWS * COLS - 1)
                     y = lax.shift_right_logical(cell, 9)
                     x = lax.bitwise_and(cell, COLS - 1)
-                    row = lax.shift_right_logical(y, 1) * (NDIR * 8) + lax.shift_right_logical(x, 7) * 2 + lax.bitwise_and(y, 1)
+                    row = place_ref[lax.shift_right_logical(y, 1)] * (NDIR * 8) + lax.shift_right_logical(x, 7) * 2 + lax.bitwise_and(y, 1)
                     got = p_ref[pl.ds(row, NDIR, stride=8), :]
                     turn = lax.bitwise_and(col - x, LANES - 1)
                     acc = jnp.where(lane == col, pltpu.roll(got, turn, 1), acc)
@@ -228,6 +292,7 @@
     return pl.pallas_call(
         pick_kernel,
         in_specs=[
+            pl.BlockSpec(memory_space=pltpu.SMEM),
             pl.BlockSpec(memory_space=pltpu.SMEM),
             pl.BlockSpec(memory_space=pltpu.SMEM),
             pl.BlockSpec(memory_space=pltpu.VMEM),
@@ -237,26 +302,28 @@
         compiler_params=pltpu.CompilerParams(vmem_limit_bytes=8 * MIB),
         cost_estimate=pl.CostEstimate(flops=10_000_000, bytes_accessed=6_000_000, transcendentals=0),
         name="pick",
-    )(group, cells, moved.reshape(32 * NDIR * 8, LANES))
+    )(group, cells, jnp.asarray(PLACE, jnp.int32), moved.reshape(32 * NDIR * 8, LANES))
 
 
 def merge_kernel(*refs):
     *ins, out = refs
-    for n in range(ins[0].shape[0]):
+    nests = ins[0].shape[0]
+    for n in range(nests):
         total = ins[0][n]
         for r in ins[1:]:
             total = total + r[n]
-        out[:, n, :] = total
+        out[pl.ds(n, NDIR, stride=nests), :] = total
 
 
 def merge(parts):
     nests = parts[0].shape[0]
-    return pl.pallas_call(
+    out = pl.pallas_call(
         merge_kernel,
-        out_shape=jax.ShapeDtypeStruct((NDIR, nests, LANES), jnp.float32),
+        out_shape=jax.ShapeDtypeStruct((NDIR * nests, LANES), jnp.float32),
         compiler_params=pltpu.CompilerParams(vmem_limit_bytes=4 * MIB),
         name="merge",
     )(*parts)
+    return out.reshape(NDIR, nests, LANES)
 
 
 FCHUNK = 4
@@ -272,10 +339,10 @@
         fetch(c).start()
     total = jnp.zeros((8, LANES), jnp.float32)
     weighted = jnp.zeros((8, LANES), jnp.float32)
-    for f in range(NFREQ):
-        if f % FCHUNK == 0:
-            fetch(f // FCHUNK).wait()
-        s = jnp.sum(buf[f], axis=0)
+    for p, f in enumerate(ORDER):
+        if p % FCHUNK == 0:
+            fetch(p // FCHUNK).wait()
+        s = jnp.sum(buf[p], axis=0)
         total = total + s
         weighted = weighted + s * float(SCALE[f] * SCALE[f])
     m0 = total * (1.0 / (NFREQ * NDIR))
@@ -293,7 +360,7 @@
             proj = u * float(COS[d]) + v * float(SIN[d])
             for i, f in enumerate(fs):
                 gain = jnp.maximum(proj * float(0.05 * SCALE[f] ** 2 * LOG2E) - float(0.05 * SCALE[f] * LOG2E), 0.0)
-                outbuf[f, d] = buf[f, d] * jnp.exp2(gain - loss[i])
+                outbuf[f, d] = buf[PLACE[f], d] * jnp.exp2(gain - loss[i])
         put(c).start()
     for c in range(NCHUNK):
         put(c).wait()
@@ -328,8 +395,9 @@
     up, down = pack(block, mask)
     from_south = lax.ppermute(up, "grp", [(i, i + 1) for i in range(size - 1)])
     from_north = lax.ppermute(down, "grp", [(i + 1, i) for i in range(size - 1)])
-    result = propagate(block, courant, mask, from_south, from_north)
-    moved = lax.all_to_all(result, "comp", split_axis=0, concat_axis=0, tiled=True)
+    inner, tiles = interior(block, courant, mask)
+    result = edges(tiles, courant, mask, from_south, from_north, inner)
+    moved = lax.all_to_all(result, "comp", split_axis=0, concat_axis=0, axis_index_groups=[list(ORDER)], tiled=True)
     picked = pick(group, boundary_cells, result, size)
     parts = [picked[0]]
     for k in range(1, size):

time: 96.3 us -> 89.2 us (0.926)
  waiting for transfers between devices: 38.4 us -> 27.5 us
  Pallas kernels: 35.4 us -> 38.5 us
    all_to_all x1, waiting for transfers between devices: 24.5 us -> 18.8 us  [per_device(): lax.all_to_all(result, 'comp', split_axis=0, concat_axis=0, axis_index_gr...]
    ppermute x1, waiting for transfers between devices: 3.23 us -> 0.01 us  [per_device(): lax.ppermute(down, 'grp', [(i + 1, i) for i in range(size - 1)])]
    pallas_call x2 -> x3, Pallas kernels: 8.44 us -> 10.5 us  [the longest x1 8.11 us: interior(): pl.pallas_call(interior_kernel, in_specs=[smem, smem, hbm, vmem], out_spe...]
    ppermute x3, waiting for transfers between devices: 10.2 us -> 8.63 us  [per_device(): lax.ppermute(picked[k], 'grp', [(i, (i + k) % size) for i in range(size)])]
    ppermute x3, starting transfers between devices: 3.43 us -> 4.82 us  [per_device(): lax.ppermute(picked[k], 'grp', [(i, (i + k) % size) for i in range(size)])]
    unnamed x15 -> x16, local copies, waits for them, and re-layouts: 3.26 us -> 2.39 us
  transfers between devices with their start and end apart: 6 -> 6, of which waited for: 6 -> 4; matrix products, arithmetic and copies ran while one was open for 1% -> 0% of each run, Pallas kernels for 22% -> 35%
where the time goes in v4:
time: 89.2 us; the launch traced here: 88 us
  Pallas kernels  38.5 us (43%)
  waiting for transfers between devices  27.5 us (31%)
  starting transfers between devices  18.2 us (20%)
  local copies, waits for them, and re-layouts  2.39 us (3%)
  between operations  1.46 us (2%)
    pallas_call x1, Pallas kernels, pick(): pl.pallas_call(pick_kernel, in_specs=[pl.BlockSpec(memory_space=pltpu.SME...  22.1 us
    all_to_all x1, waiting for transfers between devices, per_device(): lax.all_to_all(result, 'comp', split_axis=0, concat_axis=0, axis_index_gr...  18.8 us
    ppermute x3, waiting for transfers between devices, per_device(): lax.ppermute(picked[k], 'grp', [(i, (i + k) % size) for i in range(size)])  8.63 us
    pallas_call x1, Pallas kernels, interior(): pl.pallas_call(interior_kernel, in_specs=[smem, smem, hbm, vmem], out_spe...  8.11 us
    all_to_all x1, starting transfers between devices, per_device(): lax.all_to_all(result, 'comp', split_axis=0, concat_axis=0, axis_index_gr...  7.53 us
    ppermute x3, starting transfers between devices, per_device(): lax.ppermute(picked[k], 'grp', [(i, (i + k) % size) for i in range(size)])  4.82 us
    pallas_call x1, Pallas kernels, sources(): pl.pallas_call(source_kernel, in_specs=[pl.BlockSpec(memory_space=pl.ANY)...  4.81 us
    ppermute x1, starting transfers between devices, per_device(): from_south = lax.ppermute(up, 'grp', [(i, i + 1) for i in range(size - 1)])  3.4 us
  transfers between devices with their start and end apart: 6, of which 4 were waited for; matrix products, arithmetic and copies ran while one was open for 0% of the time, Pallas kernels for 35%

profile of v4, /device:TPU:34, one launch (start us, length us, event | category | flops | bytes accessed | tf_op | source)
XLA Modules:
  0.0 88.0 jit_solution(13126571986756458888)
XLA Ops:
  0.6 0.0 copy-start.6
  0.6 0.0 copy-start.1
  0.7 0.0 copy-start.2
  0.7 1.1 %pack.1 = (f32[20,4,3,1,128]{4,3,2,1,0:T(1,128)S(1)}, f32[20,4,3,1,128]{4,3,2,1,0:T(1,128)S(1)}) custom-call(f32[36,8,4,8,1,128]{5,4,3,2,1,0:T(1,128)} %bitcast.40, s32[8,4,8,1,128]{4,3,2,1,0:T(1,128)} %bitcast.33), custom_call_target="tpu_custom_call" | custom-call | tf_op jit(solution)/shard_map/pack/pallas_call | solution.py:67
  1.7 3.4 %collective-permute-start = (f32[240,128]{1,0:T(8,128)S(1)}, f32[240,128]{1,0:T(8,128)S(1)}, u32[]{:S(2)}, u32[]{:S(2)}) collective-permute-start(f32[240,128]{1,0:T(8,128)S(1)} %bitcast.39), channel_id=1, source_target_pairs={{0,1},{1,2},{2,3},{4,5},{5,6},{6,7},{8,9},{9,10},{10,11},{12,13},{... | collective-permute-start | bytes 368648 | tf_op jit(solution)/shard_map/ppermute | solution.py:396
  5.1 2.4 %collective-permute-start.1 = (f32[240,128]{1,0:T(8,128)S(1)}, f32[240,128]{1,0:T(8,128)S(1)}, u32[]{:S(2)}, u32[]{:S(2)}) collective-permute-start(f32[240,128]{1,0:T(8,128)S(1)} %bitcast.38), channel_id=1, source_target_pairs={{1,0},{2,1},{3,2},{5,4},{6,5},{7,6},{9,8},{10,9},{11,10},{13,12},{... | collective-permute-start | bytes 368648 | tf_op jit(solution)/shard_map/ppermute | solution.py:397
  8.2 0.0 copy-done.6
  8.2 0.0 copy-done.1
  8.3 8.1 %interior.1 = (f32[32,36,8,128]{3,2,1,0:T(8,128)}, f32[2,18,4,8,128]{4,3,2,1,0:T(8,128)S(1)}) custom-call(f32[1]{0:T(128)S(6)} %copy.23.courant_ref, f32[2,36]{1,0:T(2,128)S(1)} %copy-done.6, f32[36,8,4,8,128]{4,3,2,1,0:T(8,128)} %bitcast.41, s32[8,4,8,128]{3,2,1,0:T(8,128)S(1)} %bitcast.34), custom_call_target="tpu_custom_call" | custom-call | flops 40000000 | bytes 9500000 | tf_op jit(solution)/shard_map/interior/pallas_call | solution.py:151
  16.4 0.0 collective-permute-done.south_ref
  16.4 0.0 collective-permute-done.1.north_ref
  16.4 0.0 copy-done.2
  16.4 1.7 %edges.1 = f32[32,36,8,128]{3,2,1,0:T(8,128)} custom-call(f32[1]{0:T(128)S(6)} %copy.23.courant_ref, f32[4,24,128]{2,1,0:T(8,128)S(1)} %copy-done.2, f32[2,18,4,8,128]{4,3,2,1,0:T(8,128)S(1)} %get-tuple-element.10.tile_ref, s32[8,4,8,128]{3,2,1,0:T(8,128)S(1)} %bitcast.35, ...), custom_call_target="tpu_custom_call", output_to_operand_aliasing={{}: (6, {})} | custom-call | tf_op jit(solution)/shard_map/edges/pallas_call | solution.py:250
  18.1 0.0 copy-start.3
  18.1 0.0 copy-start.7
  18.1 7.5 %all-to-all-start = ((f32[32,36,8,128]{3,2,1,0:T(8,128)}), f32[32,36,8,128]{3,2,1,0:T(8,128)}, u32[]{:S(2)}, u32[]{:S(2)}) async-start(f32[32,36,8,128]{3,2,1,0:T(8,128)} %edges.1), calls=%async_computation | async-start | bytes 9437184 | tf_op jit(solution)/shard_map/all_to_all | solution.py:400
  25.7 0.0 copy-start.4
  25.7 0.0 copy-start.5
  25.7 0.0 copy-done.3
  25.7 0.0 copy-done.7
  25.7 0.0 copy-start
  25.7 2.3 %copy-done = f32[32,36,8,128]{3,2,1,0:T(8,128)S(1)} copy-done((f32[32,36,8,128]{3,2,1,0:T(8,128)S(1)}, f32[32,36,8,128]{3,2,1,0:T(8,128)}, u32[]{:S(2)}) %copy-start) | copy-done | bytes 4718616
  28.1 22.1 %pick.1 = (f32[10,36,128]{2,1,0:T(8,128)S(1)}, f32[10,36,128]{2,1,0:T(8,128)S(1)}, f32[10,36,128]{2,1,0:T(8,128)S(1)}, f32[10,36,128]{2,1,0:T(8,128)S(1)}) custom-call(s32[1]{0:T(128)} %bitcast.20.grp_ref, s32[40,128]{1,0:T(8,128)S(1)} %copy-done.3, s32[32]{0:T(128)S(1)} %copy-done.7, f32[9216,128]{1,0:T(8,128)S(1)} %bitcast.32), custom_call_target="tpu_custom_call" | custom-call | flops 10000000 | bytes 6000000 | tf_op jit(solution)/shard_map/pick/pallas_call | solution.py:292
  50.2 1.6 %collective-permute-start.2 = (f32[10,36,128]{2,1,0:T(8,128)S(1)}, f32[10,36,128]{2,1,0:T(8,128)S(1)}, u32[]{:S(2)}, u32[]{:S(2)}) collective-permute-start(f32[10,36,128]{2,1,0:T(8,128)S(1)} %get-tuple-element.15), channel_id=1, source_target_pairs={{0,1},{1,2},{2,3},{3,0},{4,5},{5,6},{6,7},{7,4},{8,9},{9,10},{10,1... | collective-permute-start | bytes 552968 | tf_op jit(solution)/shard_map/ppermute | solution.py:404
  51.7 0.7 collective-permute-start.3
  52.4 2.5 %collective-permute-start.4 = (f32[10,36,128]{2,1,0:T(8,128)S(1)}, f32[10,36,128]{2,1,0:T(8,128)S(1)}, u32[]{:S(2)}, u32[]{:S(2)}) collective-permute-start(f32[10,36,128]{2,1,0:T(8,128)S(1)} %get-tuple-element.17), channel_id=1, source_target_pairs={{0,3},{1,0},{2,1},{3,2},{4,7},{5,4},{6,5},{7,6},{8,11},{9,8},{10,9... | collective-permute-start | bytes 552968 | tf_op jit(solution)/shard_map/ppermute | solution.py:404
  55.0 3.2 %collective-permute-done.2.refs_1_ = f32[10,36,128]{2,1,0:T(8,128)S(1)} collective-permute-done((f32[10,36,128]{2,1,0:T(8,128)S(1)}, f32[10,36,128]{2,1,0:T(8,128)S(1)}, u32[]{:S(2)}, u32[]{:S(2)}) %collective-permute-start.2) | collective-permute-done | bytes 184352 | tf_op jit(solution)/shard_map/ppermute | solution.py:404
  58.2 3.0 %collective-permute-done.3.refs_2_ = f32[10,36,128]{2,1,0:T(8,128)S(1)} collective-permute-done((f32[10,36,128]{2,1,0:T(8,128)S(1)}, f32[10,36,128]{2,1,0:T(8,128)S(1)}, u32[]{:S(2)}, u32[]{:S(2)}) %collective-permute-start.3) | collective-permute-done | bytes 184352 | tf_op jit(solution)/shard_map/ppermute | solution.py:404
  61.2 2.4 %collective-permute-done.4.refs_3_ = f32[10,36,128]{2,1,0:T(8,128)S(1)} collective-permute-done((f32[10,36,128]{2,1,0:T(8,128)S(1)}, f32[10,36,128]{2,1,0:T(8,128)S(1)}, u32[]{:S(2)}, u32[]{:S(2)}) %collective-permute-start.4) | collective-permute-done | bytes 184352 | tf_op jit(solution)/shard_map/ppermute | solution.py:404
  63.6 0.7 merge.1
  64.3 18.8 %all-to-all-done.recv_ref = f32[32,36,8,128]{3,2,1,0:T(8,128)} async-done(((f32[32,36,8,128]{3,2,1,0:T(8,128)}), f32[32,36,8,128]{3,2,1,0:T(8,128)}, u32[]{:S(2)}, u32[]{:S(2)}) %all-to-all-start) | async-done | bytes 4718624 | tf_op jit(solution)/shard_map/all_to_all | solution.py:400
  83.2 4.8 %sources.1 = f32[32,36,8,128]{3,2,1,0:T(8,128)} custom-call(f32[32,36,8,128]{3,2,1,0:T(8,128)} %all-to-all-done.recv_ref, f32[8,128]{1,0:T(8,128)S(1)} %bitcast.36, f32[8,128]{1,0:T(8,128)S(1)} %bitcast.37), custom_call_target="tpu_custom_call" | custom-call | tf_op jit(solution)/shard_map/sources/pallas_call | solution.py:372
  (2 shorter events, 0.0 us)
Async XLA Ops:
  0.6 7.6 %copy-start.6 = (f32[2,36]{1,0:T(2,128)S(1)}, f32[2,36]{1,0:T(2,128)}, u32[]{:S(2)}) copy-start(f32[2,36]{1,0:T(2,128)} %constant.10.clone.trig_ref) | copy-start | bytes 868
  0.6 7.6 %copy-start.1 = (s32[1,64,512]{2,1,0:T(8,128)S(1)}, s32[1,64,512]{2,1,0:T(8,128)}, u32[]{:S(2)}) copy-start(s32[1,64,512]{2,1,0:T(8,128)} %param.11) | copy-start | bytes 393220
  0.7 15.8 %copy-start.2 = (f32[4,24,128]{2,1,0:T(8,128)S(1)}, f32[4,24,128]{2,1,0:T(8,128)}, u32[]{:S(2)}) copy-start(f32[4,24,128]{2,1,0:T(8,128)} %constant.11.clone.table_ref) | copy-start | bytes 147460
  1.7 14.7 %collective-permute-start = (f32[240,128]{1,0:T(8,128)S(1)}, f32[240,128]{1,0:T(8,128)S(1)}, u32[]{:S(2)}, u32[]{:S(2)}) collective-permute-start(f32[240,128]{1,0:T(8,128)S(1)} %bitcast.39), channel_id=1, source_target_pairs={{0,1},{1,2},{2,3},{4,5},{5,6},{6,7},{8,9},{9,10},{10,11},{12,13},{... | collective-permute-start | bytes 368648 | tf_op jit(solution)/shard_map/ppermute | solution.py:396
  5.1 11.3 %collective-permute-start.1 = (f32[240,128]{1,0:T(8,128)S(1)}, f32[240,128]{1,0:T(8,128)S(1)}, u32[]{:S(2)}, u32[]{:S(2)}) collective-permute-start(f32[240,128]{1,0:T(8,128)S(1)} %bitcast.38), channel_id=1, source_target_pairs={{1,0},{2,1},{3,2},{5,4},{6,5},{7,6},{9,8},{10,9},{11,10},{13,12},{... | collective-permute-start | bytes 368648 | tf_op jit(solution)/shard_map/ppermute | solution.py:397
  18.1 7.6 %copy-start.3 = (s32[40,128]{1,0:T(8,128)S(1)}, s32[40,128]{1,0:T(8,128)}, u32[]{:S(2)}) copy-start(s32[40,128]{1,0:T(8,128)} %cells_ref.1) | copy-start | bytes 61444
  18.1 7.6 %copy-start.7 = (s32[32]{0:T(128)S(1)}, s32[32]{0:T(128)}, u32[]{:S(2)}) copy-start(s32[32]{0:T(128)} %constant.12.clone.place_ref) | copy-start | bytes 388
  18.1 65.0 %all-to-all-start = ((f32[32,36,8,128]{3,2,1,0:T(8,128)}), f32[32,36,8,128]{3,2,1,0:T(8,128)}, u32[]{:S(2)}, u32[]{:S(2)}) async-start(f32[32,36,8,128]{3,2,1,0:T(8,128)} %edges.1), calls=%async_computation | async-start | bytes 9437184 | tf_op jit(solution)/shard_map/all_to_all | solution.py:400
  25.7 57.5 %copy-start.4 = (f32[1,2,512]{2,1,0:T(2,128)S(1)}, f32[1,2,512]{2,1,0:T(2,128)}, u32[]{:S(2)}) copy-start(f32[1,2,512]{2,1,0:T(2,128)} %param.12) | copy-start | bytes 12292
  25.7 57.5 %copy-start.5 = (f32[1,2,512]{2,1,0:T(2,128)S(1)}, f32[1,2,512]{2,1,0:T(2,128)}, u32[]{:S(2)}) copy-start(f32[1,2,512]{2,1,0:T(2,128)} %param.13) | copy-start | bytes 12292
  25.7 2.4 %copy-start = (f32[32,36,8,128]{3,2,1,0:T(8,128)S(1)}, f32[32,36,8,128]{3,2,1,0:T(8,128)}, u32[]{:S(2)}) copy-start(f32[32,36,8,128]{3,2,1,0:T(8,128)} %edges.1) | copy-start | bytes 14155780
  50.2 8.0 %collective-permute-start.2 = (f32[10,36,128]{2,1,0:T(8,128)S(1)}, f32[10,36,128]{2,1,0:T(8,128)S(1)}, u32[]{:S(2)}, u32[]{:S(2)}) collective-permute-start(f32[10,36,128]{2,1,0:T(8,128)S(1)} %get-tuple-element.15), channel_id=1, source_target_pairs={{0,1},{1,2},{2,3},{3,0},{4,5},{5,6},{6,7},{7,4},{8,9},{9,10},{10,1... | collective-permute-start | bytes 552968 | tf_op jit(solution)/shard_map/ppermute | solution.py:404
  51.7 9.5 %collective-permute-start.3 = (f32[10,36,128]{2,1,0:T(8,128)S(1)}, f32[10,36,128]{2,1,0:T(8,128)S(1)}, u32[]{:S(2)}, u32[]{:S(2)}) collective-permute-start(f32[10,36,128]{2,1,0:T(8,128)S(1)} %get-tuple-element.16), channel_id=1, source_target_pairs={{0,2},{1,3},{2,0},{3,1},{4,6},{5,7},{6,4},{7,5},{8,10},{9,11},{10,... | collective-permute-start | bytes 552968 | tf_op jit(solution)/shard_map/ppermute | solution.py:404
  52.4 11.2 %collective-permute-start.4 = (f32[10,36,128]{2,1,0:T(8,128)S(1)}, f32[10,36,128]{2,1,0:T(8,128)S(1)}, u32[]{:S(2)}, u32[]{:S(2)}) collective-permute-start(f32[10,36,128]{2,1,0:T(8,128)S(1)} %get-tuple-element.17), channel_id=1, source_target_pairs={{0,3},{1,0},{2,1},{3,2},{4,7},{5,4},{6,5},{7,6},{8,11},{9,8},{10,9... | collective-permute-start | bytes 552968 | tf_op jit(solution)/shard_map/ppermute | solution.py:404

commit v5 on v4

--- a/solution.py
+++ b/solution.py
@@ -44,36 +44,51 @@
     return pltpu.with_memory_space_constraint(value, pltpu.HBM)
 
 
-def pack_kernel(spectrum_ref, mask_ref, up_ref, down_ref, mask_s, sem):
-    sides = ((up_ref, 0, ROWS // 8 - 1, 8 - HALO), (down_ref, HALF, 0, 0))
-    copies = []
-    for side, (out, d, tile, low) in enumerate(sides):
-        for k, (src, dst) in enumerate((
-            (spectrum_ref.at[pl.ds(d, HALF), tile, :, pl.ds(low, HALO)], out.at[pl.ds(0, HALF)]),
-            (mask_ref.at[tile, :, pl.ds(low, HALO)], mask_s.at[side]),
-        )):
-            copies.append(pltpu.make_async_copy(src, dst, sem.at[2 * side + k]))
-    for c in copies:
-        c.start()
+def pack_kernel(grp_ref, spectrum_ref, mask_ref, out_ref, packed, mask_s, sem):
+    size = out_ref.shape[0]
+    group = grp_ref[0]
+    sides = (
+        (lax.rem(group + 1, size), 0, ROWS // 8 - 1, 8 - HALO),
+        (lax.rem(group + size - 1, size), HALF, 0, 0),
+    )
+    rows, masks, puts = [], [], []
+    for side, (slot, d, tile, low) in enumerate(sides):
+        near = pl.ds(low, HALO)
+        rows.append(
+            pltpu.make_async_copy(
+                spectrum_ref.at[pl.ds(d, HALF), tile, :, near], packed.at[side, pl.ds(0, HALF)], sem.at[side]
+            )
+        )
+        masks.append(pltpu.make_async_copy(mask_ref.at[tile, :, near], mask_s.at[side], sem.at[2 + side]))
+        puts.append(pltpu.make_async_copy(packed.at[side], out_ref.at[slot], sem.at[4 + side]))
+    for copy in rows + masks:
+        copy.start()
     for side in range(2):
-        copies[2 * side + 1].wait()
-        sides[side][0][HALF] = mask_s[side].astype(jnp.float32)
+        masks[side].wait()
+        packed[side, HALF] = mask_s[side].astype(jnp.float32)
+        packed[side, HALF + 1] = jnp.zeros((TILES, HALO, 1, LANES), jnp.float32)
     for side in range(2):
-        copies[2 * side].wait()
-
-
-def pack(spectrum, mask):
-    out = jax.ShapeDtypeStruct((SLOTS, TILES, HALO, 1, LANES), jnp.float32)
-    up, down = pl.pallas_call(
+        rows[side].wait()
+        puts[side].start()
+    for copy in puts:
+        copy.wait()
+
+
+def pack(group, spectrum, mask, size):
+    out = pl.pallas_call(
         pack_kernel,
-        in_specs=[pl.BlockSpec(memory_space=pl.ANY)] * 2,
-        out_specs=[pl.BlockSpec(memory_space=pltpu.VMEM)] * 2,
-        out_shape=[out, out],
-        scratch_shapes=[pltpu.VMEM((2, TILES, HALO, 1, LANES), jnp.int32), pltpu.SemaphoreType.DMA((4,))],
+        in_specs=[pl.BlockSpec(memory_space=pltpu.SMEM)] + [pl.BlockSpec(memory_space=pl.ANY)] * 2,
+        out_specs=pl.BlockSpec(memory_space=pl.ANY),
+        out_shape=pltpu.HBM((size, SLOTS, TILES, HALO, 1, LANES), jnp.float32),
+        scratch_shapes=[
+            pltpu.VMEM((2, SLOTS, TILES, HALO, 1, LANES), jnp.float32),
+            pltpu.VMEM((2, TILES, HALO, 1, LANES), jnp.int32),
+            pltpu.SemaphoreType.DMA((6,)),
+        ],
         compiler_params=pltpu.CompilerParams(vmem_limit_bytes=2 * MIB),
         name="pack",
-    )(in_hbm(spectrum[..., None, :]), in_hbm(mask[..., None, :]))
-    return up.reshape(SLOTS * SLOT, LANES), down.reshape(SLOTS * SLOT, LANES)
+    )(group, in_hbm(spectrum[..., None, :]), in_hbm(mask[..., None, :]))
+    return out.reshape(size, SLOTS * SLOT, LANES)
 
 
 FETCH = 3
@@ -172,7 +187,7 @@
 EDGE = 4
 
 
-def edges_kernel(courant_ref, table_ref, tile_ref, mask_ref, south_ref, north_ref, p_in, p_ref, fixed, sem):
+def edges_kernel(grp_ref, courant_ref, table_ref, tile_ref, mask_ref, halo_ref, p_in, p_ref, fixed, sem):
     del p_in
     sub = lax.broadcasted_iota(jnp.int32, (8, LANES), 0)
     flat_mask = mask_ref.reshape(ROWS * TILES, LANES)
@@ -183,7 +198,15 @@
         v = ref[pl.ds(start, n, stride=stride), :]
         return v if n == 8 else jnp.concatenate([v, jnp.zeros((8 - n, LANES), jnp.float32)], axis=0)
 
-    for side, halo in enumerate((south_ref, north_ref)):
+    size = halo_ref.shape[0]
+    group = grp_ref[0]
+    neighbours = (
+        (lax.rem(group + size - 1, size), group > 0),
+        (lax.rem(group + 1, size), group < size - 1),
+    )
+    for side, (source, inside) in enumerate(neighbours):
+        halo = halo_ref.at[source]
+        keep = jnp.where(inside, 1.0, 0.0)
         south = side == 0
         tiles = tile_ref.at[side].reshape(HALF * ROWBLOCK, LANES)
         rows_out = fixed.at[side].reshape(2 * HALF * 8, LANES)
@@ -208,7 +231,7 @@
             e = []
             for p in range(total):
                 if p < HALO:
-                    e.append([eight(halo, g * SLOT + j * HALO + sent(p), n, SLOT) for j in range(TILES)])
+                    e.append([keep * eight(halo, g * SLOT + j * HALO + sent(p), n, SLOT) for j in range(TILES)])
                 else:
                     e.append([eight(tiles, g * ROWBLOCK + j * 8 + own(p), n, ROWBLOCK) for j in range(TILES)])
             for k in range(SUBSTEPS):
@@ -239,7 +262,7 @@
         put.wait()
 
 
-def edges(tiles, courant, mask, from_south, from_north, inner):
+def edges(group, tiles, courant, mask, halos, inner):
     table = np.zeros((4, 24, LANES), np.float32)
     for side in range(2):
         ds = slice(side * HALF, (side + 1) * HALF)
@@ -249,14 +272,14 @@
     hbm = pl.BlockSpec(memory_space=pl.ANY)
     return pl.pallas_call(
         edges_kernel,
-        in_specs=[pl.BlockSpec(memory_space=pltpu.SMEM), vmem, vmem, vmem, vmem, vmem, hbm],
+        in_specs=[pl.BlockSpec(memory_space=pltpu.SMEM)] * 2 + [vmem, vmem, vmem, vmem, hbm],
         out_specs=hbm,
         out_shape=pltpu.HBM(inner.shape, inner.dtype),
         scratch_shapes=[pltpu.VMEM((2, 2, HALF, 8, LANES), jnp.float32), pltpu.SemaphoreType.DMA((4,))],
         input_output_aliases={6: 0},
         compiler_params=pltpu.CompilerParams(vmem_limit_bytes=4 * MIB),
         name="edges",
-    )(courant, jnp.asarray(table), tiles, mask, from_south, from_north, in_hbm(inner))
+    )(group, courant, jnp.asarray(table), tiles, mask, halos, in_hbm(inner))
 
 
 def pick_kernel(grp_ref, cells_ref, place_ref, p_ref, *out_refs):
@@ -392,11 +415,10 @@
     group = lax.axis_index("grp").astype(jnp.int32).reshape(1)
     block = tiled(spectrum.reshape(NDIR, ROWS, COLS))
     mask = tiled(sea_mask.reshape(ROWS, COLS))
-    up, down = pack(block, mask)
-    from_south = lax.ppermute(up, "grp", [(i, i + 1) for i in range(size - 1)])
-    from_north = lax.ppermute(down, "grp", [(i + 1, i) for i in range(size - 1)])
+    halos = pack(group, block, mask, size)
+    halos = lax.all_to_all(halos, "grp", split_axis=0, concat_axis=0, tiled=True)
     inner, tiles = interior(block, courant, mask)
-    result = edges(tiles, courant, mask, from_south, from_north, inner)
+    result = edges(group, tiles, courant, mask, halos, inner)
     moved = lax.all_to_all(result, "comp", split_axis=0, concat_axis=0, axis_index_groups=[list(ORDER)], tiled=True)
     picked = pick(group, boundary_cells, result, size)
     parts = [picked[0]]

time: 89.2 us -> 88.9 us (level)
  starting transfers between devices: 18.2 us -> 17.1 us
    ppermute x2 -> x0, starting transfers between devices: 5.85 us -> none  [the longest x1 3.4 us: per_device(): from_south = lax.ppermute(up, 'grp', [(i, i + 1) for i in range(size - 1)])]
    all_to_all x0 -> x1, starting transfers between devices: none -> 4.82 us  [per_device(): lax.all_to_all(halos, 'grp', split_axis=0, concat_axis=0, tiled=True)]
  transfers between devices with their start and end apart: 6 -> 5, of which waited for: 4 -> 4; matrix products, arithmetic and copies ran while one was open for 0% -> 0% of each run, Pallas kernels for 35% -> 35%
where the time goes in v5:
time: 88.9 us; the launch traced here: 87.6 us
  Pallas kernels  39.1 us (44%)
  waiting for transfers between devices  27.5 us (31%)
  starting transfers between devices  17.1 us (19%)
  local copies, waits for them, and re-layouts  2.4 us (3%)
  between operations  1.43 us (2%)
    pallas_call x1, Pallas kernels, pick(): pl.pallas_call(pick_kernel, in_specs=[pl.BlockSpec(memory_space=pltpu.SME...  22.1 us
    all_to_all x1, waiting for transfers between devices, per_device(): lax.all_to_all(result, 'comp', split_axis=0, concat_axis=0, axis_index_gr...  18.9 us
    ppermute x3, waiting for transfers between devices, per_device(): lax.ppermute(picked[k], 'grp', [(i, (i + k) % size) for i in range(size)])  8.63 us
    pallas_call x1, Pallas kernels, interior(): pl.pallas_call(interior_kernel, in_specs=[smem, smem, hbm, vmem], out_spe...  8.11 us
    all_to_all x1, starting transfers between devices, per_device(): lax.all_to_all(result, 'comp', split_axis=0, concat_axis=0, axis_index_gr...  7.53 us
    all_to_all x1, starting transfers between devices, per_device(): lax.all_to_all(halos, 'grp', split_axis=0, concat_axis=0, tiled=True)  4.82 us
    pallas_call x1, Pallas kernels, sources(): pl.pallas_call(source_kernel, in_specs=[pl.BlockSpec(memory_space=pl.ANY)...  4.81 us
    ppermute x3, starting transfers between devices, per_device(): lax.ppermute(picked[k], 'grp', [(i, (i + k) % size) for i in range(size)])  4.77 us
  transfers between devices with their start and end apart: 5, of which 4 were waited for; matrix products, arithmetic and copies ran while one was open for 0% of the time, Pallas kernels for 35%

profile of v5, /device:TPU:34, one launch (start us, length us, event | category | flops | bytes accessed | tf_op | source)
XLA Modules:
  0.0 87.6 jit_solution(11553710367872990243)
XLA Ops:
  0.6 0.0 copy-start.6
  0.6 0.0 copy-start.1
  0.7 0.0 copy-start.2
  0.7 1.7 %pack.1 = f32[4,20,4,3,1,128]{5,4,3,2,1,0:T(1,128)} custom-call(s32[1]{0:T(128)} %bitcast.grp_ref, f32[36,8,4,8,1,128]{5,4,3,2,1,0:T(1,128)} %bitcast.37, s32[8,4,8,1,128]{4,3,2,1,0:T(1,128)} %bitcast.32), custom_call_target="tpu_custom_call" | custom-call | tf_op jit(solution)/shard_map/pack/pallas_call | solution.py:78
  2.4 4.8 %all-to-all-start = ((f32[4,240,128]{2,1,0:T(8,128)}), f32[4,240,128]{2,1,0:T(8,128)S(1)}, u32[]{:S(2)}, u32[]{:S(2)}) async-start(f32[4,240,128]{2,1,0:T(8,128)} %bitcast.40), calls=%async_computation | async-start | bytes 983040 | tf_op jit(solution)/shard_map/all_to_all | solution.py:419
  7.9 0.0 copy-done.6
  7.9 0.0 copy-done.1
  7.9 8.1 %interior.1 = (f32[32,36,8,128]{3,2,1,0:T(8,128)}, f32[2,18,4,8,128]{4,3,2,1,0:T(8,128)S(1)}) custom-call(f32[1]{0:T(128)S(6)} %copy.23.courant_ref, f32[2,36]{1,0:T(2,128)S(1)} %copy-done.6, f32[36,8,4,8,128]{4,3,2,1,0:T(8,128)} %bitcast.38, s32[8,4,8,128]{3,2,1,0:T(8,128)S(1)} %bitcast.33), custom_call_target="tpu_custom_call" | custom-call | flops 40000000 | bytes 9500000 | tf_op jit(solution)/shard_map/interior/pallas_call | solution.py:166
  16.0 0.0 all-to-all-done.halo_ref
  16.0 0.0 copy-done.2
  16.0 1.7 %edges.1 = f32[32,36,8,128]{3,2,1,0:T(8,128)} custom-call(s32[1]{0:T(128)} %bitcast.grp_ref, f32[1]{0:T(128)S(6)} %copy.23.courant_ref, f32[4,24,128]{2,1,0:T(8,128)S(1)} %copy-done.2, f32[2,18,4,8,128]{4,3,2,1,0:T(8,128)S(1)} %get-tuple-element.8.tile_ref, s32[8,4,8,128]{3,2,1,0:T(8,128)S(1)} %bitcast.34, ...), custom_call_target="tpu_custom_call", output_to_operand_aliasing={{}: (6, {})} | custom-call | tf_op jit(solution)/shard_map/edges/pallas_call | solution.py:273
  17.7 0.0 copy-start.3
  17.8 0.0 copy-start.7
  17.8 7.5 %all-to-all-start.1 = ((f32[32,36,8,128]{3,2,1,0:T(8,128)}), f32[32,36,8,128]{3,2,1,0:T(8,128)}, u32[]{:S(2)}, u32[]{:S(2)}) async-start(f32[32,36,8,128]{3,2,1,0:T(8,128)} %edges.1), calls=%async_computation.1 | async-start | bytes 9437184 | tf_op jit(solution)/shard_map/all_to_all | solution.py:422
  25.3 0.0 copy-done.3
  25.3 0.0 copy-done.7
  25.3 0.0 copy-start
  25.3 2.4 %copy-done = f32[32,36,8,128]{3,2,1,0:T(8,128)S(1)} copy-done((f32[32,36,8,128]{3,2,1,0:T(8,128)S(1)}, f32[32,36,8,128]{3,2,1,0:T(8,128)}, u32[]{:S(2)}) %copy-start) | copy-done | bytes 4718616
  27.7 0.0 copy-start.4
  27.7 0.0 copy-start.5
  27.7 22.1 %pick.1 = (f32[10,36,128]{2,1,0:T(8,128)S(1)}, f32[10,36,128]{2,1,0:T(8,128)S(1)}, f32[10,36,128]{2,1,0:T(8,128)S(1)}, f32[10,36,128]{2,1,0:T(8,128)S(1)}) custom-call(s32[1]{0:T(128)} %bitcast.grp_ref, s32[40,128]{1,0:T(8,128)S(1)} %copy-done.3, s32[32]{0:T(128)S(1)} %copy-done.7, f32[9216,128]{1,0:T(8,128)S(1)} %bitcast.31), custom_call_target="tpu_custom_call" | custom-call | flops 10000000 | bytes 6000000 | tf_op jit(solution)/shard_map/pick/pallas_call | solution.py:315
  49.8 1.5 %collective-permute-start = (f32[10,36,128]{2,1,0:T(8,128)S(1)}, f32[10,36,128]{2,1,0:T(8,128)S(1)}, u32[]{:S(2)}, u32[]{:S(2)}) collective-permute-start(f32[10,36,128]{2,1,0:T(8,128)S(1)} %get-tuple-element.11), channel_id=1, source_target_pairs={{0,1},{1,2},{2,3},{3,0},{4,5},{5,6},{6,7},{7,4},{8,9},{9,10},{10,1... | collective-permute-start | bytes 552968 | tf_op jit(solution)/shard_map/ppermute | solution.py:426
  51.3 0.9 %collective-permute-start.1 = (f32[10,36,128]{2,1,0:T(8,128)S(1)}, f32[10,36,128]{2,1,0:T(8,128)S(1)}, u32[]{:S(2)}, u32[]{:S(2)}) collective-permute-start(f32[10,36,128]{2,1,0:T(8,128)S(1)} %get-tuple-element.12), channel_id=1, source_target_pairs={{0,2},{1,3},{2,0},{3,1},{4,6},{5,7},{6,4},{7,5},{8,10},{9,11},{10,... | collective-permute-start | bytes 552968 | tf_op jit(solution)/shard_map/ppermute | solution.py:426
  52.2 2.3 %collective-permute-start.2 = (f32[10,36,128]{2,1,0:T(8,128)S(1)}, f32[10,36,128]{2,1,0:T(8,128)S(1)}, u32[]{:S(2)}, u32[]{:S(2)}) collective-permute-start(f32[10,36,128]{2,1,0:T(8,128)S(1)} %get-tuple-element.13), channel_id=1, source_target_pairs={{0,3},{1,0},{2,1},{3,2},{4,7},{5,4},{6,5},{7,6},{8,11},{9,8},{10,9... | collective-permute-start | bytes 552968 | tf_op jit(solution)/shard_map/ppermute | solution.py:426
  54.5 3.2 %collective-permute-done.refs_1_ = f32[10,36,128]{2,1,0:T(8,128)S(1)} collective-permute-done((f32[10,36,128]{2,1,0:T(8,128)S(1)}, f32[10,36,128]{2,1,0:T(8,128)S(1)}, u32[]{:S(2)}, u32[]{:S(2)}) %collective-permute-start) | collective-permute-done | bytes 184352 | tf_op jit(solution)/shard_map/ppermute | solution.py:426
  57.8 3.0 %collective-permute-done.1.refs_2_ = f32[10,36,128]{2,1,0:T(8,128)S(1)} collective-permute-done((f32[10,36,128]{2,1,0:T(8,128)S(1)}, f32[10,36,128]{2,1,0:T(8,128)S(1)}, u32[]{:S(2)}, u32[]{:S(2)}) %collective-permute-start.1) | collective-permute-done | bytes 184352 | tf_op jit(solution)/shard_map/ppermute | solution.py:426
  60.8 2.4 %collective-permute-done.2.refs_3_ = f32[10,36,128]{2,1,0:T(8,128)S(1)} collective-permute-done((f32[10,36,128]{2,1,0:T(8,128)S(1)}, f32[10,36,128]{2,1,0:T(8,128)S(1)}, u32[]{:S(2)}, u32[]{:S(2)}) %collective-permute-start.2) | collective-permute-done | bytes 184352 | tf_op jit(solution)/shard_map/ppermute | solution.py:426
  63.2 0.7 merge.1
  63.9 18.9 %all-to-all-done.1.recv_ref = f32[32,36,8,128]{3,2,1,0:T(8,128)} async-done(((f32[32,36,8,128]{3,2,1,0:T(8,128)}), f32[32,36,8,128]{3,2,1,0:T(8,128)}, u32[]{:S(2)}, u32[]{:S(2)}) %all-to-all-start.1) | async-done | bytes 4718624 | tf_op jit(solution)/shard_map/all_to_all | solution.py:422
  82.8 0.0 copy-done.4
  82.8 0.0 copy-done.5
  82.8 4.8 %sources.1 = f32[32,36,8,128]{3,2,1,0:T(8,128)} custom-call(f32[32,36,8,128]{3,2,1,0:T(8,128)} %all-to-all-done.1.recv_ref, f32[8,128]{1,0:T(8,128)S(1)} %bitcast.35, f32[8,128]{1,0:T(8,128)S(1)} %bitcast.36), custom_call_target="tpu_custom_call" | custom-call | tf_op jit(solution)/shard_map/sources/pallas_call | solution.py:395
Async XLA Ops:
  0.6 7.3 %copy-start.6 = (f32[2,36]{1,0:T(2,128)S(1)}, f32[2,36]{1,0:T(2,128)}, u32[]{:S(2)}) copy-start(f32[2,36]{1,0:T(2,128)} %constant.10.clone.trig_ref) | copy-start | bytes 868
  0.6 7.2 %copy-start.1 = (s32[1,64,512]{2,1,0:T(8,128)S(1)}, s32[1,64,512]{2,1,0:T(8,128)}, u32[]{:S(2)}) copy-start(s32[1,64,512]{2,1,0:T(8,128)} %param.11) | copy-start | bytes 393220
  0.7 15.4 %copy-start.2 = (f32[4,24,128]{2,1,0:T(8,128)S(1)}, f32[4,24,128]{2,1,0:T(8,128)}, u32[]{:S(2)}) copy-start(f32[4,24,128]{2,1,0:T(8,128)} %constant.11.clone.table_ref) | copy-start | bytes 147460
  2.4 13.6 %all-to-all-start = ((f32[4,240,128]{2,1,0:T(8,128)}), f32[4,240,128]{2,1,0:T(8,128)S(1)}, u32[]{:S(2)}, u32[]{:S(2)}) async-start(f32[4,240,128]{2,1,0:T(8,128)} %bitcast.40), calls=%async_computation | async-start | bytes 983040 | tf_op jit(solution)/shard_map/all_to_all | solution.py:419
  17.7 7.6 %copy-start.3 = (s32[40,128]{1,0:T(8,128)S(1)}, s32[40,128]{1,0:T(8,128)}, u32[]{:S(2)}) copy-start(s32[40,128]{1,0:T(8,128)} %cells_ref.1) | copy-start | bytes 61444
  17.8 7.6 %copy-start.7 = (s32[32]{0:T(128)S(1)}, s32[32]{0:T(128)}, u32[]{:S(2)}) copy-start(s32[32]{0:T(128)} %constant.12.clone.place_ref) | copy-start | bytes 388
  17.8 65.0 %all-to-all-start.1 = ((f32[32,36,8,128]{3,2,1,0:T(8,128)}), f32[32,36,8,128]{3,2,1,0:T(8,128)}, u32[]{:S(2)}, u32[]{:S(2)}) async-start(f32[32,36,8,128]{3,2,1,0:T(8,128)} %edges.1), calls=%async_computation.1 | async-start | bytes 9437184 | tf_op jit(solution)/shard_map/all_to_all | solution.py:422
  25.3 2.4 %copy-start = (f32[32,36,8,128]{3,2,1,0:T(8,128)S(1)}, f32[32,36,8,128]{3,2,1,0:T(8,128)}, u32[]{:S(2)}) copy-start(f32[32,36,8,128]{3,2,1,0:T(8,128)} %edges.1) | copy-start | bytes 14155780
  27.7 55.1 %copy-start.4 = (f32[1,2,512]{2,1,0:T(2,128)S(1)}, f32[1,2,512]{2,1,0:T(2,128)}, u32[]{:S(2)}) copy-start(f32[1,2,512]{2,1,0:T(2,128)} %param.12) | copy-start | bytes 12292
  27.7 55.1 %copy-start.5 = (f32[1,2,512]{2,1,0:T(2,128)S(1)}, f32[1,2,512]{2,1,0:T(2,128)}, u32[]{:S(2)}) copy-start(f32[1,2,512]{2,1,0:T(2,128)} %param.13) | copy-start | bytes 12292
  49.8 8.0 %collective-permute-start = (f32[10,36,128]{2,1,0:T(8,128)S(1)}, f32[10,36,128]{2,1,0:T(8,128)S(1)}, u32[]{:S(2)}, u32[]{:S(2)}) collective-permute-start(f32[10,36,128]{2,1,0:T(8,128)S(1)} %get-tuple-element.11), channel_id=1, source_target_pairs={{0,1},{1,2},{2,3},{3,0},{4,5},{5,6},{6,7},{7,4},{8,9},{9,10},{10,1... | collective-permute-start | bytes 552968 | tf_op jit(solution)/shard_map/ppermute | solution.py:426
  51.3 9.5 %collective-permute-start.1 = (f32[10,36,128]{2,1,0:T(8,128)S(1)}, f32[10,36,128]{2,1,0:T(8,128)S(1)}, u32[]{:S(2)}, u32[]{:S(2)}) collective-permute-start(f32[10,36,128]{2,1,0:T(8,128)S(1)} %get-tuple-element.12), channel_id=1, source_target_pairs={{0,2},{1,3},{2,0},{3,1},{4,6},{5,7},{6,4},{7,5},{8,10},{9,11},{10,... | collective-permute-start | bytes 552968 | tf_op jit(solution)/shard_map/ppermute | solution.py:426
  52.2 10.9 %collective-permute-start.2 = (f32[10,36,128]{2,1,0:T(8,128)S(1)}, f32[10,36,128]{2,1,0:T(8,128)S(1)}, u32[]{:S(2)}, u32[]{:S(2)}) collective-permute-start(f32[10,36,128]{2,1,0:T(8,128)S(1)} %get-tuple-element.13), channel_id=1, source_target_pairs={{0,3},{1,0},{2,1},{3,2},{4,7},{5,4},{6,5},{7,6},{8,11},{9,8},{10,9... | collective-permute-start | bytes 552968 | tf_op jit(solution)/shard_map/ppermute | solution.py:426

commit v6 on v5

--- a/solution.py
+++ b/solution.py
@@ -126,8 +126,8 @@
         for stage in range(SUBSTEPS):
             new = [[None] * 8 for _ in many]
             moved = [[[pltpu.roll(v, turn, 0) for v in row] for row in e[u]] for u in many]
-            for t in range(8):
-                for u in many:
+            for u in many:
+                for t in range(8):
                     x = shifted(e[u][t], west)
                     y = moved[u][t]
                     if t != at:
@@ -195,8 +195,10 @@
     puts = []
 
     def eight(ref, start, n, stride):
-        v = ref[pl.ds(start, n, stride=stride), :]
-        return v if n == 8 else jnp.concatenate([v, jnp.zeros((8 - n, LANES), jnp.float32)], axis=0)
+        if n == 8:
+            return ref[pl.ds(start, n, stride=stride), :]
+        rows = [ref[start + k * stride : start + k * stride + 1, :] for k in range(n)]
+        return jnp.concatenate(rows + [jnp.zeros((8 - n, LANES), jnp.float32)], axis=0)
 
     size = halo_ref.shape[0]
     group = grp_ref[0]
@@ -250,7 +252,12 @@
             for p in range(HALO, total):
                 y = p - HALO if south else EDGE - 1 - (p - HALO)
                 for j in range(TILES):
-                    rows_out[pl.ds(((y // 2) * HALF + g) * 8 + 2 * j + y % 2, n, stride=8), :] = e[p][j][:n]
+                    at = ((y // 2) * HALF + g) * 8 + 2 * j + y % 2
+                    if n == 8:
+                        rows_out[pl.ds(at, n, stride=8), :] = e[p][j]
+                    else:
+                        for k in range(n):
+                            rows_out[at + 8 * k : at + 8 * k + 1, :] = e[p][j][k : k + 1]
         for i in range(2):
             place = PLACE[i if south else 30 + i]
             put = pltpu.make_async_copy(
@@ -282,7 +289,11 @@
     )(group, courant, jnp.asarray(table), tiles, mask, halos, in_hbm(inner))
 
 
-def pick_kernel(grp_ref, cells_ref, place_ref, p_ref, *out_refs):
+def pick_kernel(grp_ref, cells_ref, place_ref, source_ref, *refs):
+    *out_refs, p_ref, sem = refs
+    copy = pltpu.make_async_copy(source_ref, p_ref.at[pl.ds(0, 32 * NDIR * 8)], sem)
+    copy.start()
+    copy.wait()
     group = grp_ref[0]
     count = len(out_refs)
     lane = lax.broadcasted_iota(jnp.int32, (NDIR, LANES), 1)
@@ -318,14 +329,15 @@
             pl.BlockSpec(memory_space=pltpu.SMEM),
             pl.BlockSpec(memory_space=pltpu.SMEM),
             pl.BlockSpec(memory_space=pltpu.SMEM),
-            pl.BlockSpec(memory_space=pltpu.VMEM),
+            pl.BlockSpec(memory_space=pl.ANY),
         ],
         out_specs=[pl.BlockSpec(memory_space=pltpu.VMEM)] * count,
         out_shape=[jax.ShapeDtypeStruct((nests, NDIR, LANES), jnp.float32)] * count,
+        scratch_shapes=[pltpu.VMEM((32 * NDIR * 8 + 64, LANES), jnp.float32), pltpu.SemaphoreType.DMA],
         compiler_params=pltpu.CompilerParams(vmem_limit_bytes=8 * MIB),
         cost_estimate=pl.CostEstimate(flops=10_000_000, bytes_accessed=6_000_000, transcendentals=0),
         name="pick",
-    )(group, cells, jnp.asarray(PLACE, jnp.int32), moved.reshape(32 * NDIR * 8, LANES))
+    )(group, cells, jnp.asarray(PLACE, jnp.int32), in_hbm(moved.reshape(32 * NDIR * 8, LANES)))
 
 
 def merge_kernel(*refs):
@@ -335,7 +347,10 @@
         total = ins[0][n]
         for r in ins[1:]:
             total = total + r[n]
-        out[pl.ds(n, NDIR, stride=nests), :] = total
+        whole = NDIR // 8 * 8
+        out[pl.ds(n, whole, stride=nests), :] = total[:whole]
+        for d in range(whole, NDIR):
+            out[d * nests + n : d * nests + n + 1, :] = total[d : d + 1]
 
 
 def merge(parts):

time: 88.9 us -> 88.8 us (level)
  local copies, waits for them, and re-layouts: 2.4 us -> 0.04 us
  Pallas kernels: 39.1 us -> 41.2 us
    unnamed x16 -> x14, local copies, waits for them, and re-layouts: 2.4 us -> 0.04 us
    pallas_call x1, Pallas kernels: 22.1 us -> 24.3 us  [pick(): pl.pallas_call(pick_kernel, in_specs=[pl.BlockSpec(memory_space=pltpu.SME...]
  transfers between devices with their start and end apart: 5 -> 5, of which waited for: 4 -> 4; matrix products, arithmetic and copies ran while one was open for 0% -> 0% of each run, Pallas kernels for 35% -> 38%
where the time goes in v6:
time: 88.8 us; the launch traced here: 87.5 us
  Pallas kernels  41.2 us (46%)
  waiting for transfers between devices  27.7 us (31%)
  starting transfers between devices  17.1 us (19%)
  between operations  1.43 us (2%)
    pallas_call x1, Pallas kernels, pick(): pl.pallas_call(pick_kernel, in_specs=[pl.BlockSpec(memory_space=pltpu.SME...  24.3 us
    all_to_all x1, waiting for transfers between devices, per_device(): lax.all_to_all(result, 'comp', split_axis=0, concat_axis=0, axis_index_gr...  18.9 us
    ppermute x3, waiting for transfers between devices, per_device(): lax.ppermute(picked[k], 'grp', [(i, (i + k) % size) for i in range(size)])  8.73 us
    pallas_call x1, Pallas kernels, interior(): pl.pallas_call(interior_kernel, in_specs=[smem, smem, hbm, vmem], out_spe...  7.96 us
    all_to_all x1, starting transfers between devices, per_device(): lax.all_to_all(result, 'comp', split_axis=0, concat_axis=0, axis_index_gr...  7.53 us
    all_to_all x1, starting transfers between devices, per_device(): lax.all_to_all(halos, 'grp', split_axis=0, concat_axis=0, tiled=True)  4.82 us
    pallas_call x1, Pallas kernels, sources(): pl.pallas_call(source_kernel, in_specs=[pl.BlockSpec(memory_space=pl.ANY)...  4.81 us
    ppermute x3, starting transfers between devices, per_device(): lax.ppermute(picked[k], 'grp', [(i, (i + k) % size) for i in range(size)])  4.77 us
  transfers between devices with their start and end apart: 5, of which 4 were waited for; matrix products, arithmetic and copies ran while one was open for 0% of the time, Pallas kernels for 38%

profile of v6, /device:TPU:34, one launch (start us, length us, event | category | flops | bytes accessed | tf_op | source)
XLA Modules:
  0.0 87.5 jit_solution(17513422445044173049)
XLA Ops:
  0.6 0.0 copy-start.5
  0.6 0.0 copy-start
  0.7 0.0 copy-start.1
  0.7 1.7 %pack.1 = f32[4,20,4,3,1,128]{5,4,3,2,1,0:T(1,128)} custom-call(s32[1]{0:T(128)} %bitcast.grp_ref, f32[36,8,4,8,1,128]{5,4,3,2,1,0:T(1,128)} %bitcast.37, s32[8,4,8,1,128]{4,3,2,1,0:T(1,128)} %bitcast.31), custom_call_target="tpu_custom_call" | custom-call | tf_op jit(solution)/shard_map/pack/pallas_call | solution.py:78
  2.4 4.8 %all-to-all-start = ((f32[4,240,128]{2,1,0:T(8,128)}), f32[4,240,128]{2,1,0:T(8,128)S(1)}, u32[]{:S(2)}, u32[]{:S(2)}) async-start(f32[4,240,128]{2,1,0:T(8,128)} %bitcast.40), calls=%async_computation | async-start | bytes 983040 | tf_op jit(solution)/shard_map/all_to_all | solution.py:434
  7.9 0.0 copy-done.5
  7.9 0.0 copy-done
  7.9 8.0 %interior.1 = (f32[32,36,8,128]{3,2,1,0:T(8,128)}, f32[2,18,4,8,128]{4,3,2,1,0:T(8,128)S(1)}) custom-call(f32[1]{0:T(128)S(6)} %copy.23.courant_ref, f32[2,36]{1,0:T(2,128)S(1)} %copy-done.5, f32[36,8,4,8,128]{4,3,2,1,0:T(8,128)} %bitcast.38, s32[8,4,8,128]{3,2,1,0:T(8,128)S(1)} %bitcast.32), custom_call_target="tpu_custom_call" | custom-call | flops 40000000 | bytes 9500000 | tf_op jit(solution)/shard_map/interior/pallas_call | solution.py:166
  15.9 0.0 all-to-all-done.halo_ref
  15.9 0.0 copy-done.1
  15.9 1.7 %edges.1 = f32[32,36,8,128]{3,2,1,0:T(8,128)} custom-call(s32[1]{0:T(128)} %bitcast.grp_ref, f32[1]{0:T(128)S(6)} %copy.23.courant_ref, f32[4,24,128]{2,1,0:T(8,128)S(1)} %copy-done.1, f32[2,18,4,8,128]{4,3,2,1,0:T(8,128)S(1)} %get-tuple-element.8.tile_ref, s32[8,4,8,128]{3,2,1,0:T(8,128)S(1)} %bitcast.33, ...), custom_call_target="tpu_custom_call", output_to_operand_aliasing={{}: (6, {})} | custom-call | tf_op jit(solution)/shard_map/edges/pallas_call | solution.py:280
  17.6 0.0 copy-start.2
  17.6 0.0 copy-start.6
  17.6 7.5 %all-to-all-start.1 = ((f32[32,36,8,128]{3,2,1,0:T(8,128)}), f32[32,36,8,128]{3,2,1,0:T(8,128)}, u32[]{:S(2)}, u32[]{:S(2)}) async-start(f32[32,36,8,128]{3,2,1,0:T(8,128)} %edges.1), calls=%async_computation.1 | async-start | bytes 9437184 | tf_op jit(solution)/shard_map/all_to_all | solution.py:437
  25.2 0.0 copy-start.3
  25.2 0.0 copy-start.4
  25.2 0.0 copy-done.2
  25.2 0.0 copy-done.6
  25.2 24.3 %pick.1 = (f32[10,36,128]{2,1,0:T(8,128)S(1)}, f32[10,36,128]{2,1,0:T(8,128)S(1)}, f32[10,36,128]{2,1,0:T(8,128)S(1)}, f32[10,36,128]{2,1,0:T(8,128)S(1)}) custom-call(s32[1]{0:T(128)} %bitcast.grp_ref, s32[40,128]{1,0:T(8,128)S(1)} %copy-done.2, s32[32]{0:T(128)S(1)} %copy-done.6, f32[9216,128]{1,0:T(8,128)} %bitcast.36), custom_call_target="tpu_custom_call" | custom-call | flops 10000000 | bytes 6000000 | tf_op jit(solution)/shard_map/pick/pallas_call | solution.py:326
  49.5 1.5 %collective-permute-start = (f32[10,36,128]{2,1,0:T(8,128)S(1)}, f32[10,36,128]{2,1,0:T(8,128)S(1)}, u32[]{:S(2)}, u32[]{:S(2)}) collective-permute-start(f32[10,36,128]{2,1,0:T(8,128)S(1)} %get-tuple-element.11), channel_id=1, source_target_pairs={{0,1},{1,2},{2,3},{3,0},{4,5},{5,6},{6,7},{7,4},{8,9},{9,10},{10,1... | collective-permute-start | bytes 552968 | tf_op jit(solution)/shard_map/ppermute | solution.py:441
  51.0 1.1 %collective-permute-start.1 = (f32[10,36,128]{2,1,0:T(8,128)S(1)}, f32[10,36,128]{2,1,0:T(8,128)S(1)}, u32[]{:S(2)}, u32[]{:S(2)}) collective-permute-start(f32[10,36,128]{2,1,0:T(8,128)S(1)} %get-tuple-element.12), channel_id=1, source_target_pairs={{0,2},{1,3},{2,0},{3,1},{4,6},{5,7},{6,4},{7,5},{8,10},{9,11},{10,... | collective-permute-start | bytes 552968 | tf_op jit(solution)/shard_map/ppermute | solution.py:441
  52.1 2.2 %collective-permute-start.2 = (f32[10,36,128]{2,1,0:T(8,128)S(1)}, f32[10,36,128]{2,1,0:T(8,128)S(1)}, u32[]{:S(2)}, u32[]{:S(2)}) collective-permute-start(f32[10,36,128]{2,1,0:T(8,128)S(1)} %get-tuple-element.13), channel_id=1, source_target_pairs={{0,3},{1,0},{2,1},{3,2},{4,7},{5,4},{6,5},{7,6},{8,11},{9,8},{10,9... | collective-permute-start | bytes 552968 | tf_op jit(solution)/shard_map/ppermute | solution.py:441
  54.3 3.2 %collective-permute-done.refs_1_ = f32[10,36,128]{2,1,0:T(8,128)S(1)} collective-permute-done((f32[10,36,128]{2,1,0:T(8,128)S(1)}, f32[10,36,128]{2,1,0:T(8,128)S(1)}, u32[]{:S(2)}, u32[]{:S(2)}) %collective-permute-start) | collective-permute-done | bytes 184352 | tf_op jit(solution)/shard_map/ppermute | solution.py:441
  57.5 3.0 %collective-permute-done.1.refs_2_ = f32[10,36,128]{2,1,0:T(8,128)S(1)} collective-permute-done((f32[10,36,128]{2,1,0:T(8,128)S(1)}, f32[10,36,128]{2,1,0:T(8,128)S(1)}, u32[]{:S(2)}, u32[]{:S(2)}) %collective-permute-start.1) | collective-permute-done | bytes 184352 | tf_op jit(solution)/shard_map/ppermute | solution.py:441
  60.5 2.5 %collective-permute-done.2.refs_3_ = f32[10,36,128]{2,1,0:T(8,128)S(1)} collective-permute-done((f32[10,36,128]{2,1,0:T(8,128)S(1)}, f32[10,36,128]{2,1,0:T(8,128)S(1)}, u32[]{:S(2)}, u32[]{:S(2)}) %collective-permute-start.2) | collective-permute-done | bytes 184352 | tf_op jit(solution)/shard_map/ppermute | solution.py:441
  63.0 0.7 merge.1
  63.7 18.9 %all-to-all-done.1.recv_ref = f32[32,36,8,128]{3,2,1,0:T(8,128)} async-done(((f32[32,36,8,128]{3,2,1,0:T(8,128)}), f32[32,36,8,128]{3,2,1,0:T(8,128)}, u32[]{:S(2)}, u32[]{:S(2)}) %all-to-all-start.1) | async-done | bytes 4718624 | tf_op jit(solution)/shard_map/all_to_all | solution.py:437
  82.7 0.0 copy-done.3
  82.7 0.0 copy-done.4
  82.7 4.8 %sources.1 = f32[32,36,8,128]{3,2,1,0:T(8,128)} custom-call(f32[32,36,8,128]{3,2,1,0:T(8,128)} %all-to-all-done.1.recv_ref, f32[8,128]{1,0:T(8,128)S(1)} %bitcast.34, f32[8,128]{1,0:T(8,128)S(1)} %bitcast.35), custom_call_target="tpu_custom_call" | custom-call | tf_op jit(solution)/shard_map/sources/pallas_call | solution.py:410
Async XLA Ops:
  0.6 7.3 %copy-start.5 = (f32[2,36]{1,0:T(2,128)S(1)}, f32[2,36]{1,0:T(2,128)}, u32[]{:S(2)}) copy-start(f32[2,36]{1,0:T(2,128)} %constant.10.clone.trig_ref) | copy-start | bytes 868
  0.6 7.3 %copy-start = (s32[1,64,512]{2,1,0:T(8,128)S(1)}, s32[1,64,512]{2,1,0:T(8,128)}, u32[]{:S(2)}) copy-start(s32[1,64,512]{2,1,0:T(8,128)} %param.11) | copy-start | bytes 393220
  0.7 15.2 %copy-start.1 = (f32[4,24,128]{2,1,0:T(8,128)S(1)}, f32[4,24,128]{2,1,0:T(8,128)}, u32[]{:S(2)}) copy-start(f32[4,24,128]{2,1,0:T(8,128)} %constant.11.clone.table_ref) | copy-start | bytes 147460
  2.4 13.5 %all-to-all-start = ((f32[4,240,128]{2,1,0:T(8,128)}), f32[4,240,128]{2,1,0:T(8,128)S(1)}, u32[]{:S(2)}, u32[]{:S(2)}) async-start(f32[4,240,128]{2,1,0:T(8,128)} %bitcast.40), calls=%async_computation | async-start | bytes 983040 | tf_op jit(solution)/shard_map/all_to_all | solution.py:434
  17.6 7.6 %copy-start.2 = (s32[40,128]{1,0:T(8,128)S(1)}, s32[40,128]{1,0:T(8,128)}, u32[]{:S(2)}) copy-start(s32[40,128]{1,0:T(8,128)} %cells_ref.1) | copy-start | bytes 61444
  17.6 7.6 %copy-start.6 = (s32[32]{0:T(128)S(1)}, s32[32]{0:T(128)}, u32[]{:S(2)}) copy-start(s32[32]{0:T(128)} %constant.12.clone.place_ref) | copy-start | bytes 388
  17.6 65.1 %all-to-all-start.1 = ((f32[32,36,8,128]{3,2,1,0:T(8,128)}), f32[32,36,8,128]{3,2,1,0:T(8,128)}, u32[]{:S(2)}, u32[]{:S(2)}) async-start(f32[32,36,8,128]{3,2,1,0:T(8,128)} %edges.1), calls=%async_computation.1 | async-start | bytes 9437184 | tf_op jit(solution)/shard_map/all_to_all | solution.py:437
  25.2 57.5 %copy-start.3 = (f32[1,2,512]{2,1,0:T(2,128)S(1)}, f32[1,2,512]{2,1,0:T(2,128)}, u32[]{:S(2)}) copy-start(f32[1,2,512]{2,1,0:T(2,128)} %param.12) | copy-start | bytes 12292
  25.2 57.5 %copy-start.4 = (f32[1,2,512]{2,1,0:T(2,128)S(1)}, f32[1,2,512]{2,1,0:T(2,128)}, u32[]{:S(2)}) copy-start(f32[1,2,512]{2,1,0:T(2,128)} %param.13) | copy-start | bytes 12292
  49.5 8.0 %collective-permute-start = (f32[10,36,128]{2,1,0:T(8,128)S(1)}, f32[10,36,128]{2,1,0:T(8,128)S(1)}, u32[]{:S(2)}, u32[]{:S(2)}) collective-permute-start(f32[10,36,128]{2,1,0:T(8,128)S(1)} %get-tuple-element.11), channel_id=1, source_target_pairs={{0,1},{1,2},{2,3},{3,0},{4,5},{5,6},{6,7},{7,4},{8,9},{9,10},{10,1... | collective-permute-start | bytes 552968 | tf_op jit(solution)/shard_map/ppermute | solution.py:441
  51.0 9.5 %collective-permute-start.1 = (f32[10,36,128]{2,1,0:T(8,128)S(1)}, f32[10,36,128]{2,1,0:T(8,128)S(1)}, u32[]{:S(2)}, u32[]{:S(2)}) collective-permute-start(f32[10,36,128]{2,1,0:T(8,128)S(1)} %get-tuple-element.12), channel_id=1, source_target_pairs={{0,2},{1,3},{2,0},{3,1},{4,6},{5,7},{6,4},{7,5},{8,10},{9,11},{10,... | collective-permute-start | bytes 552968 | tf_op jit(solution)/shard_map/ppermute | solution.py:441
  52.1 10.9 %collective-permute-start.2 = (f32[10,36,128]{2,1,0:T(8,128)S(1)}, f32[10,36,128]{2,1,0:T(8,128)S(1)}, u32[]{:S(2)}, u32[]{:S(2)}) collective-permute-start(f32[10,36,128]{2,1,0:T(8,128)S(1)} %get-tuple-element.13), channel_id=1, source_target_pairs={{0,3},{1,0},{2,1},{3,2},{4,7},{5,4},{6,5},{7,6},{8,11},{9,8},{10,9... | collective-permute-start | bytes 552968 | tf_op jit(solution)/shard_map/ppermute | solution.py:441

commit v7 on v6

--- a/solution.py
+++ b/solution.py
@@ -29,7 +29,7 @@
 SCALE = (0.3 * np.float32(1.1) ** np.arange(NFREQ, dtype=np.float32)).astype(np.float32)
 LOG2E = 1.4426950408889634
 
-ORDER = (15, 27, 28, 26, 22, 18, 24, 3, 9, 25, 6, 13, 7, 31, 20, 12, 1, 17, 23, 2, 30, 14, 16, 10, 0, 21, 5, 4, 8, 11, 19, 29)
+ORDER = (15, 27, 28, 26, 21, 18, 24, 3, 9, 25, 6, 13, 7, 31, 20, 12, 1, 17, 23, 2, 30, 14, 16, 10, 0, 22, 5, 4, 8, 11, 19, 29)
 PLACE = tuple(int(p) for p in np.argsort(ORDER))
 
 

time: 88.8 us -> 88.5 us (level)
  no operation moved by 1% of the time
where the time goes in v7:
time: 88.5 us; the launch traced here: 87.7 us
  Pallas kernels  41.2 us (47%)
  waiting for transfers between devices  27.8 us (31%)
  starting transfers between devices  17.1 us (19%)
  between operations  1.43 us (2%)
    pallas_call x1, Pallas kernels, pick(): pl.pallas_call(pick_kernel, in_specs=[pl.BlockSpec(memory_space=pltpu.SME...  24.3 us
    all_to_all x1, waiting for transfers between devices, per_device(): lax.all_to_all(result, 'comp', split_axis=0, concat_axis=0, axis_index_gr...  19.1 us
    ppermute x3, waiting for transfers between devices, per_device(): lax.ppermute(picked[k], 'grp', [(i, (i + k) % size) for i in range(size)])  8.73 us
    pallas_call x1, Pallas kernels, interior(): pl.pallas_call(interior_kernel, in_specs=[smem, smem, hbm, vmem], out_spe...  7.96 us
    all_to_all x1, starting transfers between devices, per_device(): lax.all_to_all(result, 'comp', split_axis=0, concat_axis=0, axis_index_gr...  7.53 us
    all_to_all x1, starting transfers between devices, per_device(): lax.all_to_all(halos, 'grp', split_axis=0, concat_axis=0, tiled=True)  4.82 us
    pallas_call x1, Pallas kernels, sources(): pl.pallas_call(source_kernel, in_specs=[pl.BlockSpec(memory_space=pl.ANY)...  4.81 us
    ppermute x3, starting transfers between devices, per_device(): lax.ppermute(picked[k], 'grp', [(i, (i + k) % size) for i in range(size)])  4.77 us
  transfers between devices with their start and end apart: 5, of which 4 were waited for; matrix products, arithmetic and copies ran while one was open for 0% of the time, Pallas kernels for 38%

profile of v7, /device:TPU:34, one launch (start us, length us, event | category | flops | bytes accessed | tf_op | source)
XLA Modules:
  0.0 87.7 jit_solution(10716854184345658465)
XLA Ops:
  0.6 0.0 copy-start.5
  0.6 0.0 copy-start
  0.7 0.0 copy-start.1
  0.7 1.7 %pack.1 = f32[4,20,4,3,1,128]{5,4,3,2,1,0:T(1,128)} custom-call(s32[1]{0:T(128)} %bitcast.grp_ref, f32[36,8,4,8,1,128]{5,4,3,2,1,0:T(1,128)} %bitcast.37, s32[8,4,8,1,128]{4,3,2,1,0:T(1,128)} %bitcast.31), custom_call_target="tpu_custom_call" | custom-call | tf_op jit(solution)/shard_map/pack/pallas_call | solution.py:78
  2.4 4.8 %all-to-all-start = ((f32[4,240,128]{2,1,0:T(8,128)}), f32[4,240,128]{2,1,0:T(8,128)S(1)}, u32[]{:S(2)}, u32[]{:S(2)}) async-start(f32[4,240,128]{2,1,0:T(8,128)} %bitcast.40), calls=%async_computation | async-start | bytes 983040 | tf_op jit(solution)/shard_map/all_to_all | solution.py:434
  7.9 0.0 copy-done.5
  7.9 0.0 copy-done
  7.9 8.0 %interior.1 = (f32[32,36,8,128]{3,2,1,0:T(8,128)}, f32[2,18,4,8,128]{4,3,2,1,0:T(8,128)S(1)}) custom-call(f32[1]{0:T(128)S(6)} %copy.23.courant_ref, f32[2,36]{1,0:T(2,128)S(1)} %copy-done.5, f32[36,8,4,8,128]{4,3,2,1,0:T(8,128)} %bitcast.38, s32[8,4,8,128]{3,2,1,0:T(8,128)S(1)} %bitcast.32), custom_call_target="tpu_custom_call" | custom-call | flops 40000000 | bytes 9500000 | tf_op jit(solution)/shard_map/interior/pallas_call | solution.py:166
  15.9 0.0 all-to-all-done.halo_ref
  15.9 0.0 copy-done.1
  15.9 1.7 %edges.1 = f32[32,36,8,128]{3,2,1,0:T(8,128)} custom-call(s32[1]{0:T(128)} %bitcast.grp_ref, f32[1]{0:T(128)S(6)} %copy.23.courant_ref, f32[4,24,128]{2,1,0:T(8,128)S(1)} %copy-done.1, f32[2,18,4,8,128]{4,3,2,1,0:T(8,128)S(1)} %get-tuple-element.8.tile_ref, s32[8,4,8,128]{3,2,1,0:T(8,128)S(1)} %bitcast.33, ...), custom_call_target="tpu_custom_call", output_to_operand_aliasing={{}: (6, {})} | custom-call | tf_op jit(solution)/shard_map/edges/pallas_call | solution.py:280
  17.6 0.0 copy-start.2
  17.6 0.0 copy-start.6
  17.6 7.5 %all-to-all-start.1 = ((f32[32,36,8,128]{3,2,1,0:T(8,128)}), f32[32,36,8,128]{3,2,1,0:T(8,128)}, u32[]{:S(2)}, u32[]{:S(2)}) async-start(f32[32,36,8,128]{3,2,1,0:T(8,128)} %edges.1), calls=%async_computation.1 | async-start | bytes 9437184 | tf_op jit(solution)/shard_map/all_to_all | solution.py:437
  25.2 0.0 copy-start.3
  25.2 0.0 copy-start.4
  25.2 0.0 copy-done.2
  25.2 0.0 copy-done.6
  25.2 24.3 %pick.1 = (f32[10,36,128]{2,1,0:T(8,128)S(1)}, f32[10,36,128]{2,1,0:T(8,128)S(1)}, f32[10,36,128]{2,1,0:T(8,128)S(1)}, f32[10,36,128]{2,1,0:T(8,128)S(1)}) custom-call(s32[1]{0:T(128)} %bitcast.grp_ref, s32[40,128]{1,0:T(8,128)S(1)} %copy-done.2, s32[32]{0:T(128)S(1)} %copy-done.6, f32[9216,128]{1,0:T(8,128)} %bitcast.36), custom_call_target="tpu_custom_call" | custom-call | flops 10000000 | bytes 6000000 | tf_op jit(solution)/shard_map/pick/pallas_call | solution.py:326
  49.5 1.5 %collective-permute-start = (f32[10,36,128]{2,1,0:T(8,128)S(1)}, f32[10,36,128]{2,1,0:T(8,128)S(1)}, u32[]{:S(2)}, u32[]{:S(2)}) collective-permute-start(f32[10,36,128]{2,1,0:T(8,128)S(1)} %get-tuple-element.11), channel_id=1, source_target_pairs={{0,1},{1,2},{2,3},{3,0},{4,5},{5,6},{6,7},{7,4},{8,9},{9,10},{10,1... | collective-permute-start | bytes 552968 | tf_op jit(solution)/shard_map/ppermute | solution.py:441
  51.0 1.1 %collective-permute-start.1 = (f32[10,36,128]{2,1,0:T(8,128)S(1)}, f32[10,36,128]{2,1,0:T(8,128)S(1)}, u32[]{:S(2)}, u32[]{:S(2)}) collective-permute-start(f32[10,36,128]{2,1,0:T(8,128)S(1)} %get-tuple-element.12), channel_id=1, source_target_pairs={{0,2},{1,3},{2,0},{3,1},{4,6},{5,7},{6,4},{7,5},{8,10},{9,11},{10,... | collective-permute-start | bytes 552968 | tf_op jit(solution)/shard_map/ppermute | solution.py:441
  52.1 2.2 %collective-permute-start.2 = (f32[10,36,128]{2,1,0:T(8,128)S(1)}, f32[10,36,128]{2,1,0:T(8,128)S(1)}, u32[]{:S(2)}, u32[]{:S(2)}) collective-permute-start(f32[10,36,128]{2,1,0:T(8,128)S(1)} %get-tuple-element.13), channel_id=1, source_target_pairs={{0,3},{1,0},{2,1},{3,2},{4,7},{5,4},{6,5},{7,6},{8,11},{9,8},{10,9... | collective-permute-start | bytes 552968 | tf_op jit(solution)/shard_map/ppermute | solution.py:441
  54.3 3.2 %collective-permute-done.refs_1_ = f32[10,36,128]{2,1,0:T(8,128)S(1)} collective-permute-done((f32[10,36,128]{2,1,0:T(8,128)S(1)}, f32[10,36,128]{2,1,0:T(8,128)S(1)}, u32[]{:S(2)}, u32[]{:S(2)}) %collective-permute-start) | collective-permute-done | bytes 184352 | tf_op jit(solution)/shard_map/ppermute | solution.py:441
  57.5 3.0 %collective-permute-done.1.refs_2_ = f32[10,36,128]{2,1,0:T(8,128)S(1)} collective-permute-done((f32[10,36,128]{2,1,0:T(8,128)S(1)}, f32[10,36,128]{2,1,0:T(8,128)S(1)}, u32[]{:S(2)}, u32[]{:S(2)}) %collective-permute-start.1) | collective-permute-done | bytes 184352 | tf_op jit(solution)/shard_map/ppermute | solution.py:441
  60.5 2.5 %collective-permute-done.2.refs_3_ = f32[10,36,128]{2,1,0:T(8,128)S(1)} collective-permute-done((f32[10,36,128]{2,1,0:T(8,128)S(1)}, f32[10,36,128]{2,1,0:T(8,128)S(1)}, u32[]{:S(2)}, u32[]{:S(2)}) %collective-permute-start.2) | collective-permute-done | bytes 184352 | tf_op jit(solution)/shard_map/ppermute | solution.py:441
  63.0 0.7 merge.1
  63.7 19.1 %all-to-all-done.1.recv_ref = f32[32,36,8,128]{3,2,1,0:T(8,128)} async-done(((f32[32,36,8,128]{3,2,1,0:T(8,128)}), f32[32,36,8,128]{3,2,1,0:T(8,128)}, u32[]{:S(2)}, u32[]{:S(2)}) %all-to-all-start.1) | async-done | bytes 4718624 | tf_op jit(solution)/shard_map/all_to_all | solution.py:437
  82.8 0.0 copy-done.3
  82.8 0.0 copy-done.4
  82.8 4.8 %sources.1 = f32[32,36,8,128]{3,2,1,0:T(8,128)} custom-call(f32[32,36,8,128]{3,2,1,0:T(8,128)} %all-to-all-done.1.recv_ref, f32[8,128]{1,0:T(8,128)S(1)} %bitcast.34, f32[8,128]{1,0:T(8,128)S(1)} %bitcast.35), custom_call_target="tpu_custom_call" | custom-call | tf_op jit(solution)/shard_map/sources/pallas_call | solution.py:410
Async XLA Ops:
  0.6 7.3 %copy-start.5 = (f32[2,36]{1,0:T(2,128)S(1)}, f32[2,36]{1,0:T(2,128)}, u32[]{:S(2)}) copy-start(f32[2,36]{1,0:T(2,128)} %constant.10.clone.trig_ref) | copy-start | bytes 868
  0.6 7.3 %copy-start = (s32[1,64,512]{2,1,0:T(8,128)S(1)}, s32[1,64,512]{2,1,0:T(8,128)}, u32[]{:S(2)}) copy-start(s32[1,64,512]{2,1,0:T(8,128)} %param.11) | copy-start | bytes 393220
  0.7 15.2 %copy-start.1 = (f32[4,24,128]{2,1,0:T(8,128)S(1)}, f32[4,24,128]{2,1,0:T(8,128)}, u32[]{:S(2)}) copy-start(f32[4,24,128]{2,1,0:T(8,128)} %constant.11.clone.table_ref) | copy-start | bytes 147460
  2.4 13.5 %all-to-all-start = ((f32[4,240,128]{2,1,0:T(8,128)}), f32[4,240,128]{2,1,0:T(8,128)S(1)}, u32[]{:S(2)}, u32[]{:S(2)}) async-start(f32[4,240,128]{2,1,0:T(8,128)} %bitcast.40), calls=%async_computation | async-start | bytes 983040 | tf_op jit(solution)/shard_map/all_to_all | solution.py:434
  17.6 7.6 %copy-start.2 = (s32[40,128]{1,0:T(8,128)S(1)}, s32[40,128]{1,0:T(8,128)}, u32[]{:S(2)}) copy-start(s32[40,128]{1,0:T(8,128)} %cells_ref.1) | copy-start | bytes 61444
  17.6 7.6 %copy-start.6 = (s32[32]{0:T(128)S(1)}, s32[32]{0:T(128)}, u32[]{:S(2)}) copy-start(s32[32]{0:T(128)} %constant.12.clone.place_ref) | copy-start | bytes 388
  17.6 65.2 %all-to-all-start.1 = ((f32[32,36,8,128]{3,2,1,0:T(8,128)}), f32[32,36,8,128]{3,2,1,0:T(8,128)}, u32[]{:S(2)}, u32[]{:S(2)}) async-start(f32[32,36,8,128]{3,2,1,0:T(8,128)} %edges.1), calls=%async_computation.1 | async-start | bytes 9437184 | tf_op jit(solution)/shard_map/all_to_all | solution.py:437
  25.2 57.7 %copy-start.3 = (f32[1,2,512]{2,1,0:T(2,128)S(1)}, f32[1,2,512]{2,1,0:T(2,128)}, u32[]{:S(2)}) copy-start(f32[1,2,512]{2,1,0:T(2,128)} %param.12) | copy-start | bytes 12292
  25.2 57.7 %copy-start.4 = (f32[1,2,512]{2,1,0:T(2,128)S(1)}, f32[1,2,512]{2,1,0:T(2,128)}, u32[]{:S(2)}) copy-start(f32[1,2,512]{2,1,0:T(2,128)} %param.13) | copy-start | bytes 12292
  49.5 8.0 %collective-permute-start = (f32[10,36,128]{2,1,0:T(8,128)S(1)}, f32[10,36,128]{2,1,0:T(8,128)S(1)}, u32[]{:S(2)}, u32[]{:S(2)}) collective-permute-start(f32[10,36,128]{2,1,0:T(8,128)S(1)} %get-tuple-element.11), channel_id=1, source_target_pairs={{0,1},{1,2},{2,3},{3,0},{4,5},{5,6},{6,7},{7,4},{8,9},{9,10},{10,1... | collective-permute-start | bytes 552968 | tf_op jit(solution)/shard_map/ppermute | solution.py:441
  51.0 9.5 %collective-permute-start.1 = (f32[10,36,128]{2,1,0:T(8,128)S(1)}, f32[10,36,128]{2,1,0:T(8,128)S(1)}, u32[]{:S(2)}, u32[]{:S(2)}) collective-permute-start(f32[10,36,128]{2,1,0:T(8,128)S(1)} %get-tuple-element.12), channel_id=1, source_target_pairs={{0,2},{1,3},{2,0},{3,1},{4,6},{5,7},{6,4},{7,5},{8,10},{9,11},{10,... | collective-permute-start | bytes 552968 | tf_op jit(solution)/shard_map/ppermute | solution.py:441
  52.1 10.9 %collective-permute-start.2 = (f32[10,36,128]{2,1,0:T(8,128)S(1)}, f32[10,36,128]{2,1,0:T(8,128)S(1)}, u32[]{:S(2)}, u32[]{:S(2)}) collective-permute-start(f32[10,36,128]{2,1,0:T(8,128)S(1)} %get-tuple-element.13), channel_id=1, source_target_pairs={{0,3},{1,0},{2,1},{3,2},{4,7},{5,4},{6,5},{7,6},{8,11},{9,8},{10,9... | collective-permute-start | bytes 552968 | tf_op jit(solution)/shard_map/ppermute | solution.py:441
